TPU v7x, 32 devices: a whole 2x2x4 slice. The times are simulated.
32 devices in a mesh: blk: 8 (over z, x), sub: 4 (over y, core).
Axes of the slice: x: 2, y: 2, z: 4, core: 2. Of those that a mesh axis runs over, the one named last changes fastest.
Arguments:
- features: bfloat16 [16, 65536], P(None, ('blk', 'sub')), may hold values from -6 to 6
- adjacency: bfloat16 [512, 8, 128, 128], P(('blk', 'sub')), may hold values from 0.049804688 to 2
- col_tiles: int32 [512, 8], P(('blk', 'sub')), may hold values from 0 to 511, as said below
- match_one: int32 [256, 128], replicated, may hold values from 0 to 127, each once within a row
- match_two: int32 [128, 128], replicated, may hold values from 0 to 127, each once within a row
Outputs:
- coarse_adjacency: bfloat16 [128, 8, 128, 128], P(('blk', 'sub'))
- coarse_features: bfloat16 [16, 16384], P(None, ('blk', 'sub'))
Inputs may be any that keep to these rules, and one draw needn't show every extreme that they name: `col_tiles`: for each slot k, the two tiles t and t + 64 of a level-one pair ((t // 64) even) name column tiles that differ by 0 or 64; with that difference cleared, the tiles t and t + 16 ((t // 16) even, (t // 64) even) name column tiles that differ by 0 or 16. `match_one`: each row is a matching of the high tile's rows onto the low tile's rows. `match_two`: each row is a matching of the high tile's rows onto the low tile's rows.
All inputs are finite; a program needn't handle non-finite values.
Results may differ from a plain program's by a relative error of at most 0.0053.
Values may be sent and summed in bfloat16 or wider, within the bound.
No kernel may reach another device: no remote copies, remote signals or barrier semaphores. Data moves between devices by JAX's collectives and lax.ppermute only.
A program may use at most 64 MiB of HBM per device.

v0:
```python
import jax
import jax.numpy as jnp
from jax import lax
from jax.sharding import PartitionSpec as P


def swapped(value, axis, stride):
    mask = 2**stride
    pairs = [(source, source ^ mask) for source in range(lax.axis_size(axis))]
    return lax.ppermute(value, axis, pairs)


def one_hot(row_maps, positions):
    return (row_maps[..., :, None] == positions).astype(jnp.bfloat16)


def pair_of(column_ids, block_span):
    return column_ids // (2 * block_span) * block_span + column_ids % block_span


def first_maps(column_ids, match_one, block_span, positions):
    upper = column_ids // block_span % 2 == 1
    return jnp.where(upper[..., None], match_one[pair_of(column_ids, block_span)], positions)


def second_maps(column_ids, match_two, block_span, tile_count, positions):
    pair_index = pair_of(column_ids, block_span)
    group_index = pair_index // (2 * tile_count) * tile_count + pair_index % tile_count
    upper = column_ids // tile_count % 2 == 1
    return jnp.where(upper[..., None], match_two[group_index], positions)


def column_side(blocks, row_maps, positions):
    hot = one_hot(row_maps, positions)
    return jnp.einsum("jkab,jkbc->jkac", blocks, hot, preferred_element_type=jnp.float32).astype(
        jnp.bfloat16
    )


def row_side(row_hot, blocks):
    return jnp.einsum("jba,jkbc->jkac", row_hot, blocks, preferred_element_type=jnp.float32)


def feature_side(feats, row_hot):
    return jnp.einsum("fjb,jba->fja", feats, row_hot, preferred_element_type=jnp.float32)


def add_pair(first_part, second_part):
    return (first_part.astype(jnp.float32) + second_part.astype(jnp.float32)).astype(jnp.bfloat16)


def per_device(features, adjacency, col_tiles, match_one, match_two):
    tile_count = adjacency.shape[0]
    slot_count = adjacency.shape[1]
    tile_width = adjacency.shape[2]
    feat_count = features.shape[0]
    quarter = tile_count // 4
    sub_count = lax.axis_size("sub")
    block_span = sub_count * tile_count
    blk_index = lax.axis_index("blk")
    sub_index = lax.axis_index("sub")
    positions = jnp.arange(tile_width, dtype=jnp.int32)
    feats = features.reshape(feat_count, tile_count, tile_width)
    own_cols = column_side(
        adjacency, first_maps(col_tiles, match_one, block_span, positions), positions
    )
    first_pair = (blk_index // 2 * sub_count + sub_index) * tile_count
    rows_one = one_hot(lax.dynamic_slice_in_dim(match_one, first_pair, tile_count, 0), positions)
    first_group = (blk_index // 2 * (sub_count // 2) + sub_index // 2) * tile_count
    high_one = blk_index % 2 == 1
    high_two = sub_index % 2 == 1
    blk_even = blk_index % 2 == 0
    sub_even = sub_index % 2 == 0
    terms_tiles, terms_feats = lax.cond(
        high_one,
        lambda: (
            row_side(rows_one, own_cols).astype(jnp.bfloat16),
            feature_side(feats, rows_one).astype(jnp.bfloat16),
        ),
        lambda: (own_cols, feats),
    )
    grid_tiles = terms_tiles.reshape(quarter, 2, 2, slot_count, tile_width, tile_width)
    grid_feats = terms_feats.reshape(feat_count, quarter, 2, 2, tile_width)
    keep_tiles = jnp.where(blk_even, grid_tiles[:, 0], grid_tiles[:, 1])
    send_tiles = jnp.where(blk_even, grid_tiles[:, 1], grid_tiles[:, 0])
    keep_feats = jnp.where(blk_even, grid_feats[:, :, 0], grid_feats[:, :, 1])
    send_feats = jnp.where(blk_even, grid_feats[:, :, 1], grid_feats[:, :, 0])
    got_tiles, got_feats = swapped((send_tiles, send_feats), "blk", 0)
    level_tiles = add_pair(keep_tiles, got_tiles).reshape(
        2 * quarter, slot_count, tile_width, tile_width
    )
    level_feats = add_pair(keep_feats, got_feats).reshape(feat_count, 2 * quarter, tile_width)
    level_cols = col_tiles - col_tiles // block_span % 2 * block_span
    grid_cols = level_cols.reshape(quarter, 2, 2, slot_count)
    keep_cols = jnp.where(blk_even, grid_cols[:, 0], grid_cols[:, 1]).reshape(
        2 * quarter, slot_count
    )
    own_two = column_side(
        level_tiles, second_maps(keep_cols, match_two, block_span, tile_count, positions), positions
    )
    all_rows = one_hot(lax.dynamic_slice_in_dim(match_two, first_group, tile_count, 0), positions)
    grid_rows = all_rows.reshape(quarter, 2, 2, tile_width, tile_width)
    rows_two = jnp.where(blk_even, grid_rows[:, 0], grid_rows[:, 1]).reshape(
        2 * quarter, tile_width, tile_width
    )
    second_tiles, second_feats = lax.cond(
        high_two,
        lambda: (
            row_side(rows_two, own_two).astype(jnp.bfloat16),
            feature_side(level_feats, rows_two).astype(jnp.bfloat16),
        ),
        lambda: (own_two, level_feats),
    )
    grid_two = second_tiles.reshape(quarter, 2, slot_count, tile_width, tile_width)
    grid_feats_two = second_feats.reshape(feat_count, quarter, 2, tile_width)
    keep_two = jnp.where(sub_even, grid_two[:, 0], grid_two[:, 1])
    send_two = jnp.where(sub_even, grid_two[:, 1], grid_two[:, 0])
    keep_feats_two = jnp.where(sub_even, grid_feats_two[:, :, 0], grid_feats_two[:, :, 1])
    send_feats_two = jnp.where(sub_even, grid_feats_two[:, :, 1], grid_feats_two[:, :, 0])
    got_two, got_feats_two = swapped((send_two, send_feats_two), "sub", 0)
    final_tiles = add_pair(keep_two, got_two)
    final_feats = add_pair(keep_feats_two, got_feats_two)
    return (final_tiles, final_feats.reshape(feat_count, quarter * tile_width))


def solution(mesh):
    placed = (
        P(None, ("blk", "sub")),
        P(("blk", "sub"), None, None, None),
        P(("blk", "sub"), None),
        P(),
        P(),
    )
    return jax.shard_map(
        per_device,
        mesh=mesh,
        in_specs=placed,
        out_specs=(P(("blk", "sub"), None, None, None), P(None, ("blk", "sub"))),
        check_vma=False,
    )
```

profile of v0, /device:TPU:0, one launch (start us, length us, event | category | flops | bytes accessed | tf_op | source)
XLA Modules:
  0.0 92.0 jit_solution(2525428600481024207)
XLA Ops:
  0.6 0.0 copy-start
  0.7 0.8 copy.37
  1.5 0.0 copy-done
  1.6 0.3 fusion.7
  1.9 0.1 reshape.306
  2.0 0.6 gather_fusion
  2.7 0.8 copy.62
  3.5 0.1 bitcast_select_fusion
  3.6 7.2 %convert_bitcast_fusion = bf16[16,8,128,128]{2,3,1,0:T(8,128)(2,1)} fusion(bf16[16,8,128,128]{3,2,1,0:T(8,128)(2,1)} %param.10, s32[16,8,128]{2,1,0:T(8,128)S(1)} %bitcast_select_fusion), kind=kOutput, calls=%fused_computation.29 | convolution fusion | flops 541065216 | bytes 8454144 | tf_op jit(solution)/shard_map/jkab,jkbc->jkac/dot_general | solution.py:35
  10.8 18.3 %conditional.2 = (bf16[4,2,8,128,128]{3,4,2,1,0:T(8,128)(2,1)S(1)}, bf16[4,2,8,128,128]{3,4,2,1,0:T(8,128)(2,1)}, bf16[16,4,2,128]{3,0,2,1:T(8,128)(2,1)S(1)}, bf16[16,4,2,128]{3,0,2,1:T(8,128)(2,1)S(1)}) conditional(s32[]{:T(128)} %convert_element_type.89, (bf16[16,8,128,128]{2,3,1,0:T(8,128)(2,1)}, bf16[16,16,128]{2,1,0:T(8,128)(2,1)S(1)}) %tuple.63, ...), branch_computations={%region_0.1_spmd, %region_1.2_spmd} | conditional | flops 547389440 | bytes 25428000 | solution.py:74
  10.8 6.4 %copy.41 = bf16[16,8,128,128]{3,2,1,0:T(8,128)(2,1)} copy(bf16[16,8,128,128]{2,3,1,0:T(8,128)(2,1)} %get-tuple-element.118) | data formatting | bytes 8388608 | tf_op jit(solution)/shard_map
  17.2 4.8 %slice_bitcast_fusion = (bf16[4,2,8,128,128]{4,3,2,1,0:T(8,128)(2,1)}, bf16[4,2,8,128,128]{4,3,2,1,0:T(8,128)(2,1)}) fusion(bf16[4,2,2,8,128,128]{5,4,3,2,1,0:T(8,128)(2,1)} %bitcast.104), kind=kLoop, calls=%fused_computation.2 | loop fusion | bytes 8388608 | tf_op jit(solution)/shard_map/squeeze | solution.py:84
  22.0 3.0 %copy.26 = bf16[4,2,8,128,128]{3,4,2,1,0:T(8,128)(2,1)S(1)} copy(bf16[4,2,8,128,128]{4,3,2,1,0:T(8,128)(2,1)} %get-tuple-element.124) | data formatting | bytes 4194304 | tf_op jit(solution)/shard_map
  25.0 4.0 %copy.27 = bf16[4,2,8,128,128]{3,4,2,1,0:T(8,128)(2,1)} copy(bf16[4,2,8,128,128]{4,3,2,1,0:T(8,128)(2,1)} %get-tuple-element.123) | data formatting | bytes 4194304 | tf_op jit(solution)/shard_map
  29.1 0.0 copy-start.1
  29.1 3.2 %broadcast_select_fusion = bf16[4,2,8,128,128]{3,4,2,1,0:T(8,128)(2,1)} fusion(bf16[4,2,8,128,128]{3,4,2,1,0:T(8,128)(2,1)} %get-tuple-element.103, bf16[4,2,8,128,128]{3,4,2,1,0:T(8,128)(2,1)S(1)} %get-tuple-element.102, pred[]{:T(512)} %eq.94), kind=kLoop, calls=%fused_computation.34 | loop fusion | flops 1048576 | bytes 6291457 | tf_op jit(solution)/shard_map/jit(_where)/select_n | solution.py:85
  32.2 0.0 collective-permute-start
  32.2 2.0 %collective-permute-start.1 = (bf16[16,4,2,128]{3,0,2,1:T(8,128)(2,1)S(1)}, bf16[16,4,2,128]{3,0,2,1:T(8,128)(2,1)S(1)}, u32[]{:S(2)}, u32[]{:S(2)}) collective-permute-start(bf16[16,4,2,128]{3,0,2,1:T(8,128)(2,1)S(1)} %broadcast_select_fusion.2), channel_id=1, source_target_pairs={{0,4},{4,0},{8,12},{12,8},{16,20},{20,16},{24,28},{28,24},{1,5},{5... | collective-permute-start | bytes 98312 | tf_op jit(solution)/shard_map/ppermute | solution.py:10
  34.3 0.1 reshape.314
  34.4 0.0 copy-done.1
  34.4 0.6 gather_fusion.1
  35.0 0.3 fusion.8
  35.4 0.1 bitcast_select_fusion.1
  35.5 45.7 %collective-permute-done.1 = bf16[16,4,2,128]{3,0,2,1:T(8,128)(2,1)S(1)} collective-permute-done((bf16[16,4,2,128]{3,0,2,1:T(8,128)(2,1)S(1)}, bf16[16,4,2,128]{3,0,2,1:T(8,128)(2,1)S(1)}, u32[]{:S(2)}, u32[]{:S(2)}) %collective-permute-start.1) | collective-permute-done | bytes 32800 | tf_op jit(solution)/shard_map/ppermute | solution.py:10
  81.2 0.0 collective-permute-done
  81.2 2.8 %add_convert_fusion = bf16[4,2,8,128,128]{3,4,2,1,0:T(8,128)(2,1)S(1)} fusion(bf16[4,2,8,128,128]{3,4,2,1,0:T(8,128)(2,1)} %collective-permute-done, bf16[4,2,8,128,128]{3,4,2,1,0:T(8,128)(2,1)S(1)} %get-tuple-element.102, bf16[4,2,8,128,128]{3,4,2,1,0:T(8,128)(2,1)} %get-tuple-element.103, pred[]{:T(512)} %eq.94), kind=kLoop, calls=%fused_computation.28 | loop fusion | flops 5242880 | bytes 8388609 | tf_op jit(solution)/shard_map/convert_element_type | solution.py:49
  83.9 2.6 %fusion.6 = bf16[8,8,128,128]{3,2,1,0:T(8,128)(2,1)S(1)} fusion(bf16[8,8,128,128]{2,3,1,0:T(8,128)(2,1)S(1)} %bitcast.107, s32[8,8,128]{2,1,0:T(8,128)S(1)} %bitcast_select_fusion.1), kind=kOutput, calls=%fused_computation.35 | convolution fusion | flops 270532608 | bytes 4227072 | tf_op jit(solution)/shard_map/jkab,jkbc->jkac/dot_general | solution.py:35
  86.5 0.2 conditional.3
  86.5 0.1 slice_bitcast_fusion.8
  86.7 0.1 broadcast_select_fusion.1
  86.8 0.8 collective-permute-start.2
  87.6 0.1 collective-permute-start.3
  87.7 2.2 %collective-permute-done.3 = bf16[16,4,128]{2,0,1:T(8,128)(2,1)S(1)} collective-permute-done((bf16[16,4,128]{2,0,1:T(8,128)(2,1)S(1)}, bf16[16,4,128]{2,0,1:T(8,128)(2,1)S(1)}, u32[]{:S(2)}, u32[]{:S(2)}) %collective-permute-start.3) | collective-permute-done | bytes 16416 | tf_op jit(solution)/shard_map/ppermute | solution.py:10
  89.9 0.6 copy_bitcast_fusion
  90.5 0.0 collective-permute-done.2
  90.5 1.5 %add_convert_fusion.1 = bf16[4,8,128,128]{3,2,1,0:T(8,128)(2,1)} fusion(bf16[4,8,128,128]{3,2,1,0:T(8,128)(2,1)S(1)} %collective-permute-done.2, bf16[4,8,128,128]{3,2,1,0:T(8,128)(2,1)S(1)} %get-tuple-element.106, bf16[4,8,128,128]{3,2,1,0:T(8,128)(2,1)S(1)} %get-tuple-element.107, pred[]{:T(512)S(6)} %eq.92), kind=kLoop, calls=%fused_computation.32 | loop fusion | flops 2621440 | bytes 4194305 | tf_op jit(solution)/shard_map/convert_element_type | solution.py:49
  (15 shorter events, 0.2 us)
Async XLA Ops:
  0.6 0.9 %copy-start = (s32[256,128]{1,0:T(8,128)S(1)}, s32[256,128]{1,0:T(8,128)}, u32[]{:S(2)}) copy-start(s32[256,128]{1,0:T(8,128)} %param.12) | copy-start | bytes 393220
  29.1 5.3 %copy-start.1 = (s32[128,128]{1,0:T(8,128)S(1)}, s32[128,128]{1,0:T(8,128)}, u32[]{:S(2)}) copy-start(s32[128,128]{1,0:T(8,128)} %param.13) | copy-start | bytes 196612
  32.2 48.9 %collective-permute-start = (bf16[4,2,8,128,128]{3,4,2,1,0:T(8,128)(2,1)}, bf16[4,2,8,128,128]{3,4,2,1,0:T(8,128)(2,1)}, u32[]{:S(2)}, u32[]{:S(2)}) collective-permute-start(bf16[4,2,8,128,128]{3,4,2,1,0:T(8,128)(2,1)} %broadcast_select_fusion), channel_id=1, source_target_pairs={{0,4},{4,0},{8,12},{12,8},{16,20},{20,16},{24,28},{28,24},{1,5},{5... | collective-permute-start | bytes 6291464 | tf_op jit(solution)/shard_map/ppermute | solution.py:10
  32.2 48.9 %collective-permute-start.1 = (bf16[16,4,2,128]{3,0,2,1:T(8,128)(2,1)S(1)}, bf16[16,4,2,128]{3,0,2,1:T(8,128)(2,1)S(1)}, u32[]{:S(2)}, u32[]{:S(2)}) collective-permute-start(bf16[16,4,2,128]{3,0,2,1:T(8,128)(2,1)S(1)} %broadcast_select_fusion.2), channel_id=1, source_target_pairs={{0,4},{4,0},{8,12},{12,8},{16,20},{20,16},{24,28},{28,24},{1,5},{5... | collective-permute-start | bytes 98312 | tf_op jit(solution)/shard_map/ppermute | solution.py:10
  86.8 3.7 %collective-permute-start.2 = (bf16[4,8,128,128]{3,2,1,0:T(8,128)(2,1)S(1)}, bf16[4,8,128,128]{3,2,1,0:T(8,128)(2,1)S(1)}, u32[]{:S(2)}, u32[]{:S(2)}) collective-permute-start(bf16[4,8,128,128]{3,2,1,0:T(8,128)(2,1)S(1)} %broadcast_select_fusion.1), channel_id=1, source_target_pairs={{0,1},{1,0},{2,3},{3,2},{4,5},{5,4},{6,7},{7,6},{8,9},{9,8},{10,11... | collective-permute-start | bytes 3145736 | tf_op jit(solution)/shard_map/ppermute | solution.py:10
  87.6 2.3 %collective-permute-start.3 = (bf16[16,4,128]{2,0,1:T(8,128)(2,1)S(1)}, bf16[16,4,128]{2,0,1:T(8,128)(2,1)S(1)}, u32[]{:S(2)}, u32[]{:S(2)}) collective-permute-start(bf16[16,4,128]{2,0,1:T(8,128)(2,1)S(1)} %broadcast_select_fusion.3), channel_id=1, source_target_pairs={{0,1},{1,0},{2,3},{3,2},{4,5},{5,4},{6,7},{7,6},{8,9},{9,8},{10,11... | collective-permute-start | bytes 49160 | tf_op jit(solution)/shard_map/ppermute | solution.py:10
where the time goes:
time: 92.5 us; the launch traced here: 92 us
  waiting for transfers between devices  47.9 us (52%)
  local copies, waits for them, and re-layouts  21.5 us (23%)
  matrix products  9.71 us (10%)
  other arithmetic  9.08 us (10%)
  starting transfers between devices  2.92 us (3%)
    ppermute x4, waiting for transfers between devices, swapped(): return lax.ppermute(value, axis, pairs)  47.9 us
    another operation x4, local copies, waits for them, and re-layouts  13.5 us
    dot_general x2, matrix products, column_side(): jnp.einsum('jkab,jkbc->jkac', blocks, hot, preferred_element_type=jnp.flo...  9.71 us
    squeeze x1, local copies, waits for them, and re-layouts, per_device(): keep_tiles = jnp.where(blk_even, grid_tiles[:, 0], grid_tiles[:, 1])  4.78 us
    convert_element_type x3, other arithmetic, add_pair(): (first_part.astype(jnp.float32) + second_part.astype(jnp.float32)).astype...  4.24 us
    select_n x1, other arithmetic, per_device(): send_tiles = jnp.where(blk_even, grid_tiles[:, 1], grid_tiles[:, 0])  3.16 us
    ppermute x4, starting transfers between devices, swapped(): return lax.ppermute(value, axis, pairs)  2.92 us
  transfers between devices with their start and end apart: 4, of which 2 were waited for; matrix products, arithmetic and copies ran while one was open for 2% of the time, Pallas kernels for 0%

commit v1 on v0

v1 whole, which is shorter than its diff:
```python
import functools

import jax
import jax.numpy as jnp
from jax import lax
from jax.experimental import pallas as pl
from jax.experimental.pallas import tpu as pltpu
from jax.sharding import PartitionSpec as P


def swapped(value, axis):
    pairs = [(source, source ^ 1) for source in range(lax.axis_size(axis))]
    return lax.ppermute(value, axis, pairs)


def split_by(value, size):
    if size & (size - 1) == 0:
        return value >> (size.bit_length() - 1), value & (size - 1)
    return value // size, value % size


def merged_kernel(
    first, slots, span, count, scal, own_cols, other_cols, own, other, own_feat, other_feat,
    match_one, match_two, *rest
):
    (tile_out, feat_out, one_rows, two_rows) = rest
    width = own.shape[-1]
    tile = 4 * (first + pl.program_id(0)) + 2 * scal[0] + scal[1]
    lanes = lax.broadcasted_iota(jnp.int32, (1, width), 1)

    def put(row, column_id):
        block, inside = split_by(column_id, span)
        pair_block, high_one = split_by(block, 2)
        sub, place = split_by(inside, count)
        sub_pair, high_two = split_by(sub, 2)
        pair = pair_block * span + inside
        group = pair_block * (span // 2) + sub_pair * count + place
        one_rows[pl.ds(row, 1), :] = jnp.where(high_one == 1, match_one[pl.ds(pair, 1), :], lanes)
        two_rows[pl.ds(row, 1), :] = jnp.where(high_two == 1, match_two[pl.ds(group, 1), :], lanes)

    for slot in range(slots):
        put(slot, own_cols[tile, slot])
        put(slots + slot, other_cols[tile, slot])
    put(2 * slots, scal[2] + tile)
    put(2 * slots + 1, scal[3] + tile)
    maps = jnp.take_along_axis(two_rows[...], one_rows[...], axis=1)
    down = maps.T
    across = lax.broadcasted_iota(jnp.int32, (width, width), 1)
    along = lax.broadcasted_iota(jnp.int32, (width, width), 0)

    def columns(row):
        return (down[:, row : row + 1] == across).astype(jnp.bfloat16)

    def dot(a, b):
        return jnp.dot(a, b, preferred_element_type=jnp.float32)

    own_rows = (maps[2 * slots : 2 * slots + 1, :] == along).astype(jnp.bfloat16)
    other_rows = (maps[2 * slots + 1 : 2 * slots + 2, :] == along).astype(jnp.bfloat16)
    for pair in range(slots // 2):
        left, right = 2 * pair, 2 * pair + 1
        own_two = dot(own_rows, jnp.concatenate([own[0, left], own[0, right]], 1)).astype(jnp.bfloat16)
        other_two = dot(other_rows, jnp.concatenate([other[0, left], other[0, right]], 1)).astype(
            jnp.bfloat16
        )
        for half, slot in enumerate((left, right)):
            lhs = jnp.concatenate(
                [
                    own_two[:, half * width : (half + 1) * width],
                    other_two[:, half * width : (half + 1) * width],
                ],
                1,
            )
            rhs = jnp.concatenate([columns(slot), columns(slots + slot)], 0)
            total = dot(lhs, rhs).astype(jnp.bfloat16)
            if feat_out is None:
                tile_out[0, slot * width : (slot + 1) * width, :] = total
            else:
                tile_out[0, slot] = total
    feats = dot(
        jnp.concatenate([own_feat[...], other_feat[...]], 1),
        jnp.concatenate([columns(2 * slots), columns(2 * slots + 1)], 0),
    ).astype(jnp.bfloat16)
    if feat_out is None:
        tile_out[0, slots * width :, :] = feats
    else:
        feat_out[...] = feats


def packed_kernel(first, slots, span, count, *refs):
    merged_kernel(first, slots, span, count, *refs[:9], refs[9], None, *refs[10:])


def merged(first, tiles, packed, span, scal, own_cols, other_cols, adjacency, other, feats, other_feats,
           match_one, match_two):
    count, slots, width = adjacency.shape[:3]
    feat_count = feats.shape[0]
    whole = lambda array: pl.BlockSpec(array.shape, lambda i, *_: (0, 0))
    tile_of = lambda i, scal: 4 * (first + i) + 2 * scal[0] + scal[1]
    in_specs = [
        pl.BlockSpec((1, slots, width, width), lambda i, scal, *_: (tile_of(i, scal), 0, 0, 0)),
        pl.BlockSpec((1, slots, width, width), lambda i, *_: (i, 0, 0, 0)),
        pl.BlockSpec((feat_count, width), lambda i, scal, *_: (0, tile_of(i, scal))),
        pl.BlockSpec((feat_count, width), lambda i, scal, *_: (0, tile_of(i, scal))),
        whole(match_one),
        whole(match_two),
    ]
    if packed:
        body = packed_kernel
        depth = slots * width + feat_count
        out_shape = jax.ShapeDtypeStruct((tiles, depth, width), jnp.bfloat16)
        out_specs = pl.BlockSpec((1, depth, width), lambda i, *_: (i, 0, 0))
    else:
        body = merged_kernel
        out_shape = (
            jax.ShapeDtypeStruct((tiles, slots, width, width), jnp.bfloat16),
            jax.ShapeDtypeStruct((feat_count, tiles * width), jnp.bfloat16),
        )
        out_specs = (
            pl.BlockSpec((1, slots, width, width), lambda i, *_: (i, 0, 0, 0)),
            pl.BlockSpec((feat_count, width), lambda i, *_: (0, i)),
        )
    map_rows = -(-(2 * slots + 2) // 8) * 8
    return pl.pallas_call(
        functools.partial(body, first, slots, span, count),
        out_shape=out_shape,
        grid_spec=pltpu.PrefetchScalarGridSpec(
            num_scalar_prefetch=3,
            grid=(tiles,),
            in_specs=in_specs,
            out_specs=out_specs,
            scratch_shapes=[pltpu.VMEM((map_rows, width), jnp.int32)] * 2,
        ),
        compiler_params=pltpu.CompilerParams(vmem_limit_bytes=32 * 2**20),
        cost_estimate=pl.CostEstimate(
            flops=tiles * slots * 8 * width**3,
            bytes_accessed=tiles * slots * width * width * 6,
            transcendentals=0,
        ),
    )(scal, own_cols, other_cols, adjacency, other, feats, other_feats, match_one, match_two)


def add_kernel(slots, arrived, tiles_in, feats_in, tiles_out, feats_out):
    width = arrived.shape[-1]
    for slot in range(slots):
        tiles_out[0, slot] = (
            tiles_in[0, slot].astype(jnp.float32)
            + arrived[0, slot * width : (slot + 1) * width, :].astype(jnp.float32)
        ).astype(jnp.bfloat16)
    feats_out[...] = (
        feats_in[...].astype(jnp.float32) + arrived[0, slots * width :, :].astype(jnp.float32)
    ).astype(jnp.bfloat16)


def added(first, arrived, tiles, feats):
    slots, width = tiles.shape[1:3]
    feat_count = feats.shape[0]
    tile_spec = pl.BlockSpec((1, slots, width, width), lambda i: (first + i, 0, 0, 0))
    feat_spec = pl.BlockSpec((feat_count, width), lambda i: (0, first + i))
    return pl.pallas_call(
        functools.partial(add_kernel, slots),
        out_shape=(
            jax.ShapeDtypeStruct(tiles.shape, tiles.dtype),
            jax.ShapeDtypeStruct(feats.shape, feats.dtype),
        ),
        grid=(arrived.shape[0],),
        in_specs=[
            pl.BlockSpec((1,) + arrived.shape[1:], lambda i: (i, 0, 0)),
            tile_spec,
            feat_spec,
        ],
        out_specs=(tile_spec, feat_spec),
        input_output_aliases={1: 0, 2: 1},
        compiler_params=pltpu.CompilerParams(vmem_limit_bytes=32 * 2**20),
        cost_estimate=pl.CostEstimate(
            flops=arrived.size, bytes_accessed=arrived.size * 6, transcendentals=0
        ),
    )(arrived, tiles, feats)


def per_device(features, adjacency, col_tiles, match_one, match_two):
    count, slots, width = adjacency.shape[:3]
    quarter = count // 4
    sub_count = lax.axis_size("sub")
    span = sub_count * count
    blk_index = lax.axis_index("blk")
    sub_index = lax.axis_index("sub")
    own_first = (blk_index * sub_count + sub_index) * count
    other_first = (blk_index * sub_count + (sub_index ^ 1)) * count
    blk_bit = blk_index % 2
    sub_bit = sub_index % 2
    grid = adjacency.reshape(quarter, 2, 2, slots, width, width)

    def raw(first, tiles, row_bit):
        zero = jnp.int32(0)
        piece = lax.dynamic_slice(
            grid,
            (jnp.int32(first), row_bit, 1 - sub_bit, zero, zero, zero),
            (tiles, 1, 1, slots, width, width),
        )
        return swapped(piece.reshape(tiles, slots, width, width), "sub")

    cuts = [(0, 1), (1, 1), (2, 2)]
    other_cols = swapped(col_tiles, "sub")
    other_feats = swapped(features, "sub")
    others = [raw(first, tiles, 1 - blk_bit) for first, tiles in cuts]
    other_keep = raw(0, quarter, blk_bit)
    send_scal = jnp.stack([1 - blk_bit, sub_bit, own_first, other_first])
    keep_scal = jnp.stack([blk_bit, sub_bit, own_first, other_first])
    arrived = []
    for (first, tiles), other in zip(cuts, others):
        parcel = merged(
            first, tiles, True, span, send_scal, col_tiles, other_cols, adjacency, other, features,
            other_feats, match_one, match_two,
        )
        arrived.append(swapped(parcel, "blk"))
    tiles_out, feats_out = merged(
        0, quarter, False, span, keep_scal, col_tiles, other_cols, adjacency, other_keep, features,
        other_feats, match_one, match_two,
    )
    for (first, _), part in zip(cuts, arrived):
        tiles_out, feats_out = added(first, part, tiles_out, feats_out)
    return tiles_out, feats_out


def solution(mesh):
    placed = (
        P(None, ("blk", "sub")),
        P(("blk", "sub"), None, None, None),
        P(("blk", "sub"), None),
        P(),
        P(),
    )
    return jax.shard_map(
        per_device,
        mesh=mesh,
        in_specs=placed,
        out_specs=(P(("blk", "sub"), None, None, None), P(None, ("blk", "sub"))),
        check_vma=False,
    )
```

time: 92.5 us -> 44.2 us (0.48)
  waiting for transfers between devices: 47.9 us -> 9.88 us
  Pallas kernels: 0 us -> 18.3 us
  local copies, waits for them, and re-layouts: 21.5 us -> 8 us
  matrix products: 9.71 us -> 0 us
  other arithmetic: 9.08 us -> 0.15 us
  starting transfers between devices: 2.92 us -> 6.77 us
    ppermute x4 -> x9, waiting for transfers between devices: 47.9 us -> 9.88 us  [swapped(): return lax.ppermute(value, axis, pairs)]
    pallas_call x0 -> x7, Pallas kernels: none -> 18.3 us  [the longest x4 13 us: merged(): pl.pallas_call(functools.partial(body, first, slots, span, count), out_sh...]
    another operation x4 -> x0, local copies, waits for them, and re-layouts: 13.5 us -> none
    dot_general x2 -> x0, matrix products: 9.71 us -> none  [column_side(): jnp.einsum('jkab,jkbc->jkac', blocks, hot, preferred_element_type=jnp.flo...]
    reshape x0 -> x3, local copies, waits for them, and re-layouts: none -> 5.05 us  [raw(): return swapped(piece.reshape(tiles, slots, width, width), 'sub')]
    squeeze x4 -> x0, local copies, waits for them, and re-layouts: 4.93 us -> none  [the longest x1 4.78 us: per_device(): keep_tiles = jnp.where(blk_even, grid_tiles[:, 0], grid_tiles[:, 1])]
    convert_element_type x5 -> x0, other arithmetic: 4.92 us -> none  [the longest x3 4.24 us: add_pair(): (first_part.astype(jnp.float32) + second_part.astype(jnp.float32)).astype...]
    ppermute x4 -> x9, starting transfers between devices: 2.92 us -> 6.77 us  [swapped(): return lax.ppermute(value, axis, pairs)]
  transfers between devices with their start and end apart: 4 -> 9, of which waited for: 2 -> 2; matrix products, arithmetic and copies ran while one was open for 2% -> 10% of each run, Pallas kernels for 0% -> 38%
where the time goes in v1:
time: 44.2 us; the launch traced here: 43.8 us
  Pallas kernels  18.3 us (41%)
  waiting for transfers between devices  9.88 us (22%)
  local copies, waits for them, and re-layouts  8 us (18%)
  starting transfers between devices  6.77 us (15%)
  between operations  0.75 us (2%)
    pallas_call x4, Pallas kernels, merged(): pl.pallas_call(functools.partial(body, first, slots, span, count), out_sh...  13 us
    ppermute x9, waiting for transfers between devices, swapped(): return lax.ppermute(value, axis, pairs)  9.88 us
    ppermute x9, starting transfers between devices, swapped(): return lax.ppermute(value, axis, pairs)  6.77 us
    pallas_call x3, Pallas kernels, added(): pl.pallas_call(functools.partial(add_kernel, slots), out_shape=(jax.Shape...  5.27 us
    reshape x3, local copies, waits for them, and re-layouts, raw(): return swapped(piece.reshape(tiles, slots, width, width), 'sub')  5.05 us
    unnamed x9, local copies, waits for them, and re-layouts  2.95 us
  transfers between devices with their start and end apart: 9, of which 2 were waited for; matrix products, arithmetic and copies ran while one was open for 10% of the time, Pallas kernels for 38%

profile of v1, /device:TPU:0, one launch (start us, length us, event | category | flops | bytes accessed | tf_op | source)
XLA Modules:
  0.0 43.8 jit_solution(15567543680161824920)
XLA Ops:
  0.6 0.0 copy-start.2
  0.6 0.0 copy-start.1
  0.7 0.0 copy-start.3
  0.7 1.4 %dynamic-slice_bitcast_fusion = bf16[4,8,128,128]{3,2,1,0:T(8,128)(2,1)S(1)} fusion(bf16[4,2,2,8,128,128]{5,4,3,2,1,0:T(8,128)(2,1)} %bitcast.16, s32[]{:T(128)S(6)} %select_n.29, s32[]{:T(128)S(6)} %select_n.28), kind=kLoop, calls=%fused_computation | loop fusion | bytes 2097160 | tf_op jit(solution)/shard_map/reshape | solution.py:200
  2.1 0.5 %collective-permute-start.8 = (bf16[4,8,128,128]{3,2,1,0:T(8,128)(2,1)S(1)}, bf16[4,8,128,128]{3,2,1,0:T(8,128)(2,1)S(1)}, u32[]{:S(2)}, u32[]{:S(2)}) collective-permute-start(bf16[4,8,128,128]{3,2,1,0:T(8,128)(2,1)S(1)} %dynamic-slice_bitcast_fusion), channel_id=1, source_target_pairs={{0,1},{1,0},{2,3},{3,2},{4,5},{5,4},{6,7},{7,6},{8,9},{9,8},{10,11... | collective-permute-start | bytes 3145736 | tf_op jit(solution)/shard_map/ppermute | solution.py:13
  2.6 1.9 %dynamic-slice_bitcast_fusion.1 = bf16[2,8,128,128]{3,2,1,0:T(8,128)(2,1)} fusion(bf16[4,2,2,8,128,128]{5,4,3,2,1,0:T(8,128)(2,1)} %bitcast.17, s32[]{:T(128)S(6)} %select_n.27, s32[]{:T(128)S(6)} %select_n.28), kind=kLoop, calls=%fused_computation.1 | loop fusion | bytes 1048584 | tf_op jit(solution)/shard_map/reshape | solution.py:200
  4.5 0.1 collective-permute-start.1
  4.6 0.8 %copy.14.refs_1_.own_cols = s32[16,8]{1,0:T(8,128)S(1)} copy(s32[16,8]{0,1:T(8,128)} %param.7) | data formatting | bytes 1024 | tf_op args[2]
  5.3 0.5 %collective-permute-start = (s32[16,8]{1,0:T(8,128)S(1)}, s32[16,8]{1,0:T(8,128)S(1)}, u32[]{:S(2)}, u32[]{:S(2)}) collective-permute-start(s32[16,8]{1,0:T(8,128)S(1)} %copy.14.refs_1_.own_cols), channel_id=1, source_target_pairs={{0,1},{1,0},{2,3},{3,2},{4,5},{5,4},{6,7},{7,6},{8,9},{9,8},{10,11... | collective-permute-start | bytes 1544 | tf_op jit(solution)/shard_map/ppermute | solution.py:13
  5.8 0.1 collective-permute-start.2
  5.8 1.8 %dynamic-slice_bitcast_fusion.2 = (bf16[1,8,128,128]{3,2,1,0:T(8,128)(2,1)}, bf16[1,8,128,128]{3,2,1,0:T(8,128)(2,1)S(1)}) fusion(bf16[4,2,2,8,128,128]{5,4,3,2,1,0:T(8,128)(2,1)} %bitcast.18, s32[]{:T(128)S(6)} %select_n.27, s32[]{:T(128)S(6)} %select_n.28), kind=kLoop, calls=%fused_computation.2 | loop fusion | bytes 1048584 | tf_op jit(solution)/shard_map/reshape | solution.py:200
  7.6 0.5 %collective-permute-start.6 = (bf16[1,8,128,128]{3,2,1,0:T(8,128)(2,1)}, bf16[1,8,128,128]{3,2,1,0:T(8,128)(2,1)S(1)}, u32[]{:S(2)}, u32[]{:S(2)}) collective-permute-start(bf16[1,8,128,128]{3,2,1,0:T(8,128)(2,1)} %get-tuple-element.14), channel_id=1, source_target_pairs={{0,1},{1,0},{2,3},{3,2},{4,5},{5,4},{6,7},{7,6},{8,9},{9,8},{10,11... | collective-permute-start | bytes 786440 | tf_op jit(solution)/shard_map/ppermute | solution.py:13
  8.0 0.1 add_add_fusion.refs_0_
  8.1 0.0 collective-permute-done.refs_2_.other_cols
  8.1 0.1 collective-permute-start.4
  8.2 0.0 collective-permute-done.2.refs_6_.other_feat
  8.2 0.0 collective-permute-done.1.refs_4_
  8.2 0.0 copy-done.2
  8.2 0.0 copy-done.1
  8.2 0.0 copy-done.3
  8.2 0.0 copy-start
  8.2 2.2 %copy-done = bf16[16,8,128,128]{3,2,1,0:T(8,128)(2,1)S(1)} copy-done((bf16[16,8,128,128]{3,2,1,0:T(8,128)(2,1)S(1)}, bf16[16,8,128,128]{3,2,1,0:T(8,128)(2,1)}, u32[]{:S(2)}) %copy-start) | copy-done | bytes 4194328
  10.4 3.1 %shard_map.68 = bf16[2,1040,128]{2,1,0:T(8,128)(2,1)S(1)} custom-call(s32[4]{0:T(128)S(1)} %add_add_fusion.refs_0_, s32[16,8]{1,0:T(8,128)S(1)} %copy.14.refs_1_.own_cols, s32[16,8]{1,0:T(8,128)S(1)} %collective-permute-done.refs_2_.other_cols, bf16[16,8,128,128]{3,2,1,0:T(8,128)(2,1)S(1)} %copy-done, ...), custom_call_target="tpu_custom_call" | custom-call | flops 268435456 | bytes 1572864 | tf_op jit(solution)/shard_map/pallas_call | solution.py:123
  13.5 3.0 %collective-permute-start.3 = (bf16[2,1040,128]{2,1,0:T(8,128)(2,1)S(1)}, bf16[2,1040,128]{2,1,0:T(8,128)(2,1)S(1)}, u32[]{:S(2)}, u32[]{:S(2)}) collective-permute-start(bf16[2,1040,128]{2,1,0:T(8,128)(2,1)S(1)} %shard_map.68), channel_id=1, source_target_pairs={{0,4},{4,0},{8,12},{12,8},{16,20},{20,16},{24,28},{28,24},{1,5},{5... | collective-permute-start | bytes 1597448 | tf_op jit(solution)/shard_map/ppermute | solution.py:13
  16.5 0.0 collective-permute-done.6.refs_4_
  16.5 1.9 %shard_map.70 = bf16[1,1040,128]{2,1,0:T(8,128)(2,1)S(1)} custom-call(s32[4]{0:T(128)S(1)} %add_add_fusion.refs_0_, s32[16,8]{1,0:T(8,128)S(1)} %copy.14.refs_1_.own_cols, s32[16,8]{1,0:T(8,128)S(1)} %collective-permute-done.refs_2_.other_cols, bf16[16,8,128,128]{3,2,1,0:T(8,128)(2,1)S(1)} %copy-done, ...), custom_call_target="tpu_custom_call" | custom-call | flops 134217728 | bytes 786432 | tf_op jit(solution)/shard_map/pallas_call | solution.py:123
  18.4 0.1 collective-permute-start.7
  18.5 0.0 collective-permute-done.4.refs_4_
  18.5 1.9 %shard_map.69 = bf16[1,1040,128]{2,1,0:T(8,128)(2,1)S(1)} custom-call(s32[4]{0:T(128)S(1)} %add_add_fusion.refs_0_, s32[16,8]{1,0:T(8,128)S(1)} %copy.14.refs_1_.own_cols, s32[16,8]{1,0:T(8,128)S(1)} %collective-permute-done.refs_2_.other_cols, bf16[16,8,128,128]{3,2,1,0:T(8,128)(2,1)S(1)} %copy-done, ...), custom_call_target="tpu_custom_call" | custom-call | flops 134217728 | bytes 786432 | tf_op jit(solution)/shard_map/pallas_call | solution.py:123
  20.4 2.1 %collective-permute-start.5 = (bf16[1,1040,128]{2,1,0:T(8,128)(2,1)S(1)}, bf16[1,1040,128]{2,1,0:T(8,128)(2,1)S(1)}, u32[]{:S(2)}, u32[]{:S(2)}) collective-permute-start(bf16[1,1040,128]{2,1,0:T(8,128)(2,1)S(1)} %shard_map.69), channel_id=1, source_target_pairs={{0,4},{4,0},{8,12},{12,8},{16,20},{20,16},{24,28},{28,24},{1,5},{5... | collective-permute-start | bytes 798728 | tf_op jit(solution)/shard_map/ppermute | solution.py:13
  22.5 0.1 add_add_fusion.1.scal
  22.6 0.0 collective-permute-done.8.other
  22.6 6.1 %shard_map.71 = (bf16[4,8,128,128]{3,2,1,0:T(8,128)(2,1)}, bf16[16,512]{1,0:T(8,128)(2,1)}) custom-call(s32[4]{0:T(128)S(1)} %add_add_fusion.1.scal, s32[16,8]{1,0:T(8,128)S(1)} %copy.14.refs_1_.own_cols, s32[16,8]{1,0:T(8,128)S(1)} %collective-permute-done.refs_2_.other_cols, bf16[16,8,128,128]{3,2,1,0:T(8,128)(2,1)S(1)} %copy-done, ...), custom_call_target="tpu_custom_call" | custom-call | flops 536870912 | bytes 3145728 | tf_op jit(solution)/shard_map/pallas_call | solution.py:123
  28.7 6.5 %collective-permute-done.7.arrived = bf16[1,1040,128]{2,1,0:T(8,128)(2,1)S(1)} collective-permute-done((bf16[1,1040,128]{2,1,0:T(8,128)(2,1)S(1)}, bf16[1,1040,128]{2,1,0:T(8,128)(2,1)S(1)}, u32[]{:S(2)}, u32[]{:S(2)}) %collective-permute-start.7) | collective-permute-done | bytes 266272 | tf_op jit(solution)/shard_map/ppermute | solution.py:13
  35.2 1.7 %shard_map.72 = (bf16[4,8,128,128]{3,2,1,0:T(8,128)(2,1)}, bf16[16,512]{1,0:T(8,128)(2,1)}) custom-call(bf16[1,1040,128]{2,1,0:T(8,128)(2,1)S(1)} %collective-permute-done.7.arrived, bf16[4,8,128,128]{3,2,1,0:T(8,128)(2,1)} %get-tuple-element.8.tiles_in, bf16[16,512]{1,0:T(8,128)(2,1)} %get-tuple-element.9.feats_in), custom_call_target="tpu_custom_call", output_to_operand_aliasing={{0}: (1, {}), {1}: (2, {})} | custom-call | flops 133120 | bytes 798720 | tf_op jit(solution)/shard_map/pallas_call | solution.py:159
  36.9 3.4 %collective-permute-done.5.arrived = bf16[1,1040,128]{2,1,0:T(8,128)(2,1)S(1)} collective-permute-done((bf16[1,1040,128]{2,1,0:T(8,128)(2,1)S(1)}, bf16[1,1040,128]{2,1,0:T(8,128)(2,1)S(1)}, u32[]{:S(2)}, u32[]{:S(2)}) %collective-permute-start.5) | collective-permute-done | bytes 266272 | tf_op jit(solution)/shard_map/ppermute | solution.py:13
  40.3 1.7 %shard_map.73 = (bf16[4,8,128,128]{3,2,1,0:T(8,128)(2,1)}, bf16[16,512]{1,0:T(8,128)(2,1)}) custom-call(bf16[1,1040,128]{2,1,0:T(8,128)(2,1)S(1)} %collective-permute-done.5.arrived, bf16[4,8,128,128]{3,2,1,0:T(8,128)(2,1)} %get-tuple-element.10.tiles_in, bf16[16,512]{1,0:T(8,128)(2,1)} %get-tuple-element.11.feats_in), custom_call_target="tpu_custom_call", output_to_operand_aliasing={{0}: (1, {}), {1}: (2, {})} | custom-call | flops 133120 | bytes 798720 | tf_op jit(solution)/shard_map/pallas_call | solution.py:159
  42.0 0.0 collective-permute-done.3.arrived
  42.0 1.8 %shard_map.74 = (bf16[4,8,128,128]{3,2,1,0:T(8,128)(2,1)}, bf16[16,512]{1,0:T(8,128)(2,1)}) custom-call(bf16[2,1040,128]{2,1,0:T(8,128)(2,1)S(1)} %collective-permute-done.3.arrived, bf16[4,8,128,128]{3,2,1,0:T(8,128)(2,1)} %get-tuple-element.12.tiles_in, bf16[16,512]{1,0:T(8,128)(2,1)} %get-tuple-element.13.feats_in), custom_call_target="tpu_custom_call", output_to_operand_aliasing={{0}: (1, {}), {1}: (2, {})} | custom-call | flops 266240 | bytes 1597440 | tf_op jit(solution)/shard_map/pallas_call | solution.py:159
Async XLA Ops:
  0.6 7.6 %copy-start.2 = (bf16[16,2048]{1,0:T(8,128)(2,1)S(1)}, bf16[16,2048]{1,0:T(8,128)(2,1)}, u32[]{:S(2)}) copy-start(bf16[16,2048]{1,0:T(8,128)(2,1)} %own_feat.1) | copy-start | bytes 196612
  0.6 7.6 %copy-start.1 = (s32[256,128]{1,0:T(8,128)S(1)}, s32[256,128]{1,0:T(8,128)}, u32[]{:S(2)}) copy-start(s32[256,128]{1,0:T(8,128)} %match_one.1) | copy-start | bytes 393220
  0.7 7.6 %copy-start.3 = (s32[128,128]{1,0:T(8,128)S(1)}, s32[128,128]{1,0:T(8,128)}, u32[]{:S(2)}) copy-start(s32[128,128]{1,0:T(8,128)} %match_two.1) | copy-start | bytes 196612
  2.1 20.5 %collective-permute-start.8 = (bf16[4,8,128,128]{3,2,1,0:T(8,128)(2,1)S(1)}, bf16[4,8,128,128]{3,2,1,0:T(8,128)(2,1)S(1)}, u32[]{:S(2)}, u32[]{:S(2)}) collective-permute-start(bf16[4,8,128,128]{3,2,1,0:T(8,128)(2,1)S(1)} %dynamic-slice_bitcast_fusion), channel_id=1, source_target_pairs={{0,1},{1,0},{2,3},{3,2},{4,5},{5,4},{6,7},{7,6},{8,9},{9,8},{10,11... | collective-permute-start | bytes 3145736 | tf_op jit(solution)/shard_map/ppermute | solution.py:13
  4.5 3.7 %collective-permute-start.1 = (bf16[2,8,128,128]{3,2,1,0:T(8,128)(2,1)}, bf16[2,8,128,128]{3,2,1,0:T(8,128)(2,1)S(1)}, u32[]{:S(2)}, u32[]{:S(2)}) collective-permute-start(bf16[2,8,128,128]{3,2,1,0:T(8,128)(2,1)} %dynamic-slice_bitcast_fusion.1), channel_id=1, source_target_pairs={{0,1},{1,0},{2,3},{3,2},{4,5},{5,4},{6,7},{7,6},{8,9},{9,8},{10,11... | collective-permute-start | bytes 1572872 | tf_op jit(solution)/shard_map/ppermute | solution.py:13
  5.3 2.8 %collective-permute-start = (s32[16,8]{1,0:T(8,128)S(1)}, s32[16,8]{1,0:T(8,128)S(1)}, u32[]{:S(2)}, u32[]{:S(2)}) collective-permute-start(s32[16,8]{1,0:T(8,128)S(1)} %copy.14.refs_1_.own_cols), channel_id=1, source_target_pairs={{0,1},{1,0},{2,3},{3,2},{4,5},{5,4},{6,7},{7,6},{8,9},{9,8},{10,11... | collective-permute-start | bytes 1544 | tf_op jit(solution)/shard_map/ppermute | solution.py:13
  5.8 2.4 %collective-permute-start.2 = (bf16[16,2048]{1,0:T(8,128)(2,1)}, bf16[16,2048]{1,0:T(8,128)(2,1)S(1)}, u32[]{:S(2)}, u32[]{:S(2)}) collective-permute-start(bf16[16,2048]{1,0:T(8,128)(2,1)} %own_feat.1), channel_id=1, source_target_pairs={{0,1},{1,0},{2,3},{3,2},{4,5},{5,4},{6,7},{7,6},{8,9},{9,8},{10,11... | collective-permute-start | bytes 196616 | tf_op jit(solution)/shard_map/ppermute | solution.py:13
  7.6 9.0 %collective-permute-start.6 = (bf16[1,8,128,128]{3,2,1,0:T(8,128)(2,1)}, bf16[1,8,128,128]{3,2,1,0:T(8,128)(2,1)S(1)}, u32[]{:S(2)}, u32[]{:S(2)}) collective-permute-start(bf16[1,8,128,128]{3,2,1,0:T(8,128)(2,1)} %get-tuple-element.14), channel_id=1, source_target_pairs={{0,1},{1,0},{2,3},{3,2},{4,5},{5,4},{6,7},{7,6},{8,9},{9,8},{10,11... | collective-permute-start | bytes 786440 | tf_op jit(solution)/shard_map/ppermute | solution.py:13
  8.1 10.4 %collective-permute-start.4 = (bf16[1,8,128,128]{3,2,1,0:T(8,128)(2,1)S(1)}, bf16[1,8,128,128]{3,2,1,0:T(8,128)(2,1)S(1)}, u32[]{:S(2)}, u32[]{:S(2)}) collective-permute-start(bf16[1,8,128,128]{3,2,1,0:T(8,128)(2,1)S(1)} %get-tuple-element.15), channel_id=1, source_target_pairs={{0,1},{1,0},{2,3},{3,2},{4,5},{5,4},{6,7},{7,6},{8,9},{9,8},{10,11... | collective-permute-start | bytes 786440 | tf_op jit(solution)/shard_map/ppermute | solution.py:13
  8.2 2.2 %copy-start = (bf16[16,8,128,128]{3,2,1,0:T(8,128)(2,1)S(1)}, bf16[16,8,128,128]{3,2,1,0:T(8,128)(2,1)}, u32[]{:S(2)}) copy-start(bf16[16,8,128,128]{3,2,1,0:T(8,128)(2,1)} %own.1) | copy-start | bytes 12582916
  13.5 28.4 %collective-permute-start.3 = (bf16[2,1040,128]{2,1,0:T(8,128)(2,1)S(1)}, bf16[2,1040,128]{2,1,0:T(8,128)(2,1)S(1)}, u32[]{:S(2)}, u32[]{:S(2)}) collective-permute-start(bf16[2,1040,128]{2,1,0:T(8,128)(2,1)S(1)} %shard_map.68), channel_id=1, source_target_pairs={{0,4},{4,0},{8,12},{12,8},{16,20},{20,16},{24,28},{28,24},{1,5},{5... | collective-permute-start | bytes 1597448 | tf_op jit(solution)/shard_map/ppermute | solution.py:13
  18.4 16.7 %collective-permute-start.7 = (bf16[1,1040,128]{2,1,0:T(8,128)(2,1)S(1)}, bf16[1,1040,128]{2,1,0:T(8,128)(2,1)S(1)}, u32[]{:S(2)}, u32[]{:S(2)}) collective-permute-start(bf16[1,1040,128]{2,1,0:T(8,128)(2,1)S(1)} %shard_map.70), channel_id=1, source_target_pairs={{0,4},{4,0},{8,12},{12,8},{16,20},{20,16},{24,28},{28,24},{1,5},{5... | collective-permute-start | bytes 798728 | tf_op jit(solution)/shard_map/ppermute | solution.py:13
  20.4 19.8 %collective-permute-start.5 = (bf16[1,1040,128]{2,1,0:T(8,128)(2,1)S(1)}, bf16[1,1040,128]{2,1,0:T(8,128)(2,1)S(1)}, u32[]{:S(2)}, u32[]{:S(2)}) collective-permute-start(bf16[1,1040,128]{2,1,0:T(8,128)(2,1)S(1)} %shard_map.69), channel_id=1, source_target_pairs={{0,4},{4,0},{8,12},{12,8},{16,20},{20,16},{24,28},{28,24},{1,5},{5... | collective-permute-start | bytes 798728 | tf_op jit(solution)/shard_map/ppermute | solution.py:13

commit v2 on v0

v2 whole, which is shorter than its diff:
```python
import functools

import jax
import jax.numpy as jnp
from jax import lax
from jax.experimental import pallas as pl
from jax.experimental.pallas import tpu as pltpu
from jax.sharding import PartitionSpec as P

HALF = 16
LIMIT = 48 * 2**20
LIGHT = pl.CostEstimate(flops=1, bytes_accessed=1, transcendentals=0)
VMEM = pl.BlockSpec(memory_space=pltpu.VMEM)
HBM = pl.BlockSpec(memory_space=pltpu.HBM)
ANY = pl.BlockSpec(memory_space=pl.ANY)


def swapped(value, axis):
    pairs = [(source, source ^ 1) for source in range(lax.axis_size(axis))]
    return lax.ppermute(value, axis, pairs)


def in_vmem(value):
    return pltpu.with_memory_space_constraint(value, pltpu.VMEM)


def in_hbm(value):
    return pltpu.with_memory_space_constraint(value, pltpu.HBM)


def split_by(value, size):
    if size & (size - 1) == 0:
        return value >> (size.bit_length() - 1), value & (size - 1)
    return value // size, value % size


def tile_at(phase, piece, partner):
    blk_bit = lax.axis_index("blk") & 1
    sub_bit = lax.axis_index("sub") & 1
    row_bit = blk_bit if phase == 1 else 1 - blk_bit
    return 4 * piece + 2 * row_bit + (1 - sub_bit if partner else sub_bit)


def start(source, target, sem):
    copy = pltpu.make_async_copy(source, target, sem)
    copy.start()
    return copy


def compose_maps(pick, span, count, cols, one_table, two_table, one_rows, two_rows, out):
    slots = cols.shape[0]
    lanes = lax.broadcasted_iota(jnp.int32, (1, one_table.shape[-1]), 1)

    def put(row, column_id):
        block, inside = split_by(column_id, span)
        pair_block, high_one = split_by(block, 2)
        sub, place = split_by(inside, count)
        sub_pair, high_two = split_by(sub, 2)
        pair = pair_block * span + inside
        group = pair_block * (span // 2) + sub_pair * count + place
        one_rows[pl.ds(row, 1), :] = jnp.where(high_one == 1, one_table[pl.ds(pair, 1), :], lanes)
        two_rows[pl.ds(row, 1), :] = jnp.where(high_two == 1, two_table[pl.ds(group, 1), :], lanes)

    one_rows[...] = jnp.zeros_like(one_rows)
    two_rows[...] = jnp.zeros_like(two_rows)
    tile = tile_at(*pick)
    for slot in range(slots):
        put(slot, cols[slot, tile])
    put(slots, lax.axis_index("blk") * span + lax.axis_index("sub") * count + tile)
    maps = jnp.take_along_axis(two_rows[...], one_rows[...], axis=1)
    out[...] = maps.astype(jnp.float32).astype(out.dtype)


def merge_tile(slots, own, other, own_side, other_side, out):
    width = own.shape[-1]
    sides = lax.broadcasted_iota(jnp.int32, (width, width), 1).astype(jnp.float32)
    along = lax.broadcasted_iota(jnp.int32, (width, width), 0).astype(jnp.float32)
    across = jnp.concatenate([own_side[:HALF], other_side[:HALF]], 0).astype(jnp.float32)
    down = across.T

    def dot(a, b):
        return jnp.dot(a, b, preferred_element_type=jnp.float32)

    def columns(row):
        return jnp.concatenate(
            [
                (down[:, place : place + 1] == sides).astype(jnp.bfloat16)
                for place in (row, HALF + row)
            ],
            0,
        )

    own_rows = (across[slots : slots + 1, :] == along).astype(jnp.bfloat16)
    other_rows = (across[HALF + slots : HALF + slots + 1, :] == along).astype(jnp.bfloat16)
    for pair in range(slots // 2):
        both = [2 * pair, 2 * pair + 1]

        def moved(hot, ref):
            blocks = [ref[slot * width : (slot + 1) * width, :] for slot in both]
            return dot(hot, jnp.concatenate(blocks, 1)).astype(jnp.bfloat16)

        own_two = moved(own_rows, own)
        other_two = moved(other_rows, other)
        for half, slot in enumerate(both):
            part = slice(half * width, (half + 1) * width)
            lhs = jnp.concatenate([own_two[:, part], other_two[:, part]], 1)
            out[slot * width : (slot + 1) * width, :] = dot(lhs, columns(slot)).astype(out.dtype)
    feats = jnp.concatenate([own_side[HALF:], other_side[HALF:]], 1)
    out[slots * width :, :] = dot(feats, columns(slots)).astype(out.dtype)


def work_kernel(plan, refs):
    rows = plan.rows
    copies, small = [], []
    if plan.picks:
        adjacency, features, cols, match_one, match_two = [refs[at] for at in plan.sources]
        one_table, two_table, cols_here, one_rows, two_rows, sems = [refs[at] for at in plan.scratch]
        width = adjacency.shape[-1]
        small = [
            start(match_one, one_table, sems.at[0]),
            start(match_two, two_table, sems.at[1]),
            start(cols, cols_here, sems.at[2]),
        ]
        sides = []
        for i, (pick, (main, main_at, side, side_at)) in enumerate(zip(plan.picks, plan.targets)):
            tile = tile_at(*pick)
            lanes = pl.ds(pl.multiple_of(tile * width, width), width)
            sides.append(refs[side].at[pl.ds(side_at, HALF)])
            copies += [
                start(adjacency.at[tile], refs[main].at[pl.ds(main_at, rows)], sems.at[3 + 2 * i]),
                start(
                    features.at[:, lanes],
                    refs[side].at[pl.ds(side_at + HALF, features.shape[0])],
                    sems.at[4 + 2 * i],
                ),
            ]
    for i, (own, other) in enumerate(plan.merges):
        out = refs[plan.out].at[i]
        tiles = [refs[main].at[pl.ds(at, rows)] for main, at, _, _ in (own, other)]
        ends = [refs[side][at : at + plan.depth - rows, :] for _, _, side, at in (own, other)]
        merge_tile(rows // out.shape[-1], *tiles, *ends, out)
    for copy in small:
        copy.wait()
    for i, pick in enumerate(plan.picks):
        compose_maps(
            pick, plan.span, plan.count, cols_here, one_table, two_table, one_rows, two_rows,
            sides[i],
        )
    for copy in copies:
        copy.wait()


class Plan:
    pass


class Work:
    def __init__(self, features, adjacency, cols, match_one, match_two, span):
        self.sources = [in_hbm(x) for x in (adjacency, features, cols, match_one, match_two)]
        self.span = span
        self.own, self.other = {}, {}

    def run(self, merges=(), keys=(), leaving=(), apart=False, after=()):
        adjacency, features, cols, match_one, match_two = self.sources
        rows, width = adjacency.shape[1:]
        plan = Plan()
        plan.rows, plan.depth = rows, rows + HALF + features.shape[0]
        plan.span, plan.count = self.span, cols.shape[1]
        plan.picks = [(*key, True) for key in leaving] + [(*key, False) for key in keys]
        ins, specs, shapes, scratch = [], [], [], []

        def take(value, spec):
            for place, known in enumerate(ins):
                if known is value:
                    return place
            ins.append(value)
            specs.append(spec)
            return len(ins) - 1

        plan.sources = [take(value, HBM) for value in self.sources] if plan.picks else []
        plan.merges = [
            [
                (take(main, VMEM), at, take(side, VMEM), side_at)
                for main, at, side, side_at in (self.own[key], self.other[key])
            ]
            for key in merges
        ]
        for value in after:
            take(value, ANY)

        def give(depth):
            shapes.append(pltpu.VMEM((depth, width), adjacency.dtype))
            return len(ins) + len(shapes) - 1

        plan.out = len(ins)
        if merges:
            depth = rows + features.shape[0]
            shapes.append(pltpu.VMEM((len(merges), depth, width), adjacency.dtype))
        extra = plan.depth - rows
        if apart:
            side = give(len(leaving) * extra)
            plan.targets = [(give(rows), 0, side, i * extra) for i in range(len(leaving))]
        else:
            mains = [give(plan.depth) for _ in leaving]
            plan.targets = [(main, 0, main, rows) for main in mains]
        if keys:
            pack = give(len(keys) * plan.depth)
            plan.targets += [
                (pack, i * plan.depth, pack, i * plan.depth + rows) for i in range(len(keys))
            ]
        if plan.picks:
            scratch = [
                pltpu.VMEM(match_one.shape, jnp.int32),
                pltpu.VMEM(match_two.shape, jnp.int32),
                pltpu.SMEM(cols.shape, jnp.int32),
                pltpu.VMEM((HALF, width), jnp.int32),
                pltpu.VMEM((HALF, width), jnp.int32),
                pltpu.SemaphoreType.DMA((3 + 2 * len(plan.picks),)),
            ]
        plan.scratch = [len(ins) + len(shapes) + i for i in range(len(scratch))]
        outs = pl.pallas_call(
            lambda *refs: work_kernel(plan, refs),
            out_shape=shapes,
            in_specs=specs,
            out_specs=[VMEM] * len(shapes),
            scratch_shapes=scratch,
            compiler_params=pltpu.CompilerParams(vmem_limit_bytes=LIMIT),
            cost_estimate=LIGHT,
            name="work",
        )(*ins)
        made = {len(ins) + i: value for i, value in enumerate(outs)}
        crossed = {}
        for pick, (main, main_at, side, side_at) in zip(plan.picks, plan.targets):
            where = self.other if pick[2] else self.own
            for place in (main, side):
                if place not in crossed:
                    value = swapped(made[place], "sub") if pick[2] else made[place]
                    crossed[place] = in_vmem(value)
            where[pick[:2]] = (crossed[main], main_at, crossed[side], side_at)
        return outs[0]


def add_kernel(first, slots, arrived, kept, *rest):
    tiles_out, feats_out, tile_sum, feat_sum, sems = rest[-5:]
    width = arrived.shape[-1]
    rows = slots * width
    tiles = arrived.shape[0]
    copies = []
    for i in range(tiles):
        total = kept[first + i].astype(jnp.float32) + arrived[i].astype(jnp.float32)
        total = total.astype(jnp.bfloat16)
        tile_sum[i] = total[:rows]
        feat_sum[:, i * width : (i + 1) * width] = total[rows:]
        copies.append(
            pltpu.make_async_copy(tile_sum.at[i], tiles_out.at[first + i], sems.at[i])
        )
        copies[-1].start()
    copies.append(
        pltpu.make_async_copy(
            feat_sum, feats_out.at[:, pl.ds(first * width, tiles * width)], sems.at[tiles]
        )
    )
    copies[-1].start()
    for copy in copies:
        copy.wait()


def added(first, slots, feat_count, arrived, kept, before):
    tiles, depth, width = arrived.shape
    rows = slots * width
    quarter = kept.shape[0]
    shapes = (
        jax.ShapeDtypeStruct((quarter, rows, width), jnp.bfloat16),
        jax.ShapeDtypeStruct((feat_count, quarter * width), jnp.bfloat16),
    )
    before = [] if before is None else list(before)
    return pl.pallas_call(
        functools.partial(add_kernel, first, slots),
        out_shape=shapes,
        in_specs=[VMEM, VMEM] + [HBM] * len(before),
        out_specs=(HBM, HBM),
        scratch_shapes=[
            pltpu.VMEM((tiles, rows, width), jnp.bfloat16),
            pltpu.VMEM((feat_count, tiles * width), jnp.bfloat16),
            pltpu.SemaphoreType.DMA((tiles + 1,)),
        ],
        input_output_aliases={2: 0, 3: 1} if before else {},
        compiler_params=pltpu.CompilerParams(vmem_limit_bytes=LIMIT),
        cost_estimate=LIGHT,
        name="add",
    )(in_vmem(arrived), in_vmem(kept), *before)


def per_device(features, adjacency, col_tiles, match_one, match_two):
    count, slots, width = adjacency.shape[:3]
    feat_count = features.shape[0]
    quarter = count // 4
    span = lax.axis_size("sub") * count
    blocks = adjacency.reshape(count, slots * width, width)
    work = Work(features, blocks, col_tiles.T, match_one, match_two, span)

    send = [(0, piece) for piece in range(quarter)]
    keep = [(1, piece) for piece in range(quarter)]
    first = work.run(leaving=send[:1])
    work.run(keys=send[:2], leaving=send[1:2], after=[first])
    more = {1: send[2:], 2: keep}
    arrived = []
    after = []
    for piece in range(quarter):
        new = more.get(piece, [])
        parcel = work.run(
            merges=send[piece : piece + 1], keys=new, leaving=new, apart=bool(new), after=after
        )
        arrived.append(swapped(parcel, "blk"))
        after = [parcel] + arrived[piece - 1 : piece] * (piece >= 1)
    kept = work.run(merges=keep, after=[parcel])
    out = None
    for piece, part in enumerate(arrived):
        out = added(piece, slots, feat_count, part, kept, out)
    return out[0].reshape(quarter, slots, width, width), out[1]


def solution(mesh):
    placed = (
        P(None, ("blk", "sub")),
        P(("blk", "sub"), None, None, None),
        P(("blk", "sub"), None),
        P(),
        P(),
    )
    return jax.shard_map(
        per_device,
        mesh=mesh,
        in_specs=placed,
        out_specs=(P(("blk", "sub"), None, None, None), P(None, ("blk", "sub"))),
        check_vma=False,
    )
```

time: 92.5 us -> 33.4 us (0.36)
  waiting for transfers between devices: 47.9 us -> 7.88 us
  local copies, waits for them, and re-layouts: 21.5 us -> 0 us
  Pallas kernels: 0 us -> 15.2 us
  matrix products: 9.71 us -> 0 us
  other arithmetic: 9.08 us -> 0 us
  starting transfers between devices: 2.92 us -> 9.38 us
    ppermute x4 -> x14, waiting for transfers between devices: 47.9 us -> 7.88 us  [swapped(): return lax.ppermute(value, axis, pairs)]
    pallas_call x0 -> x11, Pallas kernels: none -> 15.2 us  [the longest x7 12 us: run(): pl.pallas_call(lambda *refs: work_kernel(plan, refs), out_shape=shapes, i...]
    another operation x4 -> x0, local copies, waits for them, and re-layouts: 13.5 us -> none
    dot_general x2 -> x0, matrix products: 9.71 us -> none  [column_side(): jnp.einsum('jkab,jkbc->jkac', blocks, hot, preferred_element_type=jnp.flo...]
    ppermute x4 -> x14, starting transfers between devices: 2.92 us -> 9.38 us  [swapped(): return lax.ppermute(value, axis, pairs)]
    squeeze x4 -> x0, local copies, waits for them, and re-layouts: 4.93 us -> none  [the longest x1 4.78 us: per_device(): keep_tiles = jnp.where(blk_even, grid_tiles[:, 0], grid_tiles[:, 1])]
    convert_element_type x5 -> x0, other arithmetic: 4.92 us -> none  [the longest x3 4.24 us: add_pair(): (first_part.astype(jnp.float32) + second_part.astype(jnp.float32)).astype...]
    select_n x8 -> x0, other arithmetic: 3.47 us -> none  [the longest x1 3.16 us: per_device(): send_tiles = jnp.where(blk_even, grid_tiles[:, 1], grid_tiles[:, 0])]
  transfers between devices with their start and end apart: 4 -> 14, of which waited for: 2 -> 6; matrix products, arithmetic and copies ran while one was open for 2% -> 0% of each run, Pallas kernels for 0% -> 40%
where the time goes in v2:
time: 33.4 us; the launch traced here: 33.2 us
  Pallas kernels  15.2 us (46%)
  starting transfers between devices  9.38 us (28%)
  waiting for transfers between devices  7.88 us (24%)
  between operations  0.74 us (2%)
    pallas_call x7, Pallas kernels, run(): pl.pallas_call(lambda *refs: work_kernel(plan, refs), out_shape=shapes, i...  12 us
    ppermute x14, starting transfers between devices, swapped(): return lax.ppermute(value, axis, pairs)  9.38 us
    ppermute x14, waiting for transfers between devices, swapped(): return lax.ppermute(value, axis, pairs)  7.88 us
    pallas_call x4, Pallas kernels, added(): pl.pallas_call(functools.partial(add_kernel, first, slots), out_shape=sha...  3.15 us
  transfers between devices with their start and end apart: 14, of which 6 were waited for; matrix products, arithmetic and copies ran while one was open for 0% of the time, Pallas kernels for 40%

profile of v2, /device:TPU:0, one launch (start us, length us, event | category | flops | bytes accessed | tf_op | source)
XLA Modules:
  0.0 33.2 jit_solution(6673801889440589509)
XLA Ops:
  0.6 1.1 %work.7.refs_5_ = bf16[1056,128]{1,0:T(8,128)(2,1)S(1)} custom-call(bf16[16,1024,128]{2,1,0:T(8,128)(2,1)} %bitcast.3, bf16[16,2048]{1,0:T(8,128)(2,1)} %refs_1_.7, s32[8,16]{1,0:T(8,128)} %bitcast.8, s32[256,128]{1,0:T(8,128)} %refs_3_.7, s32[128,128]{1,0:T(8,128)} %refs_4_.7), custom_call_target="tpu_custom_call" | custom-call | flops 1 | bytes 1 | tf_op jit(solution)/shard_map/work/pallas_call | solution.py:221
  1.7 0.5 %collective-permute-start.1 = (bf16[1056,128]{1,0:T(8,128)(2,1)S(1)}, bf16[1056,128]{1,0:T(8,128)(2,1)S(1)}, u32[]{:S(2)}, u32[]{:S(2)}) collective-permute-start(bf16[1056,128]{1,0:T(8,128)(2,1)S(1)} %work.7.refs_5_), channel_id=1, source_target_pairs={{0,1},{1,0},{2,3},{3,2},{4,5},{5,4},{6,7},{7,6},{8,9},{9,8},{10,11... | collective-permute-start | bytes 811016 | tf_op jit(solution)/shard_map/ppermute | solution.py:20
  2.3 1.3 %work.8 = (bf16[1056,128]{1,0:T(8,128)(2,1)S(1)}, bf16[2112,128]{1,0:T(8,128)(2,1)S(1)}) custom-call(bf16[16,1024,128]{2,1,0:T(8,128)(2,1)} %bitcast.4, bf16[16,2048]{1,0:T(8,128)(2,1)} %refs_1_.7, s32[8,16]{1,0:T(8,128)} %bitcast.9, s32[256,128]{1,0:T(8,128)} %refs_3_.7, s32[128,128]{1,0:T(8,128)} %refs_4_.7, bf16[1056,128]{1,0:T(8,128)(2,1)S(1)} %work.7.refs_5_), custom_call_target="tpu_custom_call" | custom-call | flops 1 | bytes 1 | tf_op jit(solution)/shard_map/work/pallas_call | solution.py:221
  3.6 0.1 collective-permute-start
  3.7 0.0 collective-permute-done.1.refs_1_
  3.7 0.9 %work.9.refs_7_ = bf16[1,1040,128]{2,1,0:T(8,128)(2,1)S(1)} custom-call(bf16[2112,128]{1,0:T(8,128)(2,1)S(1)} %get-tuple-element.24.refs_0_.refs_5_, bf16[1056,128]{1,0:T(8,128)(2,1)S(1)} %collective-permute-done.1.refs_1_), custom_call_target="tpu_custom_call" | custom-call | flops 1 | bytes 1 | tf_op jit(solution)/shard_map/work/pallas_call | solution.py:221
  4.6 3.0 %collective-permute-start.5 = (bf16[1,1040,128]{2,1,0:T(8,128)(2,1)S(1)}, bf16[1,1040,128]{2,1,0:T(8,128)(2,1)S(1)}, u32[]{:S(2)}, u32[]{:S(2)}) collective-permute-start(bf16[1,1040,128]{2,1,0:T(8,128)(2,1)S(1)} %work.9.refs_7_), channel_id=1, source_target_pairs={{0,4},{4,0},{8,12},{12,8},{16,20},{20,16},{24,28},{28,24},{1,5},{5... | collective-permute-start | bytes 798728 | tf_op jit(solution)/shard_map/ppermute | solution.py:20
  7.6 0.0 collective-permute-done.refs_6_
  7.7 2.1 %work.10 = (bf16[1,1040,128]{2,1,0:T(8,128)(2,1)S(1)}, bf16[64,128]{1,0:T(8,128)(2,1)S(1)}, bf16[1024,128]{1,0:T(8,128)(2,1)S(1)}, bf16[1024,128]{1,0:T(8,128)(2,1)S(1)}, bf16[2112,128]{1,0:T(8,128)(2,1)S(1)}) custom-call(bf16[16,1024,128]{2,1,0:T(8,128)(2,1)} %bitcast.5, bf16[16,2048]{1,0:T(8,128)(2,1)} %refs_1_.7, s32[8,16]{1,0:T(8,128)} %bitcast.10, ...), custom_call_target="tpu_custom_call" | custom-call | flops 1 | bytes 1 | tf_op jit(solution)/shard_map/work/pallas_call | solution.py:221
  9.8 0.1 collective-permute-start.4
  9.9 0.5 %collective-permute-start.3 = (bf16[64,128]{1,0:T(8,128)(2,1)S(1)}, bf16[64,128]{1,0:T(8,128)(2,1)S(1)}, u32[]{:S(2)}, u32[]{:S(2)}) collective-permute-start(bf16[64,128]{1,0:T(8,128)(2,1)S(1)} %get-tuple-element.28), channel_id=1, source_target_pairs={{0,1},{1,0},{2,3},{3,2},{4,5},{5,4},{6,7},{7,6},{8,9},{9,8},{10,11... | collective-permute-start | bytes 49160 | tf_op jit(solution)/shard_map/ppermute | solution.py:20
  10.4 0.2 collective-permute-start.6
  10.6 0.1 collective-permute-start.2
  10.6 0.8 %collective-permute-done.3.refs_7_.refs_2_ = bf16[64,128]{1,0:T(8,128)(2,1)S(1)} collective-permute-done((bf16[64,128]{1,0:T(8,128)(2,1)S(1)}, bf16[64,128]{1,0:T(8,128)(2,1)S(1)}, u32[]{:S(2)}, u32[]{:S(2)}) %collective-permute-start.3) | collective-permute-done | bytes 16416 | tf_op jit(solution)/shard_map/ppermute | solution.py:20
  11.4 0.0 collective-permute-done.4.refs_6_
  11.4 3.4 %collective-permute-done.5.refs_9_.arrived = bf16[1,1040,128]{2,1,0:T(8,128)(2,1)S(1)} collective-permute-done((bf16[1,1040,128]{2,1,0:T(8,128)(2,1)S(1)}, bf16[1,1040,128]{2,1,0:T(8,128)(2,1)S(1)}, u32[]{:S(2)}, u32[]{:S(2)}) %collective-permute-start.5) | collective-permute-done | bytes 266272 | tf_op jit(solution)/shard_map/ppermute | solution.py:20
  14.8 2.6 %work.11 = (bf16[1,1040,128]{2,1,0:T(8,128)(2,1)S(1)}, bf16[128,128]{1,0:T(8,128)(2,1)S(1)}, bf16[1024,128]{1,0:T(8,128)(2,1)S(1)}, bf16[1024,128]{1,0:T(8,128)(...) custom-call(bf16[16,1024,128]{2,1,0:T(8,128)(2,1)} %bitcast.6, ...), custom_call_target="tpu_custom_call" | custom-call | flops 1 | bytes 1 | tf_op jit(solution)/shard_map/work/pallas_call | solution.py:221
  17.4 0.1 collective-permute-start.10
  17.5 0.5 %collective-permute-start.9 = (bf16[128,128]{1,0:T(8,128)(2,1)S(1)}, bf16[128,128]{1,0:T(8,128)(2,1)S(1)}, u32[]{:S(2)}, u32[]{:S(2)}) collective-permute-start(bf16[128,128]{1,0:T(8,128)(2,1)S(1)} %get-tuple-element.34), channel_id=1, source_target_pairs={{0,1},{1,0},{2,3},{3,2},{4,5},{5,4},{6,7},{7,6},{8,9},{9,8},{10,11... | collective-permute-start | bytes 98312 | tf_op jit(solution)/shard_map/ppermute | solution.py:20
  18.0 2.1 %collective-permute-start.13 = (bf16[1,1040,128]{2,1,0:T(8,128)(2,1)S(1)}, bf16[1,1040,128]{2,1,0:T(8,128)(2,1)S(1)}, u32[]{:S(2)}, u32[]{:S(2)}) collective-permute-start(bf16[1,1040,128]{2,1,0:T(8,128)(2,1)S(1)} %get-tuple-element.31.refs_3_), channel_id=1, source_target_pairs={{0,4},{4,0},{8,12},{12,8},{16,20},{20,16},{24,28},{28,24},{1,5},{5... | collective-permute-start | bytes 798728 | tf_op jit(solution)/shard_map/ppermute | solution.py:20
  20.0 0.0 collective-permute-done.2.refs_1_
  20.1 0.0 collective-permute-done.6.refs_4_.arrived
  20.1 0.9 %work.12.refs_6_ = bf16[1,1040,128]{2,1,0:T(8,128)(2,1)S(1)} custom-call(bf16[2112,128]{1,0:T(8,128)(2,1)S(1)} %get-tuple-element.26.refs_5_.refs_0_, bf16[1024,128]{1,0:T(8,128)(2,1)S(1)} %collective-permute-done.2.refs_1_, bf16[64,128]{1,0:T(8,128)(2,1)S(1)} %collective-permute-done.3.refs_7_.refs_2_, bf16[1,1040,128]{2,1,0:T(8,128)(2,1)S(1)} %get-tuple-element.31.refs_3_, ...), custom_call_target="tpu_custom_call" | custom-call | flops 1 | bytes 1 | tf_op jit(solution)/shard_map/work/pallas_call | solution.py:221
  21.0 1.7 %collective-permute-start.7 = (bf16[1,1040,128]{2,1,0:T(8,128)(2,1)S(1)}, bf16[1,1040,128]{2,1,0:T(8,128)(2,1)S(1)}, u32[]{:S(2)}, u32[]{:S(2)}) collective-permute-start(bf16[1,1040,128]{2,1,0:T(8,128)(2,1)S(1)} %work.12.refs_6_), channel_id=1, source_target_pairs={{0,4},{4,0},{8,12},{12,8},{16,20},{20,16},{24,28},{28,24},{1,5},{5... | collective-permute-start | bytes 798728 | tf_op jit(solution)/shard_map/ppermute | solution.py:20
  22.7 0.0 collective-permute-start.11
  22.7 0.0 collective-permute-done.9.refs_2_
  22.7 0.5 %collective-permute-start.12 = (bf16[1024,128]{1,0:T(8,128)(2,1)S(1)}, bf16[1024,128]{1,0:T(8,128)(2,1)S(1)}, u32[]{:S(2)}, u32[]{:S(2)}) collective-permute-start(bf16[1024,128]{1,0:T(8,128)(2,1)S(1)} %get-tuple-element.37), channel_id=1, source_target_pairs={{0,1},{1,0},{2,3},{3,2},{4,5},{5,4},{6,7},{7,6},{8,9},{9,8},{10,11... | collective-permute-start | bytes 786440 | tf_op jit(solution)/shard_map/ppermute | solution.py:20
  23.2 0.0 collective-permute-done.10.refs_3_
  23.2 0.1 collective-permute-start.8
  23.3 0.9 %collective-permute-done.11.refs_4_ = bf16[1024,128]{1,0:T(8,128)(2,1)S(1)} collective-permute-done((bf16[1024,128]{1,0:T(8,128)(2,1)S(1)}, bf16[1024,128]{1,0:T(8,128)(2,1)S(1)}, u32[]{:S(2)}, u32[]{:S(2)}) %collective-permute-start.11) | collective-permute-done | bytes 262176 | tf_op jit(solution)/shard_map/ppermute | solution.py:20
  24.2 0.4 %collective-permute-done.12.refs_5_ = bf16[1024,128]{1,0:T(8,128)(2,1)S(1)} collective-permute-done((bf16[1024,128]{1,0:T(8,128)(2,1)S(1)}, bf16[1024,128]{1,0:T(8,128)(2,1)S(1)}, u32[]{:S(2)}, u32[]{:S(2)}) %collective-permute-start.12) | collective-permute-done | bytes 262176 | tf_op jit(solution)/shard_map/ppermute | solution.py:20
  24.6 0.4 %collective-permute-done.8.refs_1_ = bf16[1024,128]{1,0:T(8,128)(2,1)S(1)} collective-permute-done((bf16[1024,128]{1,0:T(8,128)(2,1)S(1)}, bf16[1024,128]{1,0:T(8,128)(2,1)S(1)}, u32[]{:S(2)}, u32[]{:S(2)}) %collective-permute-start.8) | collective-permute-done | bytes 262176 | tf_op jit(solution)/shard_map/ppermute | solution.py:20
  25.0 3.1 %work.13.kept = bf16[4,1040,128]{2,1,0:T(8,128)(2,1)S(1)} custom-call(bf16[4224,128]{1,0:T(8,128)(2,1)S(1)} %get-tuple-element.32.refs_0_, bf16[1024,128]{1,0:T(8,128)(2,1)S(1)} %collective-permute-done.8.refs_1_, bf16[128,128]{1,0:T(8,128)(2,1)S(1)} %collective-permute-done.9.refs_2_, bf16[1024,128]{1,0:T(8,128)(2,1)S(1)} %collective-permute-done.10.refs_3_, ...), custom_call_target="tpu_custom_call" | custom-call | flops 1 | bytes 1 | tf_op jit(solution)/shard_map/work/pallas_call | solution.py:221
  28.0 0.8 %add.4 = (bf16[4,1024,128]{2,1,0:T(8,128)(2,1)}, bf16[16,512]{1,0:T(8,128)(2,1)}) custom-call(bf16[1,1040,128]{2,1,0:T(8,128)(2,1)S(1)} %collective-permute-done.5.refs_9_.arrived, bf16[4,1040,128]{2,1,0:T(8,128)(2,1)S(1)} %work.13.kept), custom_call_target="tpu_custom_call" | custom-call | flops 1 | bytes 1 | tf_op jit(solution)/shard_map/add/pallas_call | solution.py:277
  28.8 0.8 %add.5 = (bf16[4,1024,128]{2,1,0:T(8,128)(2,1)}, bf16[16,512]{1,0:T(8,128)(2,1)}) custom-call(bf16[1,1040,128]{2,1,0:T(8,128)(2,1)S(1)} %collective-permute-done.6.refs_4_.arrived, bf16[4,1040,128]{2,1,0:T(8,128)(2,1)S(1)} %work.13.kept, bf16[4,1024,128]{2,1,0:T(8,128)(2,1)} %get-tuple-element.38.rest_0_, ...), custom_call_target="tpu_custom_call", output_to_operand_aliasing={{0}: (2, {}), {1}: (3, {})} | custom-call | flops 1 | bytes 1 | tf_op jit(solution)/shard_map/add/pallas_call | solution.py:277
  29.6 0.0 collective-permute-done.13.arrived
  29.6 0.8 %add.6 = (bf16[4,1024,128]{2,1,0:T(8,128)(2,1)}, bf16[16,512]{1,0:T(8,128)(2,1)}) custom-call(bf16[1,1040,128]{2,1,0:T(8,128)(2,1)S(1)} %collective-permute-done.13.arrived, bf16[4,1040,128]{2,1,0:T(8,128)(2,1)S(1)} %work.13.kept, bf16[4,1024,128]{2,1,0:T(8,128)(2,1)} %get-tuple-element.40.rest_0_, ...), custom_call_target="tpu_custom_call", output_to_operand_aliasing={{0}: (2, {}), {1}: (3, {})} | custom-call | flops 1 | bytes 1 | tf_op jit(solution)/shard_map/add/pallas_call | solution.py:277
  30.4 2.0 %collective-permute-done.7.arrived = bf16[1,1040,128]{2,1,0:T(8,128)(2,1)S(1)} collective-permute-done((bf16[1,1040,128]{2,1,0:T(8,128)(2,1)S(1)}, bf16[1,1040,128]{2,1,0:T(8,128)(2,1)S(1)}, u32[]{:S(2)}, u32[]{:S(2)}) %collective-permute-start.7) | collective-permute-done | bytes 266272 | tf_op jit(solution)/shard_map/ppermute | solution.py:20
  32.4 0.8 %add.7 = (bf16[4,1024,128]{2,1,0:T(8,128)(2,1)}, bf16[16,512]{1,0:T(8,128)(2,1)}) custom-call(bf16[1,1040,128]{2,1,0:T(8,128)(2,1)S(1)} %collective-permute-done.7.arrived, bf16[4,1040,128]{2,1,0:T(8,128)(2,1)S(1)} %work.13.kept, bf16[4,1024,128]{2,1,0:T(8,128)(2,1)} %get-tuple-element.42.rest_0_, ...), custom_call_target="tpu_custom_call", output_to_operand_aliasing={{0}: (2, {}), {1}: (3, {})} | custom-call | flops 1 | bytes 1 | tf_op jit(solution)/shard_map/add/pallas_call | solution.py:277
Async XLA Ops:
  1.7 2.0 %collective-permute-start.1 = (bf16[1056,128]{1,0:T(8,128)(2,1)S(1)}, bf16[1056,128]{1,0:T(8,128)(2,1)S(1)}, u32[]{:S(2)}, u32[]{:S(2)}) collective-permute-start(bf16[1056,128]{1,0:T(8,128)(2,1)S(1)} %work.7.refs_5_), channel_id=1, source_target_pairs={{0,1},{1,0},{2,3},{3,2},{4,5},{5,4},{6,7},{7,6},{8,9},{9,8},{10,11... | collective-permute-start | bytes 811016 | tf_op jit(solution)/shard_map/ppermute | solution.py:20
  3.6 4.1 %collective-permute-start = (bf16[1056,128]{1,0:T(8,128)(2,1)S(1)}, bf16[1056,128]{1,0:T(8,128)(2,1)S(1)}, u32[]{:S(2)}, u32[]{:S(2)}) collective-permute-start(bf16[1056,128]{1,0:T(8,128)(2,1)S(1)} %get-tuple-element.25), channel_id=1, source_target_pairs={{0,1},{1,0},{2,3},{3,2},{4,5},{5,4},{6,7},{7,6},{8,9},{9,8},{10,11... | collective-permute-start | bytes 811016 | tf_op jit(solution)/shard_map/ppermute | solution.py:20
  4.6 10.2 %collective-permute-start.5 = (bf16[1,1040,128]{2,1,0:T(8,128)(2,1)S(1)}, bf16[1,1040,128]{2,1,0:T(8,128)(2,1)S(1)}, u32[]{:S(2)}, u32[]{:S(2)}) collective-permute-start(bf16[1,1040,128]{2,1,0:T(8,128)(2,1)S(1)} %work.9.refs_7_), channel_id=1, source_target_pairs={{0,4},{4,0},{8,12},{12,8},{16,20},{20,16},{24,28},{28,24},{1,5},{5... | collective-permute-start | bytes 798728 | tf_op jit(solution)/shard_map/ppermute | solution.py:20
  9.8 1.6 %collective-permute-start.4 = (bf16[1024,128]{1,0:T(8,128)(2,1)S(1)}, bf16[1024,128]{1,0:T(8,128)(2,1)S(1)}, u32[]{:S(2)}, u32[]{:S(2)}) collective-permute-start(bf16[1024,128]{1,0:T(8,128)(2,1)S(1)} %get-tuple-element.29), channel_id=1, source_target_pairs={{0,1},{1,0},{2,3},{3,2},{4,5},{5,4},{6,7},{7,6},{8,9},{9,8},{10,11... | collective-permute-start | bytes 786440 | tf_op jit(solution)/shard_map/ppermute | solution.py:20
  9.9 1.5 %collective-permute-start.3 = (bf16[64,128]{1,0:T(8,128)(2,1)S(1)}, bf16[64,128]{1,0:T(8,128)(2,1)S(1)}, u32[]{:S(2)}, u32[]{:S(2)}) collective-permute-start(bf16[64,128]{1,0:T(8,128)(2,1)S(1)} %get-tuple-element.28), channel_id=1, source_target_pairs={{0,1},{1,0},{2,3},{3,2},{4,5},{5,4},{6,7},{7,6},{8,9},{9,8},{10,11... | collective-permute-start | bytes 49160 | tf_op jit(solution)/shard_map/ppermute | solution.py:20
  10.4 9.7 %collective-permute-start.6 = (bf16[1,1040,128]{2,1,0:T(8,128)(2,1)S(1)}, bf16[1,1040,128]{2,1,0:T(8,128)(2,1)S(1)}, u32[]{:S(2)}, u32[]{:S(2)}) collective-permute-start(bf16[1,1040,128]{2,1,0:T(8,128)(2,1)S(1)} %get-tuple-element.30.refs_8_), channel_id=1, source_target_pairs={{0,4},{4,0},{8,12},{12,8},{16,20},{20,16},{24,28},{28,24},{1,5},{5... | collective-permute-start | bytes 798728 | tf_op jit(solution)/shard_map/ppermute | solution.py:20
  10.6 9.5 %collective-permute-start.2 = (bf16[1024,128]{1,0:T(8,128)(2,1)S(1)}, bf16[1024,128]{1,0:T(8,128)(2,1)S(1)}, u32[]{:S(2)}, u32[]{:S(2)}) collective-permute-start(bf16[1024,128]{1,0:T(8,128)(2,1)S(1)} %get-tuple-element.27), channel_id=1, source_target_pairs={{0,1},{1,0},{2,3},{3,2},{4,5},{5,4},{6,7},{7,6},{8,9},{9,8},{10,11... | collective-permute-start | bytes 786440 | tf_op jit(solution)/shard_map/ppermute | solution.py:20
  17.4 5.8 %collective-permute-start.10 = (bf16[1024,128]{1,0:T(8,128)(2,1)S(1)}, bf16[1024,128]{1,0:T(8,128)(2,1)S(1)}, u32[]{:S(2)}, u32[]{:S(2)}) collective-permute-start(bf16[1024,128]{1,0:T(8,128)(2,1)S(1)} %get-tuple-element.35), channel_id=1, source_target_pairs={{0,1},{1,0},{2,3},{3,2},{4,5},{5,4},{6,7},{7,6},{8,9},{9,8},{10,11... | collective-permute-start | bytes 786440 | tf_op jit(solution)/shard_map/ppermute | solution.py:20
  17.5 5.2 %collective-permute-start.9 = (bf16[128,128]{1,0:T(8,128)(2,1)S(1)}, bf16[128,128]{1,0:T(8,128)(2,1)S(1)}, u32[]{:S(2)}, u32[]{:S(2)}) collective-permute-start(bf16[128,128]{1,0:T(8,128)(2,1)S(1)} %get-tuple-element.34), channel_id=1, source_target_pairs={{0,1},{1,0},{2,3},{3,2},{4,5},{5,4},{6,7},{7,6},{8,9},{9,8},{10,11... | collective-permute-start | bytes 98312 | tf_op jit(solution)/shard_map/ppermute | solution.py:20
  18.0 11.6 %collective-permute-start.13 = (bf16[1,1040,128]{2,1,0:T(8,128)(2,1)S(1)}, bf16[1,1040,128]{2,1,0:T(8,128)(2,1)S(1)}, u32[]{:S(2)}, u32[]{:S(2)}) collective-permute-start(bf16[1,1040,128]{2,1,0:T(8,128)(2,1)S(1)} %get-tuple-element.31.refs_3_), channel_id=1, source_target_pairs={{0,4},{4,0},{8,12},{12,8},{16,20},{20,16},{24,28},{28,24},{1,5},{5... | collective-permute-start | bytes 798728 | tf_op jit(solution)/shard_map/ppermute | solution.py:20
  21.0 11.4 %collective-permute-start.7 = (bf16[1,1040,128]{2,1,0:T(8,128)(2,1)S(1)}, bf16[1,1040,128]{2,1,0:T(8,128)(2,1)S(1)}, u32[]{:S(2)}, u32[]{:S(2)}) collective-permute-start(bf16[1,1040,128]{2,1,0:T(8,128)(2,1)S(1)} %work.12.refs_6_), channel_id=1, source_target_pairs={{0,4},{4,0},{8,12},{12,8},{16,20},{20,16},{24,28},{28,24},{1,5},{5... | collective-permute-start | bytes 798728 | tf_op jit(solution)/shard_map/ppermute | solution.py:20
  22.7 1.5 %collective-permute-start.11 = (bf16[1024,128]{1,0:T(8,128)(2,1)S(1)}, bf16[1024,128]{1,0:T(8,128)(2,1)S(1)}, u32[]{:S(2)}, u32[]{:S(2)}) collective-permute-start(bf16[1024,128]{1,0:T(8,128)(2,1)S(1)} %get-tuple-element.36), channel_id=1, source_target_pairs={{0,1},{1,0},{2,3},{3,2},{4,5},{5,4},{6,7},{7,6},{8,9},{9,8},{10,11... | collective-permute-start | bytes 786440 | tf_op jit(solution)/shard_map/ppermute | solution.py:20
  22.7 1.9 %collective-permute-start.12 = (bf16[1024,128]{1,0:T(8,128)(2,1)S(1)}, bf16[1024,128]{1,0:T(8,128)(2,1)S(1)}, u32[]{:S(2)}, u32[]{:S(2)}) collective-permute-start(bf16[1024,128]{1,0:T(8,128)(2,1)S(1)} %get-tuple-element.37), channel_id=1, source_target_pairs={{0,1},{1,0},{2,3},{3,2},{4,5},{5,4},{6,7},{7,6},{8,9},{9,8},{10,11... | collective-permute-start | bytes 786440 | tf_op jit(solution)/shard_map/ppermute | solution.py:20
  23.2 1.8 %collective-permute-start.8 = (bf16[1024,128]{1,0:T(8,128)(2,1)S(1)}, bf16[1024,128]{1,0:T(8,128)(2,1)S(1)}, u32[]{:S(2)}, u32[]{:S(2)}) collective-permute-start(bf16[1024,128]{1,0:T(8,128)(2,1)S(1)} %get-tuple-element.33), channel_id=1, source_target_pairs={{0,1},{1,0},{2,3},{3,2},{4,5},{5,4},{6,7},{7,6},{8,9},{9,8},{10,11... | collective-permute-start | bytes 786440 | tf_op jit(solution)/shard_map/ppermute | solution.py:20

commit v3 on v2

--- a/solution.py
+++ b/solution.py
@@ -8,6 +8,7 @@
 from jax.sharding import PartitionSpec as P
 
 HALF = 16
+PARTS = 4
 LIMIT = 48 * 2**20
 LIGHT = pl.CostEstimate(flops=1, bytes_accessed=1, transcendentals=0)
 VMEM = pl.BlockSpec(memory_space=pltpu.VMEM)
@@ -73,40 +74,36 @@
 
 def merge_tile(slots, own, other, own_side, other_side, out):
     width = own.shape[-1]
-    sides = lax.broadcasted_iota(jnp.int32, (width, width), 1).astype(jnp.float32)
     along = lax.broadcasted_iota(jnp.int32, (width, width), 0).astype(jnp.float32)
-    across = jnp.concatenate([own_side[:HALF], other_side[:HALF]], 0).astype(jnp.float32)
-    down = across.T
-
-    def dot(a, b):
-        return jnp.dot(a, b, preferred_element_type=jnp.float32)
+    own_maps, other_maps = (x[:HALF].astype(jnp.float32) for x in (own_side, other_side))
+
+    def hot(maps, row):
+        return (maps[row : row + 1, :] == along).astype(jnp.bfloat16)
 
     def columns(row):
-        return jnp.concatenate(
-            [
-                (down[:, place : place + 1] == sides).astype(jnp.bfloat16)
-                for place in (row, HALF + row)
-            ],
-            0,
+        return jnp.concatenate([hot(own_maps, row), hot(other_maps, row)], 1)
+
+    def across(value, row):
+        return lax.dot_general(
+            value, columns(row), (((1,), (1,)), ((), ())), preferred_element_type=jnp.float32
         )
 
-    own_rows = (across[slots : slots + 1, :] == along).astype(jnp.bfloat16)
-    other_rows = (across[HALF + slots : HALF + slots + 1, :] == along).astype(jnp.bfloat16)
+    def moved(rows_hot, tile, pair):
+        blocks = [tile[slot * width : (slot + 1) * width, :] for slot in (2 * pair, 2 * pair + 1)]
+        value = jnp.dot(
+            rows_hot, jnp.concatenate(blocks, 1), preferred_element_type=jnp.float32
+        ).astype(jnp.bfloat16)
+        return [value[:, :width], value[:, width:]]
+
+    own_rows, other_rows = hot(own_maps, slots), hot(other_maps, slots)
+    rows_done = []
     for pair in range(slots // 2):
-        both = [2 * pair, 2 * pair + 1]
-
-        def moved(hot, ref):
-            blocks = [ref[slot * width : (slot + 1) * width, :] for slot in both]
-            return dot(hot, jnp.concatenate(blocks, 1)).astype(jnp.bfloat16)
-
-        own_two = moved(own_rows, own)
-        other_two = moved(other_rows, other)
-        for half, slot in enumerate(both):
-            part = slice(half * width, (half + 1) * width)
-            lhs = jnp.concatenate([own_two[:, part], other_two[:, part]], 1)
-            out[slot * width : (slot + 1) * width, :] = dot(lhs, columns(slot)).astype(out.dtype)
+        halves = moved(own_rows, own, pair), moved(other_rows, other, pair)
+        rows_done += [jnp.concatenate(both, 1) for both in zip(*halves)]
+    for slot, value in enumerate(rows_done):
+        out[slot * width : (slot + 1) * width, :] = across(value, slot).astype(out.dtype)
     feats = jnp.concatenate([own_side[HALF:], other_side[HALF:]], 1)
-    out[slots * width :, :] = dot(feats, columns(slots)).astype(out.dtype)
+    out[slots * width :, :] = across(feats, slots).astype(out.dtype)
 
 
 def work_kernel(plan, refs):
@@ -245,22 +242,26 @@
     width = arrived.shape[-1]
     rows = slots * width
     tiles = arrived.shape[0]
-    copies = []
+    part = rows // PARTS
+
+    def total(i, here):
+        value = kept[first + i, here].astype(jnp.float32) + arrived[i, here].astype(jnp.float32)
+        return value.astype(jnp.bfloat16)
+
     for i in range(tiles):
-        total = kept[first + i].astype(jnp.float32) + arrived[i].astype(jnp.float32)
-        total = total.astype(jnp.bfloat16)
-        tile_sum[i] = total[:rows]
-        feat_sum[:, i * width : (i + 1) * width] = total[rows:]
-        copies.append(
-            pltpu.make_async_copy(tile_sum.at[i], tiles_out.at[first + i], sems.at[i])
-        )
-        copies[-1].start()
-    copies.append(
-        pltpu.make_async_copy(
-            feat_sum, feats_out.at[:, pl.ds(first * width, tiles * width)], sems.at[tiles]
-        )
-    )
-    copies[-1].start()
+        feat_sum[:, i * width : (i + 1) * width] = total(i, slice(rows, None))
+    copies = [
+        start(feat_sum, feats_out.at[:, pl.ds(first * width, tiles * width)], sems.at[tiles * PARTS])
+    ]
+    for i in range(tiles):
+        for at in range(PARTS):
+            tile_sum[i, at * part : (at + 1) * part] = total(i, slice(at * part, (at + 1) * part))
+            here = pl.ds(at * part, part)
+            copies.append(
+                start(
+                    tile_sum.at[i, here], tiles_out.at[first + i, here], sems.at[i * PARTS + at]
+                )
+            )
     for copy in copies:
         copy.wait()
 
@@ -282,7 +283,7 @@
         scratch_shapes=[
             pltpu.VMEM((tiles, rows, width), jnp.bfloat16),
             pltpu.VMEM((feat_count, tiles * width), jnp.bfloat16),
-            pltpu.SemaphoreType.DMA((tiles + 1,)),
+            pltpu.SemaphoreType.DMA((tiles * PARTS + 1,)),
         ],
         input_output_aliases={2: 0, 3: 1} if before else {},
         compiler_params=pltpu.CompilerParams(vmem_limit_bytes=LIMIT),
@@ -303,20 +304,19 @@
     keep = [(1, piece) for piece in range(quarter)]
     first = work.run(leaving=send[:1])
     work.run(keys=send[:2], leaving=send[1:2], after=[first])
-    more = {1: send[2:], 2: keep}
-    arrived = []
-    after = []
-    for piece in range(quarter):
-        new = more.get(piece, [])
-        parcel = work.run(
-            merges=send[piece : piece + 1], keys=new, leaving=new, apart=bool(new), after=after
-        )
-        arrived.append(swapped(parcel, "blk"))
-        after = [parcel] + arrived[piece - 1 : piece] * (piece >= 1)
-    kept = work.run(merges=keep, after=[parcel])
+    lead = work.run(merges=send[:1])
+    arrived = [swapped(lead, "blk")]
+    parcel = work.run(merges=send[1:2], keys=send[2:], leaving=send[2:], apart=True, after=[lead])
+    arrived.append(swapped(parcel, "blk"))
+    parcel = work.run(merges=send[2:], after=[parcel, arrived[0]])
+    arrived.append(swapped(parcel, "blk"))
+    last = work.run(keys=keep, leaving=keep, apart=True, after=[parcel, arrived[1]])
+    kept = work.run(merges=keep, after=[last])
     out = None
-    for piece, part in enumerate(arrived):
+    piece = 0
+    for part in arrived:
         out = added(piece, slots, feat_count, part, kept, out)
+        piece += part.shape[0]
     return out[0].reshape(quarter, slots, width, width), out[1]
 
 

time: 33.4 us -> 32 us (0.958)
  Pallas kernels: 15.2 us -> 10.8 us
  waiting for transfers between devices: 7.88 us -> 11.9 us
  starting transfers between devices: 9.38 us -> 8.34 us
    ppermute x14 -> x13, waiting for transfers between devices: 7.88 us -> 11.9 us  [swapped(): return lax.ppermute(value, axis, pairs)]
    pallas_call x7, Pallas kernels: 12 us -> 8.36 us  [run(): pl.pallas_call(lambda *refs: work_kernel(plan, refs), out_shape=shapes, i...]
    ppermute x14 -> x13, starting transfers between devices: 9.38 us -> 8.34 us  [swapped(): return lax.ppermute(value, axis, pairs)]
    pallas_call x4 -> x3, Pallas kernels: 3.15 us -> 2.4 us  [added(): pl.pallas_call(functools.partial(add_kernel, first, slots), out_shape=sha...]
  transfers between devices with their start and end apart: 14 -> 13, of which waited for: 6 -> 9; matrix products, arithmetic and copies ran while one was open for 0% -> 0% of each run, Pallas kernels for 40% -> 28%
where the time goes in v3:
time: 32 us; the launch traced here: 31.7 us
  waiting for transfers between devices  11.9 us (37%)
  Pallas kernels  10.8 us (34%)
  starting transfers between devices  8.34 us (26%)
  between operations  0.72 us (2%)
    ppermute x13, waiting for transfers between devices, swapped(): return lax.ppermute(value, axis, pairs)  11.9 us
    pallas_call x7, Pallas kernels, run(): pl.pallas_call(lambda *refs: work_kernel(plan, refs), out_shape=shapes, i...  8.36 us
    ppermute x13, starting transfers between devices, swapped(): return lax.ppermute(value, axis, pairs)  8.34 us
    pallas_call x3, Pallas kernels, added(): pl.pallas_call(functools.partial(add_kernel, first, slots), out_shape=sha...  2.4 us
  transfers between devices with their start and end apart: 13, of which 9 were waited for; matrix products, arithmetic and copies ran while one was open for 0% of the time, Pallas kernels for 28%

profile of v3, /device:TPU:0, one launch (start us, length us, event | category | flops | bytes accessed | tf_op | source)
XLA Modules:
  0.0 31.7 jit_solution(980882404016865694)
XLA Ops:
  0.6 1.1 %work.7.refs_5_ = bf16[1056,128]{1,0:T(8,128)(2,1)S(1)} custom-call(bf16[16,1024,128]{2,1,0:T(8,128)(2,1)} %bitcast.3, bf16[16,2048]{1,0:T(8,128)(2,1)} %refs_1_.7, s32[8,16]{1,0:T(8,128)} %bitcast.8, s32[256,128]{1,0:T(8,128)} %refs_3_.7, s32[128,128]{1,0:T(8,128)} %refs_4_.7), custom_call_target="tpu_custom_call" | custom-call | flops 1 | bytes 1 | tf_op jit(solution)/shard_map/work/pallas_call | solution.py:218
  1.7 0.5 %collective-permute-start.1 = (bf16[1056,128]{1,0:T(8,128)(2,1)S(1)}, bf16[1056,128]{1,0:T(8,128)(2,1)S(1)}, u32[]{:S(2)}, u32[]{:S(2)}) collective-permute-start(bf16[1056,128]{1,0:T(8,128)(2,1)S(1)} %work.7.refs_5_), channel_id=1, source_target_pairs={{0,1},{1,0},{2,3},{3,2},{4,5},{5,4},{6,7},{7,6},{8,9},{9,8},{10,11... | collective-permute-start | bytes 811016 | tf_op jit(solution)/shard_map/ppermute | solution.py:21
  2.3 1.3 %work.8 = (bf16[1056,128]{1,0:T(8,128)(2,1)S(1)}, bf16[2112,128]{1,0:T(8,128)(2,1)S(1)}) custom-call(bf16[16,1024,128]{2,1,0:T(8,128)(2,1)} %bitcast.4, bf16[16,2048]{1,0:T(8,128)(2,1)} %refs_1_.7, s32[8,16]{1,0:T(8,128)} %bitcast.9, s32[256,128]{1,0:T(8,128)} %refs_3_.7, s32[128,128]{1,0:T(8,128)} %refs_4_.7, bf16[1056,128]{1,0:T(8,128)(2,1)S(1)} %work.7.refs_5_), custom_call_target="tpu_custom_call" | custom-call | flops 1 | bytes 1 | tf_op jit(solution)/shard_map/work/pallas_call | solution.py:218
  3.6 0.1 collective-permute-start
  3.7 0.0 collective-permute-done.1.refs_1_
  3.7 0.4 %work.9.refs_7_ = bf16[1,1040,128]{2,1,0:T(8,128)(2,1)S(1)} custom-call(bf16[2112,128]{1,0:T(8,128)(2,1)S(1)} %get-tuple-element.21.refs_0_.refs_5_, bf16[1056,128]{1,0:T(8,128)(2,1)S(1)} %collective-permute-done.1.refs_1_), custom_call_target="tpu_custom_call" | custom-call | flops 1 | bytes 1 | tf_op jit(solution)/shard_map/work/pallas_call | solution.py:218
  4.2 3.0 %collective-permute-start.5 = (bf16[1,1040,128]{2,1,0:T(8,128)(2,1)S(1)}, bf16[1,1040,128]{2,1,0:T(8,128)(2,1)S(1)}, u32[]{:S(2)}, u32[]{:S(2)}) collective-permute-start(bf16[1,1040,128]{2,1,0:T(8,128)(2,1)S(1)} %work.9.refs_7_), channel_id=1, source_target_pairs={{0,4},{4,0},{8,12},{12,8},{16,20},{20,16},{24,28},{28,24},{1,5},{5... | collective-permute-start | bytes 798728 | tf_op jit(solution)/shard_map/ppermute | solution.py:21
  7.2 0.0 collective-permute-done.refs_6_
  7.2 1.7 %work.10 = (bf16[1,1040,128]{2,1,0:T(8,128)(2,1)S(1)}, bf16[64,128]{1,0:T(8,128)(2,1)S(1)}, bf16[1024,128]{1,0:T(8,128)(2,1)S(1)}, bf16[1024,128]{1,0:T(8,128)(2,1)S(1)}, bf16[2112,128]{1,0:T(8,128)(2,1)S(1)}) custom-call(bf16[16,1024,128]{2,1,0:T(8,128)(2,1)} %bitcast.5, bf16[16,2048]{1,0:T(8,128)(2,1)} %refs_1_.7, s32[8,16]{1,0:T(8,128)} %bitcast.10, ...), custom_call_target="tpu_custom_call" | custom-call | flops 1 | bytes 1 | tf_op jit(solution)/shard_map/work/pallas_call | solution.py:218
  8.8 0.1 collective-permute-start.2
  8.9 0.5 %collective-permute-start.4 = (bf16[1024,128]{1,0:T(8,128)(2,1)S(1)}, bf16[1024,128]{1,0:T(8,128)(2,1)S(1)}, u32[]{:S(2)}, u32[]{:S(2)}) collective-permute-start(bf16[1024,128]{1,0:T(8,128)(2,1)S(1)} %get-tuple-element.26), channel_id=1, source_target_pairs={{0,1},{1,0},{2,3},{3,2},{4,5},{5,4},{6,7},{7,6},{8,9},{9,8},{10,11... | collective-permute-start | bytes 786440 | tf_op jit(solution)/shard_map/ppermute | solution.py:21
  9.4 0.7 %collective-permute-start.7 = (bf16[1,1040,128]{2,1,0:T(8,128)(2,1)S(1)}, bf16[1,1040,128]{2,1,0:T(8,128)(2,1)S(1)}, u32[]{:S(2)}, u32[]{:S(2)}) collective-permute-start(bf16[1,1040,128]{2,1,0:T(8,128)(2,1)S(1)} %get-tuple-element.27.refs_4_), channel_id=1, source_target_pairs={{0,4},{4,0},{8,12},{12,8},{16,20},{20,16},{24,28},{28,24},{1,5},{5... | collective-permute-start | bytes 798728 | tf_op jit(solution)/shard_map/ppermute | solution.py:21
  10.1 0.1 collective-permute-start.3
  10.2 1.1 %collective-permute-done.3.refs_2_ = bf16[64,128]{1,0:T(8,128)(2,1)S(1)} collective-permute-done((bf16[64,128]{1,0:T(8,128)(2,1)S(1)}, bf16[64,128]{1,0:T(8,128)(2,1)S(1)}, u32[]{:S(2)}, u32[]{:S(2)}) %collective-permute-start.3) | collective-permute-done | bytes 16416 | tf_op jit(solution)/shard_map/ppermute | solution.py:21
  11.3 0.0 collective-permute-done.2.refs_1_
  11.3 0.0 collective-permute-done.4.refs_3_
  11.3 3.1 %collective-permute-done.5.refs_5_.arrived = bf16[1,1040,128]{2,1,0:T(8,128)(2,1)S(1)} collective-permute-done((bf16[1,1040,128]{2,1,0:T(8,128)(2,1)S(1)}, bf16[1,1040,128]{2,1,0:T(8,128)(2,1)S(1)}, u32[]{:S(2)}, u32[]{:S(2)}) %collective-permute-start.5) | collective-permute-done | bytes 266272 | tf_op jit(solution)/shard_map/ppermute | solution.py:21
  14.4 0.7 %work.11.refs_5_ = bf16[2,1040,128]{2,1,0:T(8,128)(2,1)S(1)} custom-call(bf16[2112,128]{1,0:T(8,128)(2,1)S(1)} %get-tuple-element.23.refs_0_, bf16[1024,128]{1,0:T(8,128)(2,1)S(1)} %collective-permute-done.2.refs_1_, bf16[64,128]{1,0:T(8,128)(2,1)S(1)} %collective-permute-done.3.refs_2_, bf16[1024,128]{1,0:T(8,128)(2,1)S(1)} %collective-permute-done.4.refs_3_, ...), custom_call_target="tpu_custom_call" | custom-call | flops 1 | bytes 1 | tf_op jit(solution)/shard_map/work/pallas_call | solution.py:218
  15.1 2.1 %collective-permute-start.6 = (bf16[2,1040,128]{2,1,0:T(8,128)(2,1)S(1)}, bf16[2,1040,128]{2,1,0:T(8,128)(2,1)S(1)}, u32[]{:S(2)}, u32[]{:S(2)}) collective-permute-start(bf16[2,1040,128]{2,1,0:T(8,128)(2,1)S(1)} %work.11.refs_5_), channel_id=1, source_target_pairs={{0,4},{4,0},{8,12},{12,8},{16,20},{20,16},{24,28},{28,24},{1,5},{5... | collective-permute-start | bytes 1597448 | tf_op jit(solution)/shard_map/ppermute | solution.py:21
  17.2 2.9 %collective-permute-done.7.refs_6_.arrived = bf16[1,1040,128]{2,1,0:T(8,128)(2,1)S(1)} collective-permute-done((bf16[1,1040,128]{2,1,0:T(8,128)(2,1)S(1)}, bf16[1,1040,128]{2,1,0:T(8,128)(2,1)S(1)}, u32[]{:S(2)}, u32[]{:S(2)}) %collective-permute-start.7) | collective-permute-done | bytes 266272 | tf_op jit(solution)/shard_map/ppermute | solution.py:21
  20.1 1.8 %work.12 = (bf16[128,128]{1,0:T(8,128)(2,1)S(1)}, bf16[1024,128]{1,0:T(8,128)(2,1)S(1)}, bf16[1024,128]{1,0:T(8,128)(2,1)S(1)}, bf16[1024,128]{1,0:T(8,128)(2,1)...) custom-call(bf16[16,1024,128]{2,1,0:T(8,128)(2,1)} %bitcast.6, bf16[16,2048]{1,0:T(8,128)(2,1)} %refs_1_.7, ...), custom_call_target="tpu_custom_call" | custom-call | flops 1 | bytes 1 | tf_op jit(solution)/shard_map/work/pallas_call | solution.py:218
  21.9 0.1 collective-permute-start.9
  22.0 0.5 %collective-permute-start.8 = (bf16[1024,128]{1,0:T(8,128)(2,1)S(1)}, bf16[1024,128]{1,0:T(8,128)(2,1)S(1)}, u32[]{:S(2)}, u32[]{:S(2)}) collective-permute-start(bf16[1024,128]{1,0:T(8,128)(2,1)S(1)} %get-tuple-element.29), channel_id=1, source_target_pairs={{0,1},{1,0},{2,3},{3,2},{4,5},{5,4},{6,7},{7,6},{8,9},{9,8},{10,11... | collective-permute-start | bytes 786440 | tf_op jit(solution)/shard_map/ppermute | solution.py:21
  22.5 0.1 collective-permute-start.10
  22.6 0.4 %collective-permute-start.11 = (bf16[1024,128]{1,0:T(8,128)(2,1)S(1)}, bf16[1024,128]{1,0:T(8,128)(2,1)S(1)}, u32[]{:S(2)}, u32[]{:S(2)}) collective-permute-start(bf16[1024,128]{1,0:T(8,128)(2,1)S(1)} %get-tuple-element.32), channel_id=1, source_target_pairs={{0,1},{1,0},{2,3},{3,2},{4,5},{5,4},{6,7},{7,6},{8,9},{9,8},{10,11... | collective-permute-start | bytes 786440 | tf_op jit(solution)/shard_map/ppermute | solution.py:21
  23.0 0.2 collective-permute-done.9.refs_2_
  23.2 0.2 collective-permute-start.12
  23.3 0.3 collective-permute-done.8.refs_1_
  23.6 0.4 %collective-permute-done.10.refs_3_ = bf16[1024,128]{1,0:T(8,128)(2,1)S(1)} collective-permute-done((bf16[1024,128]{1,0:T(8,128)(2,1)S(1)}, bf16[1024,128]{1,0:T(8,128)(2,1)S(1)}, u32[]{:S(2)}, u32[]{:S(2)}) %collective-permute-start.10) | collective-permute-done | bytes 262176 | tf_op jit(solution)/shard_map/ppermute | solution.py:21
  24.0 0.4 %collective-permute-done.11.refs_4_ = bf16[1024,128]{1,0:T(8,128)(2,1)S(1)} collective-permute-done((bf16[1024,128]{1,0:T(8,128)(2,1)S(1)}, bf16[1024,128]{1,0:T(8,128)(2,1)S(1)}, u32[]{:S(2)}, u32[]{:S(2)}) %collective-permute-start.11) | collective-permute-done | bytes 262176 | tf_op jit(solution)/shard_map/ppermute | solution.py:21
  24.4 0.4 %collective-permute-done.12.refs_5_ = bf16[1024,128]{1,0:T(8,128)(2,1)S(1)} collective-permute-done((bf16[1024,128]{1,0:T(8,128)(2,1)S(1)}, bf16[1024,128]{1,0:T(8,128)(2,1)S(1)}, u32[]{:S(2)}, u32[]{:S(2)}) %collective-permute-start.12) | collective-permute-done | bytes 262176 | tf_op jit(solution)/shard_map/ppermute | solution.py:21
  24.8 1.3 %work.13.kept = bf16[4,1040,128]{2,1,0:T(8,128)(2,1)S(1)} custom-call(bf16[4224,128]{1,0:T(8,128)(2,1)S(1)} %get-tuple-element.28.refs_0_, bf16[1024,128]{1,0:T(8,128)(2,1)S(1)} %collective-permute-done.8.refs_1_, bf16[128,128]{1,0:T(8,128)(2,1)S(1)} %collective-permute-done.9.refs_2_, bf16[1024,128]{1,0:T(8,128)(2,1)S(1)} %collective-permute-done.10.refs_3_, ...), custom_call_target="tpu_custom_call" | custom-call | flops 1 | bytes 1 | tf_op jit(solution)/shard_map/work/pallas_call | solution.py:218
  26.1 0.8 %add.3 = (bf16[4,1024,128]{2,1,0:T(8,128)(2,1)}, bf16[16,512]{1,0:T(8,128)(2,1)}) custom-call(bf16[1,1040,128]{2,1,0:T(8,128)(2,1)S(1)} %collective-permute-done.5.refs_5_.arrived, bf16[4,1040,128]{2,1,0:T(8,128)(2,1)S(1)} %work.13.kept), custom_call_target="tpu_custom_call" | custom-call | flops 1 | bytes 1 | tf_op jit(solution)/shard_map/add/pallas_call | solution.py:278
  26.8 0.8 %add.4 = (bf16[4,1024,128]{2,1,0:T(8,128)(2,1)}, bf16[16,512]{1,0:T(8,128)(2,1)}) custom-call(bf16[1,1040,128]{2,1,0:T(8,128)(2,1)S(1)} %collective-permute-done.7.refs_6_.arrived, bf16[4,1040,128]{2,1,0:T(8,128)(2,1)S(1)} %work.13.kept, bf16[4,1024,128]{2,1,0:T(8,128)(2,1)} %get-tuple-element.34.rest_0_, ...), custom_call_target="tpu_custom_call", output_to_operand_aliasing={{0}: (2, {}), {1}: (3, {})} | custom-call | flops 1 | bytes 1 | tf_op jit(solution)/shard_map/add/pallas_call | solution.py:278
  27.6 3.3 %collective-permute-done.6.arrived = bf16[2,1040,128]{2,1,0:T(8,128)(2,1)S(1)} collective-permute-done((bf16[2,1040,128]{2,1,0:T(8,128)(2,1)S(1)}, bf16[2,1040,128]{2,1,0:T(8,128)(2,1)S(1)}, u32[]{:S(2)}, u32[]{:S(2)}) %collective-permute-start.6) | collective-permute-done | bytes 532512 | tf_op jit(solution)/shard_map/ppermute | solution.py:21
  30.9 0.9 %add.5 = (bf16[4,1024,128]{2,1,0:T(8,128)(2,1)}, bf16[16,512]{1,0:T(8,128)(2,1)}) custom-call(bf16[2,1040,128]{2,1,0:T(8,128)(2,1)S(1)} %collective-permute-done.6.arrived, bf16[4,1040,128]{2,1,0:T(8,128)(2,1)S(1)} %work.13.kept, bf16[4,1024,128]{2,1,0:T(8,128)(2,1)} %get-tuple-element.36.rest_0_, ...), custom_call_target="tpu_custom_call", output_to_operand_aliasing={{0}: (2, {}), {1}: (3, {})} | custom-call | flops 1 | bytes 1 | tf_op jit(solution)/shard_map/add/pallas_call | solution.py:278
Async XLA Ops:
  1.7 2.0 %collective-permute-start.1 = (bf16[1056,128]{1,0:T(8,128)(2,1)S(1)}, bf16[1056,128]{1,0:T(8,128)(2,1)S(1)}, u32[]{:S(2)}, u32[]{:S(2)}) collective-permute-start(bf16[1056,128]{1,0:T(8,128)(2,1)S(1)} %work.7.refs_5_), channel_id=1, source_target_pairs={{0,1},{1,0},{2,3},{3,2},{4,5},{5,4},{6,7},{7,6},{8,9},{9,8},{10,11... | collective-permute-start | bytes 811016 | tf_op jit(solution)/shard_map/ppermute | solution.py:21
  3.6 3.6 %collective-permute-start = (bf16[1056,128]{1,0:T(8,128)(2,1)S(1)}, bf16[1056,128]{1,0:T(8,128)(2,1)S(1)}, u32[]{:S(2)}, u32[]{:S(2)}) collective-permute-start(bf16[1056,128]{1,0:T(8,128)(2,1)S(1)} %get-tuple-element.22), channel_id=1, source_target_pairs={{0,1},{1,0},{2,3},{3,2},{4,5},{5,4},{6,7},{7,6},{8,9},{9,8},{10,11... | collective-permute-start | bytes 811016 | tf_op jit(solution)/shard_map/ppermute | solution.py:21
  4.2 10.2 %collective-permute-start.5 = (bf16[1,1040,128]{2,1,0:T(8,128)(2,1)S(1)}, bf16[1,1040,128]{2,1,0:T(8,128)(2,1)S(1)}, u32[]{:S(2)}, u32[]{:S(2)}) collective-permute-start(bf16[1,1040,128]{2,1,0:T(8,128)(2,1)S(1)} %work.9.refs_7_), channel_id=1, source_target_pairs={{0,4},{4,0},{8,12},{12,8},{16,20},{20,16},{24,28},{28,24},{1,5},{5... | collective-permute-start | bytes 798728 | tf_op jit(solution)/shard_map/ppermute | solution.py:21
  8.8 2.4 %collective-permute-start.2 = (bf16[1024,128]{1,0:T(8,128)(2,1)S(1)}, bf16[1024,128]{1,0:T(8,128)(2,1)S(1)}, u32[]{:S(2)}, u32[]{:S(2)}) collective-permute-start(bf16[1024,128]{1,0:T(8,128)(2,1)S(1)} %get-tuple-element.24), channel_id=1, source_target_pairs={{0,1},{1,0},{2,3},{3,2},{4,5},{5,4},{6,7},{7,6},{8,9},{9,8},{10,11... | collective-permute-start | bytes 786440 | tf_op jit(solution)/shard_map/ppermute | solution.py:21
  8.9 2.4 %collective-permute-start.4 = (bf16[1024,128]{1,0:T(8,128)(2,1)S(1)}, bf16[1024,128]{1,0:T(8,128)(2,1)S(1)}, u32[]{:S(2)}, u32[]{:S(2)}) collective-permute-start(bf16[1024,128]{1,0:T(8,128)(2,1)S(1)} %get-tuple-element.26), channel_id=1, source_target_pairs={{0,1},{1,0},{2,3},{3,2},{4,5},{5,4},{6,7},{7,6},{8,9},{9,8},{10,11... | collective-permute-start | bytes 786440 | tf_op jit(solution)/shard_map/ppermute | solution.py:21
  9.4 10.6 %collective-permute-start.7 = (bf16[1,1040,128]{2,1,0:T(8,128)(2,1)S(1)}, bf16[1,1040,128]{2,1,0:T(8,128)(2,1)S(1)}, u32[]{:S(2)}, u32[]{:S(2)}) collective-permute-start(bf16[1,1040,128]{2,1,0:T(8,128)(2,1)S(1)} %get-tuple-element.27.refs_4_), channel_id=1, source_target_pairs={{0,4},{4,0},{8,12},{12,8},{16,20},{20,16},{24,28},{28,24},{1,5},{5... | collective-permute-start | bytes 798728 | tf_op jit(solution)/shard_map/ppermute | solution.py:21
  10.1 1.2 %collective-permute-start.3 = (bf16[64,128]{1,0:T(8,128)(2,1)S(1)}, bf16[64,128]{1,0:T(8,128)(2,1)S(1)}, u32[]{:S(2)}, u32[]{:S(2)}) collective-permute-start(bf16[64,128]{1,0:T(8,128)(2,1)S(1)} %get-tuple-element.25), channel_id=1, source_target_pairs={{0,1},{1,0},{2,3},{3,2},{4,5},{5,4},{6,7},{7,6},{8,9},{9,8},{10,11... | collective-permute-start | bytes 49160 | tf_op jit(solution)/shard_map/ppermute | solution.py:21
  15.1 15.8 %collective-permute-start.6 = (bf16[2,1040,128]{2,1,0:T(8,128)(2,1)S(1)}, bf16[2,1040,128]{2,1,0:T(8,128)(2,1)S(1)}, u32[]{:S(2)}, u32[]{:S(2)}) collective-permute-start(bf16[2,1040,128]{2,1,0:T(8,128)(2,1)S(1)} %work.11.refs_5_), channel_id=1, source_target_pairs={{0,4},{4,0},{8,12},{12,8},{16,20},{20,16},{24,28},{28,24},{1,5},{5... | collective-permute-start | bytes 1597448 | tf_op jit(solution)/shard_map/ppermute | solution.py:21
  21.9 1.3 %collective-permute-start.9 = (bf16[128,128]{1,0:T(8,128)(2,1)S(1)}, bf16[128,128]{1,0:T(8,128)(2,1)S(1)}, u32[]{:S(2)}, u32[]{:S(2)}) collective-permute-start(bf16[128,128]{1,0:T(8,128)(2,1)S(1)} %get-tuple-element.30.refs_6_), channel_id=1, source_target_pairs={{0,1},{1,0},{2,3},{3,2},{4,5},{5,4},{6,7},{7,6},{8,9},{9,8},{10,11... | collective-permute-start | bytes 98312 | tf_op jit(solution)/shard_map/ppermute | solution.py:21
  22.0 1.7 %collective-permute-start.8 = (bf16[1024,128]{1,0:T(8,128)(2,1)S(1)}, bf16[1024,128]{1,0:T(8,128)(2,1)S(1)}, u32[]{:S(2)}, u32[]{:S(2)}) collective-permute-start(bf16[1024,128]{1,0:T(8,128)(2,1)S(1)} %get-tuple-element.29), channel_id=1, source_target_pairs={{0,1},{1,0},{2,3},{3,2},{4,5},{5,4},{6,7},{7,6},{8,9},{9,8},{10,11... | collective-permute-start | bytes 786440 | tf_op jit(solution)/shard_map/ppermute | solution.py:21
  22.5 1.5 %collective-permute-start.10 = (bf16[1024,128]{1,0:T(8,128)(2,1)S(1)}, bf16[1024,128]{1,0:T(8,128)(2,1)S(1)}, u32[]{:S(2)}, u32[]{:S(2)}) collective-permute-start(bf16[1024,128]{1,0:T(8,128)(2,1)S(1)} %get-tuple-element.31), channel_id=1, source_target_pairs={{0,1},{1,0},{2,3},{3,2},{4,5},{5,4},{6,7},{7,6},{8,9},{9,8},{10,11... | collective-permute-start | bytes 786440 | tf_op jit(solution)/shard_map/ppermute | solution.py:21
  22.6 1.8 %collective-permute-start.11 = (bf16[1024,128]{1,0:T(8,128)(2,1)S(1)}, bf16[1024,128]{1,0:T(8,128)(2,1)S(1)}, u32[]{:S(2)}, u32[]{:S(2)}) collective-permute-start(bf16[1024,128]{1,0:T(8,128)(2,1)S(1)} %get-tuple-element.32), channel_id=1, source_target_pairs={{0,1},{1,0},{2,3},{3,2},{4,5},{5,4},{6,7},{7,6},{8,9},{9,8},{10,11... | collective-permute-start | bytes 786440 | tf_op jit(solution)/shard_map/ppermute | solution.py:21
  23.2 1.6 %collective-permute-start.12 = (bf16[1024,128]{1,0:T(8,128)(2,1)S(1)}, bf16[1024,128]{1,0:T(8,128)(2,1)S(1)}, u32[]{:S(2)}, u32[]{:S(2)}) collective-permute-start(bf16[1024,128]{1,0:T(8,128)(2,1)S(1)} %get-tuple-element.33), channel_id=1, source_target_pairs={{0,1},{1,0},{2,3},{3,2},{4,5},{5,4},{6,7},{7,6},{8,9},{9,8},{10,11... | collective-permute-start | bytes 786440 | tf_op jit(solution)/shard_map/ppermute | solution.py:21

commit v4 on v3

v4 whole, which is shorter than its diff:
```python
import functools

import jax
import jax.numpy as jnp
from jax import lax
from jax.experimental import pallas as pl
from jax.experimental.pallas import tpu as pltpu
from jax.sharding import PartitionSpec as P

HALF = 16
LIMIT = 48 * 2**20
LIGHT = pl.CostEstimate(flops=1, bytes_accessed=1, transcendentals=0)
VMEM = pl.BlockSpec(memory_space=pltpu.VMEM)
HBM = pl.BlockSpec(memory_space=pltpu.HBM)
ANY = pl.BlockSpec(memory_space=pl.ANY)


def swapped(value, axis):
    pairs = [(source, source ^ 1) for source in range(lax.axis_size(axis))]
    return lax.ppermute(value, axis, pairs)


def in_vmem(value):
    return pltpu.with_memory_space_constraint(value, pltpu.VMEM)


def in_hbm(value):
    return pltpu.with_memory_space_constraint(value, pltpu.HBM)


def split_by(value, size):
    if size & (size - 1) == 0:
        return value >> (size.bit_length() - 1), value & (size - 1)
    return value // size, value % size


def tile_at(phase, piece, partner):
    blk_bit = lax.axis_index("blk") & 1
    sub_bit = lax.axis_index("sub") & 1
    row_bit = blk_bit if phase == 1 else 1 - blk_bit
    return 4 * piece + 2 * row_bit + (1 - sub_bit if partner else sub_bit)


def start(source, target, sem):
    copy = pltpu.make_async_copy(source, target, sem)
    copy.start()
    return copy


def compose_maps(pick, span, count, cols, one_table, two_table, one_rows, two_rows, out):
    slots = cols.shape[0]
    lanes = lax.broadcasted_iota(jnp.int32, (1, one_table.shape[-1]), 1)

    def put(row, column_id):
        block, inside = split_by(column_id, span)
        pair_block, high_one = split_by(block, 2)
        sub, place = split_by(inside, count)
        sub_pair, high_two = split_by(sub, 2)
        pair = pair_block * span + inside
        group = pair_block * (span // 2) + sub_pair * count + place
        one_rows[pl.ds(row, 1), :] = jnp.where(high_one == 1, one_table[pl.ds(pair, 1), :], lanes)
        two_rows[pl.ds(row, 1), :] = jnp.where(high_two == 1, two_table[pl.ds(group, 1), :], lanes)

    one_rows[...] = jnp.zeros_like(one_rows)
    two_rows[...] = jnp.zeros_like(two_rows)
    tile = tile_at(*pick)
    for slot in range(slots):
        put(slot, cols[slot, tile])
    put(slots, lax.axis_index("blk") * span + lax.axis_index("sub") * count + tile)
    maps = jnp.take_along_axis(two_rows[...], one_rows[...], axis=1)
    out[...] = maps.astype(jnp.float32).astype(out.dtype)


def merge_tile(slots, width, own, other, own_side, other_side, put):
    along = lax.broadcasted_iota(jnp.int32, (width, width), 0).astype(jnp.float32)
    own_maps, other_maps = (x[:HALF].astype(jnp.float32) for x in (own_side, other_side))

    def hot(maps, row):
        return (maps[row : row + 1, :] == along).astype(jnp.bfloat16)

    def columns(row):
        return jnp.concatenate([hot(own_maps, row), hot(other_maps, row)], 1)

    def across(value, row):
        return lax.dot_general(
            value, columns(row), (((1,), (1,)), ((), ())), preferred_element_type=jnp.float32
        )

    def block_of(parts, slot):
        here, at = divmod(slot, slots // len(parts))
        return parts[here][at * width : (at + 1) * width, :]

    def moved(rows_hot, tile, pair):
        blocks = [block_of(tile, slot) for slot in (2 * pair, 2 * pair + 1)]
        value = jnp.dot(
            rows_hot, jnp.concatenate(blocks, 1), preferred_element_type=jnp.float32
        ).astype(jnp.bfloat16)
        return [value[:, :width], value[:, width:]]

    own_rows, other_rows = hot(own_maps, slots), hot(other_maps, slots)
    rows_done = []
    for pair in range(slots // 2):
        halves = moved(own_rows, own, pair), moved(other_rows, other, pair)
        rows_done += [jnp.concatenate(both, 1) for both in zip(*halves)]
    for slot, value in enumerate(rows_done):
        put(slot * width, across(value, slot).astype(jnp.bfloat16))
    feats = jnp.concatenate([own_side[HALF:], other_side[HALF:]], 1)
    put(slots * width, across(feats, slots).astype(jnp.bfloat16))


def work_kernel(plan, refs):
    rows = plan.rows
    copies, small = [], []
    if plan.picks:
        adjacency, features, cols, match_one, match_two = [refs[at] for at in plan.sources]
        cols_here, one_rows, two_rows, sems = [refs[at] for at in plan.scratch]
        one_table, two_table = [refs[at] for at in plan.tables]
        width = adjacency.shape[-1]
        small = [start(cols, cols_here, sems.at[2])]
        if plan.first:
            small += [
                start(match_one, one_table, sems.at[0]),
                start(match_two, two_table, sems.at[1]),
            ]
        sides = []
        for i, (pick, (mains, main_at, side, side_at)) in enumerate(zip(plan.picks, plan.targets)):
            tile = tile_at(*pick)
            lanes = pl.ds(pl.multiple_of(tile * width, width), width)
            sides.append(refs[side].at[pl.ds(side_at, HALF)])
            part = rows // len(mains)
            for at, main in enumerate(mains):
                copies.append(
                    start(
                        adjacency.at[tile, pl.ds(at * part, part)],
                        refs[main].at[pl.ds(main_at, part)],
                        sems.at[plan.sems[i] + at],
                    )
                )
            copies.append(
                start(
                    features.at[:, lanes],
                    refs[side].at[pl.ds(side_at + HALF, features.shape[0])],
                    sems.at[plan.sems[i] + len(mains)],
                )
            )
    for i, (own, other) in enumerate(plan.merges):
        tiles = [
            [refs[main].at[pl.ds(at, rows // len(mains))] for main in mains]
            for mains, at, _, _ in (own, other)
        ]
        ends = [refs[side][at : at + plan.depth - rows, :] for _, _, side, at in (own, other)]

        def put(row, value, base=i * plan.sum_depth):
            first, out = max(known for known in plan.outs if known[0] <= base + row)
            here = pl.ds(base + row - first, value.shape[0])
            refs[out][here, :] = value

        merge_tile(rows // plan.width, plan.width, *tiles, *ends, put)
    for copy in small:
        copy.wait()
    for i, pick in enumerate(plan.picks):
        compose_maps(
            pick, plan.span, plan.count, cols_here, one_table, two_table, one_rows, two_rows,
            sides[i],
        )
    for copy in copies:
        copy.wait()


class Plan:
    pass


class Work:
    def __init__(self, features, adjacency, cols, match_one, match_two, span):
        self.sources = [in_hbm(x) for x in (adjacency, features, cols, match_one, match_two)]
        self.tables = []
        self.span = span
        self.own, self.other = {}, {}

    def run(self, merges=(), keys=(), leaving=(), apart=(), after=(), cuts=()):
        adjacency, features, cols, match_one, match_two = self.sources
        rows, width = adjacency.shape[1:]
        plan = Plan()
        plan.rows, plan.depth = rows, rows + HALF + features.shape[0]
        plan.width, plan.sum_depth = width, rows + features.shape[0]
        plan.span, plan.count = self.span, cols.shape[1]
        plan.picks = [(*key, True) for key in leaving] + [(*key, False) for key in keys]
        ins, specs, shapes, scratch = [], [], [], []

        def take(value, spec):
            for place, known in enumerate(ins):
                if known is value:
                    return place
            ins.append(value)
            specs.append(spec)
            return len(ins) - 1

        plan.sources = [take(value, HBM) for value in self.sources] if plan.picks else []
        plan.first = not self.tables
        plan.tables = [take(value, VMEM) for value in self.tables] if plan.picks else []
        plan.merges = [
            [
                ([take(main, VMEM) for main in mains], at, take(side, VMEM), side_at)
                for mains, at, side, side_at in (self.own[key], self.other[key])
            ]
            for key in merges
        ]
        for value in after:
            take(value, ANY)

        def give(depth):
            shapes.append(pltpu.VMEM((depth, width), adjacency.dtype))
            return len(ins) + len(shapes) - 1

        edges = [0, *cuts, len(merges) * plan.sum_depth]
        sizes = [high - low for low, high in zip(edges, edges[1:])] if merges else []
        plan.outs = [(low, give(size)) for low, size in zip(edges, sizes)]
        extra = plan.depth - rows
        if apart:
            side = give(len(leaving) * extra)
            plan.targets = [
                ([give(rows // parts) for _ in range(parts)], 0, side, i * extra)
                for i, parts in enumerate(apart)
            ]
        else:
            mains = [give(plan.depth) for _ in leaving]
            plan.targets = [([main], 0, main, rows) for main in mains]
        if keys:
            pack = give(len(keys) * plan.depth)
            plan.targets += [
                ([pack], i * plan.depth, pack, i * plan.depth + rows) for i in range(len(keys))
            ]
        if plan.first:
            for table in (match_one, match_two):
                plan.tables.append(len(ins) + len(shapes))
                shapes.append(pltpu.VMEM(table.shape, table.dtype))
        plan.sems, total = [], 3
        for mains, _, _, _ in plan.targets:
            plan.sems.append(total)
            total += len(mains) + 1
        if plan.picks:
            scratch = [
                pltpu.SMEM(cols.shape, jnp.int32),
                pltpu.VMEM((HALF, width), jnp.int32),
                pltpu.VMEM((HALF, width), jnp.int32),
                pltpu.SemaphoreType.DMA((total,)),
            ]
        plan.scratch = [len(ins) + len(shapes) + i for i in range(len(scratch))]
        outs = pl.pallas_call(
            lambda *refs: work_kernel(plan, refs),
            out_shape=shapes,
            in_specs=specs,
            out_specs=[VMEM] * len(shapes),
            scratch_shapes=scratch,
            compiler_params=pltpu.CompilerParams(vmem_limit_bytes=LIMIT),
            cost_estimate=LIGHT,
            name="work",
        )(*ins)
        made = {len(ins) + i: value for i, value in enumerate(outs)}
        if plan.first:
            self.tables = [in_vmem(made[at]) for at in plan.tables]
        crossed = {}
        for pick, (mains, main_at, side, side_at) in zip(plan.picks, plan.targets):
            where = self.other if pick[2] else self.own
            for place in (*mains, side):
                if place not in crossed:
                    value = swapped(made[place], "sub") if pick[2] else made[place]
                    crossed[place] = in_vmem(value)
            where[pick[:2]] = ([crossed[main] for main in mains], main_at, crossed[side], side_at)
        return list(outs[: len(sizes)] if merges else outs)


def add_kernel(begin, depth, rows, arrived, kept, *rest):
    tiles_out, feats_out, total, sems = rest[-4:]
    width = arrived.shape[-1]
    end = begin + arrived.shape[0]
    copies = []
    for tile in range(begin // depth, -(-end // depth)):
        for low, high in ((0, rows), (rows, depth)):
            low, high = max(begin, tile * depth + low), min(end, tile * depth + high)
            if low >= high:
                continue
            here = slice(low - begin, high - begin)
            value = kept[low:high].astype(jnp.float32) + arrived[here].astype(jnp.float32)
            total[here] = value.astype(jnp.bfloat16)
            if high - tile * depth > rows:
                target = feats_out.at[:, pl.ds(tile * width, width)]
            else:
                target = tiles_out.at[tile, pl.ds(low - tile * depth, high - low)]
            source = total.at[pl.ds(low - begin, high - low)]
            copies.append(start(source, target, sems.at[len(copies)]))
    for copy in copies:
        copy.wait()


def added(begin, depth, rows, arrived, kept, before):
    size, width = arrived.shape
    quarter = kept.shape[0] // depth
    shapes = (
        jax.ShapeDtypeStruct((quarter, rows, width), jnp.bfloat16),
        jax.ShapeDtypeStruct((depth - rows, quarter * width), jnp.bfloat16),
    )
    return pl.pallas_call(
        functools.partial(add_kernel, begin, depth, rows),
        out_shape=shapes,
        in_specs=[VMEM, VMEM] + [HBM] * len(before),
        out_specs=(HBM, HBM),
        scratch_shapes=[
            pltpu.VMEM((size, width), jnp.bfloat16),
            pltpu.SemaphoreType.DMA((2 * quarter,)),
        ],
        input_output_aliases={2: 0, 3: 1} if before else {},
        compiler_params=pltpu.CompilerParams(vmem_limit_bytes=LIMIT),
        cost_estimate=LIGHT,
        name="add",
    )(in_vmem(arrived), in_vmem(kept), *before)


def per_device(features, adjacency, col_tiles, match_one, match_two):
    count, slots, width = adjacency.shape[:3]
    feat_count = features.shape[0]
    quarter = count // 4
    span = lax.axis_size("sub") * count
    blocks = adjacency.reshape(count, slots * width, width)
    work = Work(features, blocks, col_tiles.T, match_one, match_two, span)

    send = [(0, piece) for piece in range(quarter)]
    keep = [(1, piece) for piece in range(quarter)]
    rows = slots * width
    depth = rows + feat_count
    first = work.run(leaving=send[:1])
    work.run(keys=send[:1], leaving=send[1:2], after=first[:1])
    parcels = work.run(merges=send[:1])
    arrived = [swapped(parcels[0], "blk")]
    work.run(keys=send[1:], leaving=send[2:], apart=[1] * (quarter - 2), after=parcels)
    parcels = work.run(merges=send[1:2])
    arrived.append(swapped(parcels[0], "blk"))
    cut = (quarter - 3) * depth + slots // 2 * width
    parcels = work.run(merges=send[2:], after=parcels + arrived[:1], cuts=[cut])
    arrived += [swapped(parcel, "blk") for parcel in parcels]
    last = work.run(
        keys=keep, leaving=keep, apart=[1] * quarter, after=parcels[:1] + arrived[1:2]
    )
    kept = work.run(merges=keep, after=last[:1])[0]
    out = []
    begin = 0
    for part in arrived:
        out = added(begin, depth, rows, part, kept, out)
        begin += part.shape[0]
    return out[0].reshape(quarter, slots, width, width), out[1]


def solution(mesh):
    placed = (
        P(None, ("blk", "sub")),
        P(("blk", "sub"), None, None, None),
        P(("blk", "sub"), None),
        P(),
        P(),
    )
    return jax.shard_map(
        per_device,
        mesh=mesh,
        in_specs=placed,
        out_specs=(P(("blk", "sub"), None, None, None), P(None, ("blk", "sub"))),
        check_vma=False,
    )
```

time: 32 us -> 31.7 us (level)
  waiting for transfers between devices: 11.9 us -> 9.29 us
  starting transfers between devices: 8.34 us -> 9.78 us
  Pallas kernels: 10.8 us -> 11.6 us
    ppermute x13 -> x14, waiting for transfers between devices: 11.9 us -> 9.29 us  [swapped(): return lax.ppermute(value, axis, pairs)]
    ppermute x13 -> x14, starting transfers between devices: 8.34 us -> 9.78 us  [swapped(): return lax.ppermute(value, axis, pairs)]
    pallas_call x3 -> x4, Pallas kernels: 2.4 us -> 3.33 us  [added(): pl.pallas_call(functools.partial(add_kernel, begin, depth, rows), out_sha...]
    pallas_call x7 -> x8, Pallas kernels: 8.36 us -> 8.27 us  [run(): pl.pallas_call(lambda *refs: work_kernel(plan, refs), out_shape=shapes, i...]
  transfers between devices with their start and end apart: 13 -> 14, of which waited for: 9 -> 5; matrix products, arithmetic and copies ran while one was open for 0% -> 0% of each run, Pallas kernels for 28% -> 31%
where the time goes in v4:
time: 31.7 us; the launch traced here: 31.4 us
  Pallas kernels  11.6 us (37%)
  starting transfers between devices  9.78 us (31%)
  waiting for transfers between devices  9.29 us (29%)
  between operations  0.75 us (2%)
    ppermute x14, starting transfers between devices, swapped(): return lax.ppermute(value, axis, pairs)  9.78 us
    ppermute x14, waiting for transfers between devices, swapped(): return lax.ppermute(value, axis, pairs)  9.29 us
    pallas_call x8, Pallas kernels, run(): pl.pallas_call(lambda *refs: work_kernel(plan, refs), out_shape=shapes, i...  8.27 us
    pallas_call x4, Pallas kernels, added(): pl.pallas_call(functools.partial(add_kernel, begin, depth, rows), out_sha...  3.33 us
  transfers between devices with their start and end apart: 14, of which 5 were waited for; matrix products, arithmetic and copies ran while one was open for 0% of the time, Pallas kernels for 31%

profile of v4, /device:TPU:0, one launch (start us, length us, event | category | flops | bytes accessed | tf_op | source)
XLA Modules:
  0.0 31.4 jit_solution(2624297923078839885)
XLA Ops:
  0.6 1.1 %work.8 = (bf16[1056,128]{1,0:T(8,128)(2,1)S(1)}, s32[256,128]{1,0:T(8,128)S(1)}, s32[128,128]{1,0:T(8,128)S(1)}) custom-call(bf16[16,1024,128]{2,1,0:T(8,128)(2,1)} %bitcast.3, bf16[16,2048]{1,0:T(8,128)(2,1)} %refs_1_.7, s32[8,16]{1,0:T(8,128)} %bitcast.8, s32[256,128]{1,0:T(8,128)} %refs_3_.7, s32[128,128]{1,0:T(8,128)} %refs_4_.7), custom_call_target="tpu_custom_call" | custom-call | flops 1 | bytes 1 | tf_op jit(solution)/shard_map/work/pallas_call | solution.py:250
  1.7 0.5 %collective-permute-start = (bf16[1056,128]{1,0:T(8,128)(2,1)S(1)}, bf16[1056,128]{1,0:T(8,128)(2,1)S(1)}, u32[]{:S(2)}, u32[]{:S(2)}) collective-permute-start(bf16[1056,128]{1,0:T(8,128)(2,1)S(1)} %get-tuple-element.29.refs_7_), channel_id=1, source_target_pairs={{0,1},{1,0},{2,3},{3,2},{4,5},{5,4},{6,7},{7,6},{8,9},{9,8},{10,11... | collective-permute-start | bytes 811016 | tf_op jit(solution)/shard_map/ppermute | solution.py:20
  2.3 1.1 %work.9 = (bf16[1056,128]{1,0:T(8,128)(2,1)S(1)}, bf16[1056,128]{1,0:T(8,128)(2,1)S(1)}) custom-call(bf16[16,1024,128]{2,1,0:T(8,128)(2,1)} %bitcast.4, bf16[16,2048]{1,0:T(8,128)(2,1)} %refs_1_.7, s32[8,16]{1,0:T(8,128)} %bitcast.9, s32[256,128]{1,0:T(8,128)} %refs_3_.7, s32[128,128]{1,0:T(8,128)} %refs_4_.7, s32[256,128]{1,0:T(8,128)S(1)} %get-tuple-element.27.refs_5_, ...), custom_call_target="tpu_custom_call" | custom-call | flops 1 | bytes 1 | tf_op jit(solution)/shard_map/work/pallas_call | solution.py:250
  3.4 0.1 collective-permute-start.4
  3.5 0.0 collective-permute-done.refs_1_
  3.5 0.4 %work.10.refs_7_ = bf16[1040,128]{1,0:T(8,128)(2,1)S(1)} custom-call(bf16[1056,128]{1,0:T(8,128)(2,1)S(1)} %get-tuple-element.30.refs_0_, bf16[1056,128]{1,0:T(8,128)(2,1)S(1)} %collective-permute-done.refs_1_), custom_call_target="tpu_custom_call" | custom-call | flops 1 | bytes 1 | tf_op jit(solution)/shard_map/work/pallas_call | solution.py:250
  3.9 3.0 %collective-permute-start.5 = (bf16[1040,128]{1,0:T(8,128)(2,1)S(1)}, bf16[1040,128]{1,0:T(8,128)(2,1)S(1)}, u32[]{:S(2)}, u32[]{:S(2)}) collective-permute-start(bf16[1040,128]{1,0:T(8,128)(2,1)S(1)} %work.10.refs_7_), channel_id=1, source_target_pairs={{0,4},{4,0},{8,12},{12,8},{16,20},{20,16},{24,28},{28,24},{1,5},{5... | collective-permute-start | bytes 798728 | tf_op jit(solution)/shard_map/ppermute | solution.py:20
  6.9 1.4 %work.11 = (bf16[64,128]{1,0:T(8,128)(2,1)S(1)}, bf16[1024,128]{1,0:T(8,128)(2,1)S(1)}, bf16[1024,128]{1,0:T(8,128)(2,1)S(1)}, bf16[3168,128]{1,0:T(8,128)(2,1)S(1)}) custom-call(bf16[16,1024,128]{2,1,0:T(8,128)(2,1)} %bitcast.5, bf16[16,2048]{1,0:T(8,128)(2,1)} %refs_1_.7, s32[8,16]{1,0:T(8,128)} %bitcast.10, s32[256,128]{1,0:T(8,128)} %refs_3_.7, ...), custom_call_target="tpu_custom_call" | custom-call | flops 1 | bytes 1 | tf_op jit(solution)/shard_map/work/pallas_call | solution.py:250
  8.4 0.0 collective-permute-done.4.refs_1_
  8.4 0.4 %work.12.refs_4_ = bf16[1040,128]{1,0:T(8,128)(2,1)S(1)} custom-call(bf16[3168,128]{1,0:T(8,128)(2,1)S(1)} %get-tuple-element.31.refs_0_, bf16[1056,128]{1,0:T(8,128)(2,1)S(1)} %collective-permute-done.4.refs_1_), custom_call_target="tpu_custom_call" | custom-call | flops 1 | bytes 1 | tf_op jit(solution)/shard_map/work/pallas_call | solution.py:250
  8.8 0.1 collective-permute-start.7
  8.9 0.1 collective-permute-start.1
  9.0 0.5 %collective-permute-start.3 = (bf16[1024,128]{1,0:T(8,128)(2,1)S(1)}, bf16[1024,128]{1,0:T(8,128)(2,1)S(1)}, u32[]{:S(2)}, u32[]{:S(2)}) collective-permute-start(bf16[1024,128]{1,0:T(8,128)(2,1)S(1)} %get-tuple-element.34), channel_id=1, source_target_pairs={{0,1},{1,0},{2,3},{3,2},{4,5},{5,4},{6,7},{7,6},{8,9},{9,8},{10,11... | collective-permute-start | bytes 786440 | tf_op jit(solution)/shard_map/ppermute | solution.py:20
  9.5 0.1 collective-permute-start.2
  9.6 1.3 %collective-permute-done.2.refs_2_ = bf16[64,128]{1,0:T(8,128)(2,1)S(1)} collective-permute-done((bf16[64,128]{1,0:T(8,128)(2,1)S(1)}, bf16[64,128]{1,0:T(8,128)(2,1)S(1)}, u32[]{:S(2)}, u32[]{:S(2)}) %collective-permute-start.2) | collective-permute-done | bytes 16416 | tf_op jit(solution)/shard_map/ppermute | solution.py:20
  10.9 0.0 collective-permute-done.1.refs_1_
  10.9 0.0 collective-permute-done.3.refs_3_
  10.9 3.2 %collective-permute-done.5.refs_5_.arrived = bf16[1040,128]{1,0:T(8,128)(2,1)S(1)} collective-permute-done((bf16[1040,128]{1,0:T(8,128)(2,1)S(1)}, bf16[1040,128]{1,0:T(8,128)(2,1)S(1)}, u32[]{:S(2)}, u32[]{:S(2)}) %collective-permute-start.5) | collective-permute-done | bytes 266272 | tf_op jit(solution)/shard_map/ppermute | solution.py:20
  14.1 0.7 %work.13 = (bf16[1552,128]{1,0:T(8,128)(2,1)S(1)}, bf16[528,128]{1,0:T(8,128)(2,1)S(1)}) custom-call(bf16[3168,128]{1,0:T(8,128)(2,1)S(1)} %get-tuple-element.31.refs_0_, bf16[1024,128]{1,0:T(8,128)(2,1)S(1)} %collective-permute-done.1.refs_1_, bf16[64,128]{1,0:T(8,128)(2,1)S(1)} %collective-permute-done.2.refs_2_, ...), custom_call_target="tpu_custom_call" | custom-call | flops 1 | bytes 1 | tf_op jit(solution)/shard_map/work/pallas_call | solution.py:250
  14.9 2.1 %collective-permute-start.13 = (bf16[1552,128]{1,0:T(8,128)(2,1)S(1)}, bf16[1552,128]{1,0:T(8,128)(2,1)S(1)}, u32[]{:S(2)}, u32[]{:S(2)}) collective-permute-start(bf16[1552,128]{1,0:T(8,128)(2,1)S(1)} %get-tuple-element.37.refs_7_), channel_id=1, source_target_pairs={{0,4},{4,0},{8,12},{12,8},{16,20},{20,16},{24,28},{28,24},{1,5},{5... | collective-permute-start | bytes 1191944 | tf_op jit(solution)/shard_map/ppermute | solution.py:20
  17.0 2.9 %collective-permute-done.7.refs_8_.arrived = bf16[1040,128]{1,0:T(8,128)(2,1)S(1)} collective-permute-done((bf16[1040,128]{1,0:T(8,128)(2,1)S(1)}, bf16[1040,128]{1,0:T(8,128)(2,1)S(1)}, u32[]{:S(2)}, u32[]{:S(2)}) %collective-permute-start.7) | collective-permute-done | bytes 266272 | tf_op jit(solution)/shard_map/ppermute | solution.py:20
  19.8 1.7 %work.14 = (bf16[128,128]{1,0:T(8,128)(2,1)S(1)}, bf16[1024,128]{1,0:T(8,128)(2,1)S(1)}, bf16[1024,128]{1,0:T(8,128)(2,1)S(1)}, bf16[1024,128]{1,0:T(8,128)(2,1)...) custom-call(bf16[16,1024,128]{2,1,0:T(8,128)(2,1)} %bitcast.6, bf16[16,2048]{1,0:T(8,128)(2,1)} %refs_1_.7, ...), custom_call_target="tpu_custom_call" | custom-call | flops 1 | bytes 1 | tf_op jit(solution)/shard_map/work/pallas_call | solution.py:250
  21.6 0.1 collective-permute-start.8
  21.7 0.5 %collective-permute-start.9 = (bf16[128,128]{1,0:T(8,128)(2,1)S(1)}, bf16[128,128]{1,0:T(8,128)(2,1)S(1)}, u32[]{:S(2)}, u32[]{:S(2)}) collective-permute-start(bf16[128,128]{1,0:T(8,128)(2,1)S(1)} %get-tuple-element.40.refs_6_), channel_id=1, source_target_pairs={{0,1},{1,0},{2,3},{3,2},{4,5},{5,4},{6,7},{7,6},{8,9},{9,8},{10,11... | collective-permute-start | bytes 98312 | tf_op jit(solution)/shard_map/ppermute | solution.py:20
  22.2 0.1 collective-permute-start.10
  22.3 0.4 %collective-permute-start.11 = (bf16[1024,128]{1,0:T(8,128)(2,1)S(1)}, bf16[1024,128]{1,0:T(8,128)(2,1)S(1)}, u32[]{:S(2)}, u32[]{:S(2)}) collective-permute-start(bf16[1024,128]{1,0:T(8,128)(2,1)S(1)} %get-tuple-element.42), channel_id=1, source_target_pairs={{0,1},{1,0},{2,3},{3,2},{4,5},{5,4},{6,7},{7,6},{8,9},{9,8},{10,11... | collective-permute-start | bytes 786440 | tf_op jit(solution)/shard_map/ppermute | solution.py:20
  22.7 0.6 %collective-permute-done.9.refs_2_ = bf16[128,128]{1,0:T(8,128)(2,1)S(1)} collective-permute-done((bf16[128,128]{1,0:T(8,128)(2,1)S(1)}, bf16[128,128]{1,0:T(8,128)(2,1)S(1)}, u32[]{:S(2)}, u32[]{:S(2)}) %collective-permute-start.9) | collective-permute-done | bytes 32800 | tf_op jit(solution)/shard_map/ppermute | solution.py:20
  23.2 0.1 collective-permute-start.12
  23.4 0.0 collective-permute-done.8.refs_1_
  23.4 2.1 %collective-permute-start.6 = (bf16[528,128]{1,0:T(8,128)(2,1)S(1)}, bf16[528,128]{1,0:T(8,128)(2,1)S(1)}, u32[]{:S(2)}, u32[]{:S(2)}) collective-permute-start(bf16[528,128]{1,0:T(8,128)(2,1)S(1)} %get-tuple-element.36), channel_id=1, source_target_pairs={{0,4},{4,0},{8,12},{12,8},{16,20},{20,16},{24,28},{28,24},{1,5},{5... | collective-permute-start | bytes 405512 | tf_op jit(solution)/shard_map/ppermute | solution.py:20
  25.5 0.0 collective-permute-done.10.refs_3_
  25.5 0.0 collective-permute-done.11.refs_4_
  25.5 0.0 collective-permute-done.12.refs_5_
  25.5 1.3 %work.15.kept = bf16[4160,128]{1,0:T(8,128)(2,1)S(1)} custom-call(bf16[4224,128]{1,0:T(8,128)(2,1)S(1)} %get-tuple-element.38.refs_0_, bf16[1024,128]{1,0:T(8,128)(2,1)S(1)} %collective-permute-done.8.refs_1_, bf16[128,128]{1,0:T(8,128)(2,1)S(1)} %collective-permute-done.9.refs_2_, bf16[1024,128]{1,0:T(8,128)(2,1)S(1)} %collective-permute-done.10.refs_3_, ...), custom_call_target="tpu_custom_call" | custom-call | flops 1 | bytes 1 | tf_op jit(solution)/shard_map/work/pallas_call | solution.py:250
  26.8 0.8 %add.4 = (bf16[4,1024,128]{2,1,0:T(8,128)(2,1)}, bf16[16,512]{1,0:T(8,128)(2,1)}) custom-call(bf16[1040,128]{1,0:T(8,128)(2,1)S(1)} %collective-permute-done.5.refs_5_.arrived, bf16[4160,128]{1,0:T(8,128)(2,1)S(1)} %work.15.kept), custom_call_target="tpu_custom_call" | custom-call | flops 1 | bytes 1 | tf_op jit(solution)/shard_map/add/pallas_call | solution.py:304
  27.6 0.8 %add.5 = (bf16[4,1024,128]{2,1,0:T(8,128)(2,1)}, bf16[16,512]{1,0:T(8,128)(2,1)}) custom-call(bf16[1040,128]{1,0:T(8,128)(2,1)S(1)} %collective-permute-done.7.refs_8_.arrived, bf16[4160,128]{1,0:T(8,128)(2,1)S(1)} %work.15.kept, bf16[4,1024,128]{2,1,0:T(8,128)(2,1)} %get-tuple-element.44.rest_0_, ...), custom_call_target="tpu_custom_call", output_to_operand_aliasing={{0}: (2, {}), {1}: (3, {})} | custom-call | flops 1 | bytes 1 | tf_op jit(solution)/shard_map/add/pallas_call | solution.py:304
  28.5 0.0 collective-permute-done.13.arrived
  28.5 0.9 %add.6 = (bf16[4,1024,128]{2,1,0:T(8,128)(2,1)}, bf16[16,512]{1,0:T(8,128)(2,1)}) custom-call(bf16[1552,128]{1,0:T(8,128)(2,1)S(1)} %collective-permute-done.13.arrived, bf16[4160,128]{1,0:T(8,128)(2,1)S(1)} %work.15.kept, bf16[4,1024,128]{2,1,0:T(8,128)(2,1)} %get-tuple-element.46.rest_0_, ...), custom_call_target="tpu_custom_call", output_to_operand_aliasing={{0}: (2, {}), {1}: (3, {})} | custom-call | flops 1 | bytes 1 | tf_op jit(solution)/shard_map/add/pallas_call | solution.py:304
  29.4 1.3 %collective-permute-done.6.arrived = bf16[528,128]{1,0:T(8,128)(2,1)S(1)} collective-permute-done((bf16[528,128]{1,0:T(8,128)(2,1)S(1)}, bf16[528,128]{1,0:T(8,128)(2,1)S(1)}, u32[]{:S(2)}, u32[]{:S(2)}) %collective-permute-start.6) | collective-permute-done | bytes 135200 | tf_op jit(solution)/shard_map/ppermute | solution.py:20
  30.7 0.8 %add.7 = (bf16[4,1024,128]{2,1,0:T(8,128)(2,1)}, bf16[16,512]{1,0:T(8,128)(2,1)}) custom-call(bf16[528,128]{1,0:T(8,128)(2,1)S(1)} %collective-permute-done.6.arrived, bf16[4160,128]{1,0:T(8,128)(2,1)S(1)} %work.15.kept, bf16[4,1024,128]{2,1,0:T(8,128)(2,1)} %get-tuple-element.48.rest_0_, ...), custom_call_target="tpu_custom_call", output_to_operand_aliasing={{0}: (2, {}), {1}: (3, {})} | custom-call | flops 1 | bytes 1 | tf_op jit(solution)/shard_map/add/pallas_call | solution.py:304
Async XLA Ops:
  1.7 1.8 %collective-permute-start = (bf16[1056,128]{1,0:T(8,128)(2,1)S(1)}, bf16[1056,128]{1,0:T(8,128)(2,1)S(1)}, u32[]{:S(2)}, u32[]{:S(2)}) collective-permute-start(bf16[1056,128]{1,0:T(8,128)(2,1)S(1)} %get-tuple-element.29.refs_7_), channel_id=1, source_target_pairs={{0,1},{1,0},{2,3},{3,2},{4,5},{5,4},{6,7},{7,6},{8,9},{9,8},{10,11... | collective-permute-start | bytes 811016 | tf_op jit(solution)/shard_map/ppermute | solution.py:20
  3.4 5.0 %collective-permute-start.4 = (bf16[1056,128]{1,0:T(8,128)(2,1)S(1)}, bf16[1056,128]{1,0:T(8,128)(2,1)S(1)}, u32[]{:S(2)}, u32[]{:S(2)}) collective-permute-start(bf16[1056,128]{1,0:T(8,128)(2,1)S(1)} %get-tuple-element.35), channel_id=1, source_target_pairs={{0,1},{1,0},{2,3},{3,2},{4,5},{5,4},{6,7},{7,6},{8,9},{9,8},{10,11... | collective-permute-start | bytes 811016 | tf_op jit(solution)/shard_map/ppermute | solution.py:20
  3.9 10.2 %collective-permute-start.5 = (bf16[1040,128]{1,0:T(8,128)(2,1)S(1)}, bf16[1040,128]{1,0:T(8,128)(2,1)S(1)}, u32[]{:S(2)}, u32[]{:S(2)}) collective-permute-start(bf16[1040,128]{1,0:T(8,128)(2,1)S(1)} %work.10.refs_7_), channel_id=1, source_target_pairs={{0,4},{4,0},{8,12},{12,8},{16,20},{20,16},{24,28},{28,24},{1,5},{5... | collective-permute-start | bytes 798728 | tf_op jit(solution)/shard_map/ppermute | solution.py:20
  8.8 11.0 %collective-permute-start.7 = (bf16[1040,128]{1,0:T(8,128)(2,1)S(1)}, bf16[1040,128]{1,0:T(8,128)(2,1)S(1)}, u32[]{:S(2)}, u32[]{:S(2)}) collective-permute-start(bf16[1040,128]{1,0:T(8,128)(2,1)S(1)} %work.12.refs_4_), channel_id=1, source_target_pairs={{0,4},{4,0},{8,12},{12,8},{16,20},{20,16},{24,28},{28,24},{1,5},{5... | collective-permute-start | bytes 798728 | tf_op jit(solution)/shard_map/ppermute | solution.py:20
  8.9 2.0 %collective-permute-start.1 = (bf16[1024,128]{1,0:T(8,128)(2,1)S(1)}, bf16[1024,128]{1,0:T(8,128)(2,1)S(1)}, u32[]{:S(2)}, u32[]{:S(2)}) collective-permute-start(bf16[1024,128]{1,0:T(8,128)(2,1)S(1)} %get-tuple-element.32), channel_id=1, source_target_pairs={{0,1},{1,0},{2,3},{3,2},{4,5},{5,4},{6,7},{7,6},{8,9},{9,8},{10,11... | collective-permute-start | bytes 786440 | tf_op jit(solution)/shard_map/ppermute | solution.py:20
  9.0 1.9 %collective-permute-start.3 = (bf16[1024,128]{1,0:T(8,128)(2,1)S(1)}, bf16[1024,128]{1,0:T(8,128)(2,1)S(1)}, u32[]{:S(2)}, u32[]{:S(2)}) collective-permute-start(bf16[1024,128]{1,0:T(8,128)(2,1)S(1)} %get-tuple-element.34), channel_id=1, source_target_pairs={{0,1},{1,0},{2,3},{3,2},{4,5},{5,4},{6,7},{7,6},{8,9},{9,8},{10,11... | collective-permute-start | bytes 786440 | tf_op jit(solution)/shard_map/ppermute | solution.py:20
  9.5 1.4 %collective-permute-start.2 = (bf16[64,128]{1,0:T(8,128)(2,1)S(1)}, bf16[64,128]{1,0:T(8,128)(2,1)S(1)}, u32[]{:S(2)}, u32[]{:S(2)}) collective-permute-start(bf16[64,128]{1,0:T(8,128)(2,1)S(1)} %get-tuple-element.33), channel_id=1, source_target_pairs={{0,1},{1,0},{2,3},{3,2},{4,5},{5,4},{6,7},{7,6},{8,9},{9,8},{10,11... | collective-permute-start | bytes 49160 | tf_op jit(solution)/shard_map/ppermute | solution.py:20
  14.9 13.6 %collective-permute-start.13 = (bf16[1552,128]{1,0:T(8,128)(2,1)S(1)}, bf16[1552,128]{1,0:T(8,128)(2,1)S(1)}, u32[]{:S(2)}, u32[]{:S(2)}) collective-permute-start(bf16[1552,128]{1,0:T(8,128)(2,1)S(1)} %get-tuple-element.37.refs_7_), channel_id=1, source_target_pairs={{0,4},{4,0},{8,12},{12,8},{16,20},{20,16},{24,28},{28,24},{1,5},{5... | collective-permute-start | bytes 1191944 | tf_op jit(solution)/shard_map/ppermute | solution.py:20
  21.6 1.8 %collective-permute-start.8 = (bf16[1024,128]{1,0:T(8,128)(2,1)S(1)}, bf16[1024,128]{1,0:T(8,128)(2,1)S(1)}, u32[]{:S(2)}, u32[]{:S(2)}) collective-permute-start(bf16[1024,128]{1,0:T(8,128)(2,1)S(1)} %get-tuple-element.39), channel_id=1, source_target_pairs={{0,1},{1,0},{2,3},{3,2},{4,5},{5,4},{6,7},{7,6},{8,9},{9,8},{10,11... | collective-permute-start | bytes 786440 | tf_op jit(solution)/shard_map/ppermute | solution.py:20
  21.7 1.6 %collective-permute-start.9 = (bf16[128,128]{1,0:T(8,128)(2,1)S(1)}, bf16[128,128]{1,0:T(8,128)(2,1)S(1)}, u32[]{:S(2)}, u32[]{:S(2)}) collective-permute-start(bf16[128,128]{1,0:T(8,128)(2,1)S(1)} %get-tuple-element.40.refs_6_), channel_id=1, source_target_pairs={{0,1},{1,0},{2,3},{3,2},{4,5},{5,4},{6,7},{7,6},{8,9},{9,8},{10,11... | collective-permute-start | bytes 98312 | tf_op jit(solution)/shard_map/ppermute | solution.py:20
  22.2 3.3 %collective-permute-start.10 = (bf16[1024,128]{1,0:T(8,128)(2,1)S(1)}, bf16[1024,128]{1,0:T(8,128)(2,1)S(1)}, u32[]{:S(2)}, u32[]{:S(2)}) collective-permute-start(bf16[1024,128]{1,0:T(8,128)(2,1)S(1)} %get-tuple-element.41), channel_id=1, source_target_pairs={{0,1},{1,0},{2,3},{3,2},{4,5},{5,4},{6,7},{7,6},{8,9},{9,8},{10,11... | collective-permute-start | bytes 786440 | tf_op jit(solution)/shard_map/ppermute | solution.py:20
  22.3 3.2 %collective-permute-start.11 = (bf16[1024,128]{1,0:T(8,128)(2,1)S(1)}, bf16[1024,128]{1,0:T(8,128)(2,1)S(1)}, u32[]{:S(2)}, u32[]{:S(2)}) collective-permute-start(bf16[1024,128]{1,0:T(8,128)(2,1)S(1)} %get-tuple-element.42), channel_id=1, source_target_pairs={{0,1},{1,0},{2,3},{3,2},{4,5},{5,4},{6,7},{7,6},{8,9},{9,8},{10,11... | collective-permute-start | bytes 786440 | tf_op jit(solution)/shard_map/ppermute | solution.py:20
  23.2 2.2 %collective-permute-start.12 = (bf16[1024,128]{1,0:T(8,128)(2,1)S(1)}, bf16[1024,128]{1,0:T(8,128)(2,1)S(1)}, u32[]{:S(2)}, u32[]{:S(2)}) collective-permute-start(bf16[1024,128]{1,0:T(8,128)(2,1)S(1)} %get-tuple-element.43), channel_id=1, source_target_pairs={{0,1},{1,0},{2,3},{3,2},{4,5},{5,4},{6,7},{7,6},{8,9},{9,8},{10,11... | collective-permute-start | bytes 786440 | tf_op jit(solution)/shard_map/ppermute | solution.py:20
  23.4 7.3 %collective-permute-start.6 = (bf16[528,128]{1,0:T(8,128)(2,1)S(1)}, bf16[528,128]{1,0:T(8,128)(2,1)S(1)}, u32[]{:S(2)}, u32[]{:S(2)}) collective-permute-start(bf16[528,128]{1,0:T(8,128)(2,1)S(1)} %get-tuple-element.36), channel_id=1, source_target_pairs={{0,4},{4,0},{8,12},{12,8},{16,20},{20,16},{24,28},{28,24},{1,5},{5... | collective-permute-start | bytes 405512 | tf_op jit(solution)/shard_map/ppermute | solution.py:20

commit v5 on v4

--- a/solution.py
+++ b/solution.py
@@ -20,6 +20,13 @@
     return lax.ppermute(value, axis, pairs)
 
 
+def crossed_over(value):
+    subs = lax.axis_size("sub")
+    count = lax.axis_size("blk") * subs
+    pairs = [(at, (at // subs ^ 1) * subs + (at % subs ^ 1)) for at in range(count)]
+    return lax.ppermute(value, ("blk", "sub"), pairs)
+
+
 def in_vmem(value):
     return pltpu.with_memory_space_constraint(value, pltpu.VMEM)
 
@@ -37,8 +44,11 @@
 def tile_at(phase, piece, partner):
     blk_bit = lax.axis_index("blk") & 1
     sub_bit = lax.axis_index("sub") & 1
-    row_bit = blk_bit if phase == 1 else 1 - blk_bit
-    return 4 * piece + 2 * row_bit + (1 - sub_bit if partner else sub_bit)
+    if phase == 0:
+        blk_bit = 1 - blk_bit
+    if partner == (phase == 1):
+        sub_bit = 1 - sub_bit
+    return 4 * piece + 2 * blk_bit + sub_bit
 
 
 def start(source, target, sem):
@@ -332,13 +342,13 @@
     first = work.run(leaving=send[:1])
     work.run(keys=send[:1], leaving=send[1:2], after=first[:1])
     parcels = work.run(merges=send[:1])
-    arrived = [swapped(parcels[0], "blk")]
+    arrived = [crossed_over(parcels[0])]
     work.run(keys=send[1:], leaving=send[2:], apart=[1] * (quarter - 2), after=parcels)
     parcels = work.run(merges=send[1:2])
-    arrived.append(swapped(parcels[0], "blk"))
+    arrived.append(crossed_over(parcels[0]))
     cut = (quarter - 3) * depth + slots // 2 * width
     parcels = work.run(merges=send[2:], after=parcels + arrived[:1], cuts=[cut])
-    arrived += [swapped(parcel, "blk") for parcel in parcels]
+    arrived += [crossed_over(parcel) for parcel in parcels]
     last = work.run(
         keys=keep, leaving=keep, apart=[1] * quarter, after=parcels[:1] + arrived[1:2]
     )

time: 31.7 us -> 31.3 us (0.987)
  waiting for transfers between devices: 9.29 us -> 8.66 us
    ppermute x14 -> x10, waiting for transfers between devices: 9.29 us -> 1.69 us  [swapped(): return lax.ppermute(value, axis, pairs)]
    ppermute x0 -> x4, waiting for transfers between devices: none -> 6.97 us  [crossed_over(): return lax.ppermute(value, ('blk', 'sub'), pairs)]
    ppermute x0 -> x4, starting transfers between devices: none -> 6.46 us  [crossed_over(): return lax.ppermute(value, ('blk', 'sub'), pairs)]
    ppermute x14 -> x10, starting transfers between devices: 9.78 us -> 3.59 us  [swapped(): return lax.ppermute(value, axis, pairs)]
where the time goes in v5:
time: 31.3 us; the launch traced here: 31 us
  Pallas kernels  11.6 us (37%)
  starting transfers between devices  10 us (32%)
  waiting for transfers between devices  8.66 us (28%)
  between operations  0.74 us (2%)
    pallas_call x8, Pallas kernels, run(): pl.pallas_call(lambda *refs: work_kernel(plan, refs), out_shape=shapes, i...  8.27 us
    ppermute x4, waiting for transfers between devices, crossed_over(): return lax.ppermute(value, ('blk', 'sub'), pairs)  6.97 us
    ppermute x4, starting transfers between devices, crossed_over(): return lax.ppermute(value, ('blk', 'sub'), pairs)  6.46 us
    ppermute x10, starting transfers between devices, swapped(): return lax.ppermute(value, axis, pairs)  3.59 us
    pallas_call x4, Pallas kernels, added(): pl.pallas_call(functools.partial(add_kernel, begin, depth, rows), out_sha...  3.33 us
    ppermute x10, waiting for transfers between devices, swapped(): return lax.ppermute(value, axis, pairs)  1.69 us
  transfers between devices with their start and end apart: 14, of which 5 were waited for; matrix products, arithmetic and copies ran while one was open for 0% of the time, Pallas kernels for 31%

profile of v5, /device:TPU:0, one launch (start us, length us, event | category | flops | bytes accessed | tf_op | source)
XLA Modules:
  0.0 31.0 jit_solution(5611462858606366127)
XLA Ops:
  0.6 1.1 %work.8 = (bf16[1056,128]{1,0:T(8,128)(2,1)S(1)}, s32[256,128]{1,0:T(8,128)S(1)}, s32[128,128]{1,0:T(8,128)S(1)}) custom-call(bf16[16,1024,128]{2,1,0:T(8,128)(2,1)} %bitcast.3, bf16[16,2048]{1,0:T(8,128)(2,1)} %refs_1_.7, s32[8,16]{1,0:T(8,128)} %bitcast.8, s32[256,128]{1,0:T(8,128)} %refs_3_.7, s32[128,128]{1,0:T(8,128)} %refs_4_.7), custom_call_target="tpu_custom_call" | custom-call | flops 1 | bytes 1 | tf_op jit(solution)/shard_map/work/pallas_call | solution.py:260
  1.7 0.5 %collective-permute-start = (bf16[1056,128]{1,0:T(8,128)(2,1)S(1)}, bf16[1056,128]{1,0:T(8,128)(2,1)S(1)}, u32[]{:S(2)}, u32[]{:S(2)}) collective-permute-start(bf16[1056,128]{1,0:T(8,128)(2,1)S(1)} %get-tuple-element.29.refs_7_), channel_id=1, source_target_pairs={{0,1},{1,0},{2,3},{3,2},{4,5},{5,4},{6,7},{7,6},{8,9},{9,8},{10,11... | collective-permute-start | bytes 811016 | tf_op jit(solution)/shard_map/ppermute | solution.py:20
  2.3 1.1 %work.9 = (bf16[1056,128]{1,0:T(8,128)(2,1)S(1)}, bf16[1056,128]{1,0:T(8,128)(2,1)S(1)}) custom-call(bf16[16,1024,128]{2,1,0:T(8,128)(2,1)} %bitcast.4, bf16[16,2048]{1,0:T(8,128)(2,1)} %refs_1_.7, s32[8,16]{1,0:T(8,128)} %bitcast.9, s32[256,128]{1,0:T(8,128)} %refs_3_.7, s32[128,128]{1,0:T(8,128)} %refs_4_.7, s32[256,128]{1,0:T(8,128)S(1)} %get-tuple-element.27.refs_5_, ...), custom_call_target="tpu_custom_call" | custom-call | flops 1 | bytes 1 | tf_op jit(solution)/shard_map/work/pallas_call | solution.py:260
  3.4 0.1 collective-permute-start.4
  3.5 0.0 collective-permute-done.refs_1_
  3.5 0.4 %work.10.refs_7_ = bf16[1040,128]{1,0:T(8,128)(2,1)S(1)} custom-call(bf16[1056,128]{1,0:T(8,128)(2,1)S(1)} %get-tuple-element.30.refs_0_, bf16[1056,128]{1,0:T(8,128)(2,1)S(1)} %collective-permute-done.refs_1_), custom_call_target="tpu_custom_call" | custom-call | flops 1 | bytes 1 | tf_op jit(solution)/shard_map/work/pallas_call | solution.py:260
  3.9 2.6 %collective-permute-start.5 = (bf16[1040,128]{1,0:T(8,128)(2,1)S(1)}, bf16[1040,128]{1,0:T(8,128)(2,1)S(1)}, u32[]{:S(2)}, u32[]{:S(2)}) collective-permute-start(bf16[1040,128]{1,0:T(8,128)(2,1)S(1)} %work.10.refs_7_), channel_id=1, source_target_pairs={{0,5},{1,4},{2,7},{3,6},{4,1},{5,0},{6,3},{7,2},{8,13},{9,12},{10,... | collective-permute-start | bytes 798728 | tf_op jit(solution)/shard_map/ppermute | solution.py:27
  6.6 1.4 %work.11 = (bf16[64,128]{1,0:T(8,128)(2,1)S(1)}, bf16[1024,128]{1,0:T(8,128)(2,1)S(1)}, bf16[1024,128]{1,0:T(8,128)(2,1)S(1)}, bf16[3168,128]{1,0:T(8,128)(2,1)S(1)}) custom-call(bf16[16,1024,128]{2,1,0:T(8,128)(2,1)} %bitcast.5, bf16[16,2048]{1,0:T(8,128)(2,1)} %refs_1_.7, s32[8,16]{1,0:T(8,128)} %bitcast.10, s32[256,128]{1,0:T(8,128)} %refs_3_.7, ...), custom_call_target="tpu_custom_call" | custom-call | flops 1 | bytes 1 | tf_op jit(solution)/shard_map/work/pallas_call | solution.py:260
  8.0 0.0 collective-permute-done.4.refs_1_
  8.0 0.4 %work.12.refs_4_ = bf16[1040,128]{1,0:T(8,128)(2,1)S(1)} custom-call(bf16[3168,128]{1,0:T(8,128)(2,1)S(1)} %get-tuple-element.31.refs_0_, bf16[1056,128]{1,0:T(8,128)(2,1)S(1)} %collective-permute-done.4.refs_1_), custom_call_target="tpu_custom_call" | custom-call | flops 1 | bytes 1 | tf_op jit(solution)/shard_map/work/pallas_call | solution.py:260
  8.5 0.1 collective-permute-start.7
  8.6 0.5 %collective-permute-start.1 = (bf16[1024,128]{1,0:T(8,128)(2,1)S(1)}, bf16[1024,128]{1,0:T(8,128)(2,1)S(1)}, u32[]{:S(2)}, u32[]{:S(2)}) collective-permute-start(bf16[1024,128]{1,0:T(8,128)(2,1)S(1)} %get-tuple-element.32), channel_id=1, source_target_pairs={{0,1},{1,0},{2,3},{3,2},{4,5},{5,4},{6,7},{7,6},{8,9},{9,8},{10,11... | collective-permute-start | bytes 786440 | tf_op jit(solution)/shard_map/ppermute | solution.py:20
  9.1 0.1 collective-permute-start.3
  9.2 0.4 %collective-permute-start.2 = (bf16[64,128]{1,0:T(8,128)(2,1)S(1)}, bf16[64,128]{1,0:T(8,128)(2,1)S(1)}, u32[]{:S(2)}, u32[]{:S(2)}) collective-permute-start(bf16[64,128]{1,0:T(8,128)(2,1)S(1)} %get-tuple-element.33), channel_id=1, source_target_pairs={{0,1},{1,0},{2,3},{3,2},{4,5},{5,4},{6,7},{7,6},{8,9},{9,8},{10,11... | collective-permute-start | bytes 49160 | tf_op jit(solution)/shard_map/ppermute | solution.py:20
  9.6 1.0 %collective-permute-done.2.refs_2_ = bf16[64,128]{1,0:T(8,128)(2,1)S(1)} collective-permute-done((bf16[64,128]{1,0:T(8,128)(2,1)S(1)}, bf16[64,128]{1,0:T(8,128)(2,1)S(1)}, u32[]{:S(2)}, u32[]{:S(2)}) %collective-permute-start.2) | collective-permute-done | bytes 16416 | tf_op jit(solution)/shard_map/ppermute | solution.py:20
  10.7 0.0 collective-permute-done.1.refs_1_
  10.7 0.0 collective-permute-done.3.refs_3_
  10.7 2.7 %collective-permute-done.5.refs_5_.arrived = bf16[1040,128]{1,0:T(8,128)(2,1)S(1)} collective-permute-done((bf16[1040,128]{1,0:T(8,128)(2,1)S(1)}, bf16[1040,128]{1,0:T(8,128)(2,1)S(1)}, u32[]{:S(2)}, u32[]{:S(2)}) %collective-permute-start.5) | collective-permute-done | bytes 266272 | tf_op jit(solution)/shard_map/ppermute | solution.py:27
  13.4 0.7 %work.13 = (bf16[1552,128]{1,0:T(8,128)(2,1)S(1)}, bf16[528,128]{1,0:T(8,128)(2,1)S(1)}) custom-call(bf16[3168,128]{1,0:T(8,128)(2,1)S(1)} %get-tuple-element.31.refs_0_, bf16[1024,128]{1,0:T(8,128)(2,1)S(1)} %collective-permute-done.1.refs_1_, bf16[64,128]{1,0:T(8,128)(2,1)S(1)} %collective-permute-done.2.refs_2_, ...), custom_call_target="tpu_custom_call" | custom-call | flops 1 | bytes 1 | tf_op jit(solution)/shard_map/work/pallas_call | solution.py:260
  14.1 2.3 %collective-permute-start.13 = (bf16[1552,128]{1,0:T(8,128)(2,1)S(1)}, bf16[1552,128]{1,0:T(8,128)(2,1)S(1)}, u32[]{:S(2)}, u32[]{:S(2)}) collective-permute-start(bf16[1552,128]{1,0:T(8,128)(2,1)S(1)} %get-tuple-element.37.refs_7_), channel_id=1, source_target_pairs={{0,5},{1,4},{2,7},{3,6},{4,1},{5,0},{6,3},{7,2},{8,13},{9,12},{10,... | collective-permute-start | bytes 1191944 | tf_op jit(solution)/shard_map/ppermute | solution.py:27
  16.4 2.7 %collective-permute-done.7.refs_8_.arrived = bf16[1040,128]{1,0:T(8,128)(2,1)S(1)} collective-permute-done((bf16[1040,128]{1,0:T(8,128)(2,1)S(1)}, bf16[1040,128]{1,0:T(8,128)(2,1)S(1)}, u32[]{:S(2)}, u32[]{:S(2)}) %collective-permute-start.7) | collective-permute-done | bytes 266272 | tf_op jit(solution)/shard_map/ppermute | solution.py:27
  19.1 1.7 %work.14 = (bf16[128,128]{1,0:T(8,128)(2,1)S(1)}, bf16[1024,128]{1,0:T(8,128)(2,1)S(1)}, bf16[1024,128]{1,0:T(8,128)(2,1)S(1)}, bf16[1024,128]{1,0:T(8,128)(2,1)...) custom-call(bf16[16,1024,128]{2,1,0:T(8,128)(2,1)} %bitcast.6, bf16[16,2048]{1,0:T(8,128)(2,1)} %refs_1_.7, ...), custom_call_target="tpu_custom_call" | custom-call | flops 1 | bytes 1 | tf_op jit(solution)/shard_map/work/pallas_call | solution.py:260
  20.8 1.0 %collective-permute-start.8 = (bf16[1024,128]{1,0:T(8,128)(2,1)S(1)}, bf16[1024,128]{1,0:T(8,128)(2,1)S(1)}, u32[]{:S(2)}, u32[]{:S(2)}) collective-permute-start(bf16[1024,128]{1,0:T(8,128)(2,1)S(1)} %get-tuple-element.39), channel_id=1, source_target_pairs={{0,1},{1,0},{2,3},{3,2},{4,5},{5,4},{6,7},{7,6},{8,9},{9,8},{10,11... | collective-permute-start | bytes 786440 | tf_op jit(solution)/shard_map/ppermute | solution.py:20
  21.8 0.1 collective-permute-start.9
  21.9 0.4 %collective-permute-start.10 = (bf16[1024,128]{1,0:T(8,128)(2,1)S(1)}, bf16[1024,128]{1,0:T(8,128)(2,1)S(1)}, u32[]{:S(2)}, u32[]{:S(2)}) collective-permute-start(bf16[1024,128]{1,0:T(8,128)(2,1)S(1)} %get-tuple-element.41), channel_id=1, source_target_pairs={{0,1},{1,0},{2,3},{3,2},{4,5},{5,4},{6,7},{7,6},{8,9},{9,8},{10,11... | collective-permute-start | bytes 786440 | tf_op jit(solution)/shard_map/ppermute | solution.py:20
  22.3 0.1 collective-permute-start.11
  22.4 0.6 %collective-permute-done.9.refs_2_ = bf16[128,128]{1,0:T(8,128)(2,1)S(1)} collective-permute-done((bf16[128,128]{1,0:T(8,128)(2,1)S(1)}, bf16[128,128]{1,0:T(8,128)(2,1)S(1)}, u32[]{:S(2)}, u32[]{:S(2)}) %collective-permute-start.9) | collective-permute-done | bytes 32800 | tf_op jit(solution)/shard_map/ppermute | solution.py:20
  23.0 0.4 %collective-permute-start.12 = (bf16[1024,128]{1,0:T(8,128)(2,1)S(1)}, bf16[1024,128]{1,0:T(8,128)(2,1)S(1)}, u32[]{:S(2)}, u32[]{:S(2)}) collective-permute-start(bf16[1024,128]{1,0:T(8,128)(2,1)S(1)} %get-tuple-element.43), channel_id=1, source_target_pairs={{0,1},{1,0},{2,3},{3,2},{4,5},{5,4},{6,7},{7,6},{8,9},{9,8},{10,11... | collective-permute-start | bytes 786440 | tf_op jit(solution)/shard_map/ppermute | solution.py:20
  23.4 0.0 collective-permute-done.8.refs_1_
  23.4 1.4 %collective-permute-start.6 = (bf16[528,128]{1,0:T(8,128)(2,1)S(1)}, bf16[528,128]{1,0:T(8,128)(2,1)S(1)}, u32[]{:S(2)}, u32[]{:S(2)}) collective-permute-start(bf16[528,128]{1,0:T(8,128)(2,1)S(1)} %get-tuple-element.36), channel_id=1, source_target_pairs={{0,5},{1,4},{2,7},{3,6},{4,1},{5,0},{6,3},{7,2},{8,13},{9,12},{10,... | collective-permute-start | bytes 405512 | tf_op jit(solution)/shard_map/ppermute | solution.py:27
  24.8 0.0 collective-permute-done.10.refs_3_
  24.8 0.0 collective-permute-done.11.refs_4_
  24.8 0.0 collective-permute-done.12.refs_5_
  24.8 1.3 %work.15.kept = bf16[4160,128]{1,0:T(8,128)(2,1)S(1)} custom-call(bf16[4224,128]{1,0:T(8,128)(2,1)S(1)} %get-tuple-element.38.refs_0_, bf16[1024,128]{1,0:T(8,128)(2,1)S(1)} %collective-permute-done.8.refs_1_, bf16[128,128]{1,0:T(8,128)(2,1)S(1)} %collective-permute-done.9.refs_2_, bf16[1024,128]{1,0:T(8,128)(2,1)S(1)} %collective-permute-done.10.refs_3_, ...), custom_call_target="tpu_custom_call" | custom-call | flops 1 | bytes 1 | tf_op jit(solution)/shard_map/work/pallas_call | solution.py:260
  26.1 0.8 %add.4 = (bf16[4,1024,128]{2,1,0:T(8,128)(2,1)}, bf16[16,512]{1,0:T(8,128)(2,1)}) custom-call(bf16[1040,128]{1,0:T(8,128)(2,1)S(1)} %collective-permute-done.5.refs_5_.arrived, bf16[4160,128]{1,0:T(8,128)(2,1)S(1)} %work.15.kept), custom_call_target="tpu_custom_call" | custom-call | flops 1 | bytes 1 | tf_op jit(solution)/shard_map/add/pallas_call | solution.py:314
  27.0 0.8 %add.5 = (bf16[4,1024,128]{2,1,0:T(8,128)(2,1)}, bf16[16,512]{1,0:T(8,128)(2,1)}) custom-call(bf16[1040,128]{1,0:T(8,128)(2,1)S(1)} %collective-permute-done.7.refs_8_.arrived, bf16[4160,128]{1,0:T(8,128)(2,1)S(1)} %work.15.kept, bf16[4,1024,128]{2,1,0:T(8,128)(2,1)} %get-tuple-element.44.rest_0_, ...), custom_call_target="tpu_custom_call", output_to_operand_aliasing={{0}: (2, {}), {1}: (3, {})} | custom-call | flops 1 | bytes 1 | tf_op jit(solution)/shard_map/add/pallas_call | solution.py:314
  27.8 0.0 collective-permute-done.13.arrived
  27.8 0.9 %add.6 = (bf16[4,1024,128]{2,1,0:T(8,128)(2,1)}, bf16[16,512]{1,0:T(8,128)(2,1)}) custom-call(bf16[1552,128]{1,0:T(8,128)(2,1)S(1)} %collective-permute-done.13.arrived, bf16[4160,128]{1,0:T(8,128)(2,1)S(1)} %work.15.kept, bf16[4,1024,128]{2,1,0:T(8,128)(2,1)} %get-tuple-element.46.rest_0_, ...), custom_call_target="tpu_custom_call", output_to_operand_aliasing={{0}: (2, {}), {1}: (3, {})} | custom-call | flops 1 | bytes 1 | tf_op jit(solution)/shard_map/add/pallas_call | solution.py:314
  28.7 1.6 %collective-permute-done.6.arrived = bf16[528,128]{1,0:T(8,128)(2,1)S(1)} collective-permute-done((bf16[528,128]{1,0:T(8,128)(2,1)S(1)}, bf16[528,128]{1,0:T(8,128)(2,1)S(1)}, u32[]{:S(2)}, u32[]{:S(2)}) %collective-permute-start.6) | collective-permute-done | bytes 135200 | tf_op jit(solution)/shard_map/ppermute | solution.py:27
  30.3 0.8 %add.7 = (bf16[4,1024,128]{2,1,0:T(8,128)(2,1)}, bf16[16,512]{1,0:T(8,128)(2,1)}) custom-call(bf16[528,128]{1,0:T(8,128)(2,1)S(1)} %collective-permute-done.6.arrived, bf16[4160,128]{1,0:T(8,128)(2,1)S(1)} %work.15.kept, bf16[4,1024,128]{2,1,0:T(8,128)(2,1)} %get-tuple-element.48.rest_0_, ...), custom_call_target="tpu_custom_call", output_to_operand_aliasing={{0}: (2, {}), {1}: (3, {})} | custom-call | flops 1 | bytes 1 | tf_op jit(solution)/shard_map/add/pallas_call | solution.py:314
Async XLA Ops:
  1.7 1.8 %collective-permute-start = (bf16[1056,128]{1,0:T(8,128)(2,1)S(1)}, bf16[1056,128]{1,0:T(8,128)(2,1)S(1)}, u32[]{:S(2)}, u32[]{:S(2)}) collective-permute-start(bf16[1056,128]{1,0:T(8,128)(2,1)S(1)} %get-tuple-element.29.refs_7_), channel_id=1, source_target_pairs={{0,1},{1,0},{2,3},{3,2},{4,5},{5,4},{6,7},{7,6},{8,9},{9,8},{10,11... | collective-permute-start | bytes 811016 | tf_op jit(solution)/shard_map/ppermute | solution.py:20
  3.4 4.7 %collective-permute-start.4 = (bf16[1056,128]{1,0:T(8,128)(2,1)S(1)}, bf16[1056,128]{1,0:T(8,128)(2,1)S(1)}, u32[]{:S(2)}, u32[]{:S(2)}) collective-permute-start(bf16[1056,128]{1,0:T(8,128)(2,1)S(1)} %get-tuple-element.35), channel_id=1, source_target_pairs={{0,1},{1,0},{2,3},{3,2},{4,5},{5,4},{6,7},{7,6},{8,9},{9,8},{10,11... | collective-permute-start | bytes 811016 | tf_op jit(solution)/shard_map/ppermute | solution.py:20
  3.9 9.4 %collective-permute-start.5 = (bf16[1040,128]{1,0:T(8,128)(2,1)S(1)}, bf16[1040,128]{1,0:T(8,128)(2,1)S(1)}, u32[]{:S(2)}, u32[]{:S(2)}) collective-permute-start(bf16[1040,128]{1,0:T(8,128)(2,1)S(1)} %work.10.refs_7_), channel_id=1, source_target_pairs={{0,5},{1,4},{2,7},{3,6},{4,1},{5,0},{6,3},{7,2},{8,13},{9,12},{10,... | collective-permute-start | bytes 798728 | tf_op jit(solution)/shard_map/ppermute | solution.py:27
  8.5 10.6 %collective-permute-start.7 = (bf16[1040,128]{1,0:T(8,128)(2,1)S(1)}, bf16[1040,128]{1,0:T(8,128)(2,1)S(1)}, u32[]{:S(2)}, u32[]{:S(2)}) collective-permute-start(bf16[1040,128]{1,0:T(8,128)(2,1)S(1)} %work.12.refs_4_), channel_id=1, source_target_pairs={{0,5},{1,4},{2,7},{3,6},{4,1},{5,0},{6,3},{7,2},{8,13},{9,12},{10,... | collective-permute-start | bytes 798728 | tf_op jit(solution)/shard_map/ppermute | solution.py:27
  8.6 2.1 %collective-permute-start.1 = (bf16[1024,128]{1,0:T(8,128)(2,1)S(1)}, bf16[1024,128]{1,0:T(8,128)(2,1)S(1)}, u32[]{:S(2)}, u32[]{:S(2)}) collective-permute-start(bf16[1024,128]{1,0:T(8,128)(2,1)S(1)} %get-tuple-element.32), channel_id=1, source_target_pairs={{0,1},{1,0},{2,3},{3,2},{4,5},{5,4},{6,7},{7,6},{8,9},{9,8},{10,11... | collective-permute-start | bytes 786440 | tf_op jit(solution)/shard_map/ppermute | solution.py:20
  9.1 1.6 %collective-permute-start.3 = (bf16[1024,128]{1,0:T(8,128)(2,1)S(1)}, bf16[1024,128]{1,0:T(8,128)(2,1)S(1)}, u32[]{:S(2)}, u32[]{:S(2)}) collective-permute-start(bf16[1024,128]{1,0:T(8,128)(2,1)S(1)} %get-tuple-element.34), channel_id=1, source_target_pairs={{0,1},{1,0},{2,3},{3,2},{4,5},{5,4},{6,7},{7,6},{8,9},{9,8},{10,11... | collective-permute-start | bytes 786440 | tf_op jit(solution)/shard_map/ppermute | solution.py:20
  9.2 1.5 %collective-permute-start.2 = (bf16[64,128]{1,0:T(8,128)(2,1)S(1)}, bf16[64,128]{1,0:T(8,128)(2,1)S(1)}, u32[]{:S(2)}, u32[]{:S(2)}) collective-permute-start(bf16[64,128]{1,0:T(8,128)(2,1)S(1)} %get-tuple-element.33), channel_id=1, source_target_pairs={{0,1},{1,0},{2,3},{3,2},{4,5},{5,4},{6,7},{7,6},{8,9},{9,8},{10,11... | collective-permute-start | bytes 49160 | tf_op jit(solution)/shard_map/ppermute | solution.py:20
  14.1 13.7 %collective-permute-start.13 = (bf16[1552,128]{1,0:T(8,128)(2,1)S(1)}, bf16[1552,128]{1,0:T(8,128)(2,1)S(1)}, u32[]{:S(2)}, u32[]{:S(2)}) collective-permute-start(bf16[1552,128]{1,0:T(8,128)(2,1)S(1)} %get-tuple-element.37.refs_7_), channel_id=1, source_target_pairs={{0,5},{1,4},{2,7},{3,6},{4,1},{5,0},{6,3},{7,2},{8,13},{9,12},{10,... | collective-permute-start | bytes 1191944 | tf_op jit(solution)/shard_map/ppermute | solution.py:27
  20.8 2.5 %collective-permute-start.8 = (bf16[1024,128]{1,0:T(8,128)(2,1)S(1)}, bf16[1024,128]{1,0:T(8,128)(2,1)S(1)}, u32[]{:S(2)}, u32[]{:S(2)}) collective-permute-start(bf16[1024,128]{1,0:T(8,128)(2,1)S(1)} %get-tuple-element.39), channel_id=1, source_target_pairs={{0,1},{1,0},{2,3},{3,2},{4,5},{5,4},{6,7},{7,6},{8,9},{9,8},{10,11... | collective-permute-start | bytes 786440 | tf_op jit(solution)/shard_map/ppermute | solution.py:20
  21.8 1.2 %collective-permute-start.9 = (bf16[128,128]{1,0:T(8,128)(2,1)S(1)}, bf16[128,128]{1,0:T(8,128)(2,1)S(1)}, u32[]{:S(2)}, u32[]{:S(2)}) collective-permute-start(bf16[128,128]{1,0:T(8,128)(2,1)S(1)} %get-tuple-element.40.refs_6_), channel_id=1, source_target_pairs={{0,1},{1,0},{2,3},{3,2},{4,5},{5,4},{6,7},{7,6},{8,9},{9,8},{10,11... | collective-permute-start | bytes 98312 | tf_op jit(solution)/shard_map/ppermute | solution.py:20
  21.9 3.0 %collective-permute-start.10 = (bf16[1024,128]{1,0:T(8,128)(2,1)S(1)}, bf16[1024,128]{1,0:T(8,128)(2,1)S(1)}, u32[]{:S(2)}, u32[]{:S(2)}) collective-permute-start(bf16[1024,128]{1,0:T(8,128)(2,1)S(1)} %get-tuple-element.41), channel_id=1, source_target_pairs={{0,1},{1,0},{2,3},{3,2},{4,5},{5,4},{6,7},{7,6},{8,9},{9,8},{10,11... | collective-permute-start | bytes 786440 | tf_op jit(solution)/shard_map/ppermute | solution.py:20
  22.3 2.5 %collective-permute-start.11 = (bf16[1024,128]{1,0:T(8,128)(2,1)S(1)}, bf16[1024,128]{1,0:T(8,128)(2,1)S(1)}, u32[]{:S(2)}, u32[]{:S(2)}) collective-permute-start(bf16[1024,128]{1,0:T(8,128)(2,1)S(1)} %get-tuple-element.42), channel_id=1, source_target_pairs={{0,1},{1,0},{2,3},{3,2},{4,5},{5,4},{6,7},{7,6},{8,9},{9,8},{10,11... | collective-permute-start | bytes 786440 | tf_op jit(solution)/shard_map/ppermute | solution.py:20
  23.0 1.8 %collective-permute-start.12 = (bf16[1024,128]{1,0:T(8,128)(2,1)S(1)}, bf16[1024,128]{1,0:T(8,128)(2,1)S(1)}, u32[]{:S(2)}, u32[]{:S(2)}) collective-permute-start(bf16[1024,128]{1,0:T(8,128)(2,1)S(1)} %get-tuple-element.43), channel_id=1, source_target_pairs={{0,1},{1,0},{2,3},{3,2},{4,5},{5,4},{6,7},{7,6},{8,9},{9,8},{10,11... | collective-permute-start | bytes 786440 | tf_op jit(solution)/shard_map/ppermute | solution.py:20
  23.4 6.9 %collective-permute-start.6 = (bf16[528,128]{1,0:T(8,128)(2,1)S(1)}, bf16[528,128]{1,0:T(8,128)(2,1)S(1)}, u32[]{:S(2)}, u32[]{:S(2)}) collective-permute-start(bf16[528,128]{1,0:T(8,128)(2,1)S(1)} %get-tuple-element.36), channel_id=1, source_target_pairs={{0,5},{1,4},{2,7},{3,6},{4,1},{5,0},{6,3},{7,2},{8,13},{9,12},{10,... | collective-permute-start | bytes 405512 | tf_op jit(solution)/shard_map/ppermute | solution.py:27

commit v6 on v5

--- a/solution.py
+++ b/solution.py
@@ -339,8 +339,8 @@
     keep = [(1, piece) for piece in range(quarter)]
     rows = slots * width
     depth = rows + feat_count
-    first = work.run(leaving=send[:1])
-    work.run(keys=send[:1], leaving=send[1:2], after=first[:1])
+    first = work.run(leaving=send[:2])
+    work.run(keys=send[:1], after=first[:1])
     parcels = work.run(merges=send[:1])
     arrived = [crossed_over(parcels[0])]
     work.run(keys=send[1:], leaving=send[2:], apart=[1] * (quarter - 2), after=parcels)

time: 31.3 us -> 31.3 us (level)
  transfers between devices with their start and end apart: 14 -> 14, of which waited for: 5 -> 6; matrix products, arithmetic and copies ran while one was open for 0% -> 0% of each run, Pallas kernels for 31% -> 31%
where the time goes in v6:
time: 31.3 us; the launch traced here: 31 us
  Pallas kernels  11.6 us (37%)
  starting transfers between devices  9.92 us (32%)
  waiting for transfers between devices  8.75 us (28%)
  between operations  0.74 us (2%)
    pallas_call x8, Pallas kernels, run(): pl.pallas_call(lambda *refs: work_kernel(plan, refs), out_shape=shapes, i...  8.27 us
    ppermute x4, waiting for transfers between devices, crossed_over(): return lax.ppermute(value, ('blk', 'sub'), pairs)  6.97 us
    ppermute x4, starting transfers between devices, crossed_over(): return lax.ppermute(value, ('blk', 'sub'), pairs)  6.6 us
    pallas_call x4, Pallas kernels, added(): pl.pallas_call(functools.partial(add_kernel, begin, depth, rows), out_sha...  3.33 us
    ppermute x10, starting transfers between devices, swapped(): return lax.ppermute(value, axis, pairs)  3.32 us
    ppermute x10, waiting for transfers between devices, swapped(): return lax.ppermute(value, axis, pairs)  1.78 us
  transfers between devices with their start and end apart: 14, of which 6 were waited for; matrix products, arithmetic and copies ran while one was open for 0% of the time, Pallas kernels for 31%

profile of v6, /device:TPU:0, one launch (start us, length us, event | category | flops | bytes accessed | tf_op | source)
XLA Modules:
  0.0 31.0 jit_solution(635827270606913482)
XLA Ops:
  0.6 1.2 %work.8 = (bf16[1056,128]{1,0:T(8,128)(2,1)S(1)}, bf16[1056,128]{1,0:T(8,128)(2,1)S(1)}, s32[256,128]{1,0:T(8,128)S(1)}, s32[128,128]{1,0:T(8,128)S(1)}) custom-call(bf16[16,1024,128]{2,1,0:T(8,128)(2,1)} %bitcast.3, bf16[16,2048]{1,0:T(8,128)(2,1)} %refs_1_.7, s32[8,16]{1,0:T(8,128)} %bitcast.8, s32[256,128]{1,0:T(8,128)} %refs_3_.7, s32[128,128]{1,0:T(8,128)} %refs_4_.7), custom_call_target="tpu_custom_call" | custom-call | flops 1 | bytes 1 | tf_op jit(solution)/shard_map/work/pallas_call | solution.py:260
  1.9 0.5 %collective-permute-start = (bf16[1056,128]{1,0:T(8,128)(2,1)S(1)}, bf16[1056,128]{1,0:T(8,128)(2,1)S(1)}, u32[]{:S(2)}, u32[]{:S(2)}) collective-permute-start(bf16[1056,128]{1,0:T(8,128)(2,1)S(1)} %get-tuple-element.28.refs_7_), channel_id=1, source_target_pairs={{0,1},{1,0},{2,3},{3,2},{4,5},{5,4},{6,7},{7,6},{8,9},{9,8},{10,11... | collective-permute-start | bytes 811016 | tf_op jit(solution)/shard_map/ppermute | solution.py:20
  2.4 0.1 collective-permute-start.4
  2.5 1.0 %work.9.refs_0_ = bf16[1056,128]{1,0:T(8,128)(2,1)S(1)} custom-call(bf16[16,1024,128]{2,1,0:T(8,128)(2,1)} %bitcast.4, bf16[16,2048]{1,0:T(8,128)(2,1)} %refs_1_.7, s32[8,16]{1,0:T(8,128)} %bitcast.9, s32[256,128]{1,0:T(8,128)} %refs_3_.7, s32[128,128]{1,0:T(8,128)} %refs_4_.7, s32[256,128]{1,0:T(8,128)S(1)} %get-tuple-element.26.refs_5_, ...), custom_call_target="tpu_custom_call" | custom-call | flops 1 | bytes 1 | tf_op jit(solution)/shard_map/work/pallas_call | solution.py:260
  3.5 0.1 collective-permute-done.refs_1_
  3.6 0.4 %work.10.refs_7_ = bf16[1040,128]{1,0:T(8,128)(2,1)S(1)} custom-call(bf16[1056,128]{1,0:T(8,128)(2,1)S(1)} %work.9.refs_0_, bf16[1056,128]{1,0:T(8,128)(2,1)S(1)} %collective-permute-done.refs_1_), custom_call_target="tpu_custom_call" | custom-call | flops 1 | bytes 1 | tf_op jit(solution)/shard_map/work/pallas_call | solution.py:260
  4.0 2.7 %collective-permute-start.5 = (bf16[1040,128]{1,0:T(8,128)(2,1)S(1)}, bf16[1040,128]{1,0:T(8,128)(2,1)S(1)}, u32[]{:S(2)}, u32[]{:S(2)}) collective-permute-start(bf16[1040,128]{1,0:T(8,128)(2,1)S(1)} %work.10.refs_7_), channel_id=1, source_target_pairs={{0,5},{1,4},{2,7},{3,6},{4,1},{5,0},{6,3},{7,2},{8,13},{9,12},{10,... | collective-permute-start | bytes 798728 | tf_op jit(solution)/shard_map/ppermute | solution.py:27
  6.7 1.4 %work.11 = (bf16[64,128]{1,0:T(8,128)(2,1)S(1)}, bf16[1024,128]{1,0:T(8,128)(2,1)S(1)}, bf16[1024,128]{1,0:T(8,128)(2,1)S(1)}, bf16[3168,128]{1,0:T(8,128)(2,1)S(1)}) custom-call(bf16[16,1024,128]{2,1,0:T(8,128)(2,1)} %bitcast.5, bf16[16,2048]{1,0:T(8,128)(2,1)} %refs_1_.7, s32[8,16]{1,0:T(8,128)} %bitcast.10, s32[256,128]{1,0:T(8,128)} %refs_3_.7, ...), custom_call_target="tpu_custom_call" | custom-call | flops 1 | bytes 1 | tf_op jit(solution)/shard_map/work/pallas_call | solution.py:260
  8.1 0.0 collective-permute-done.4.refs_1_
  8.1 0.4 %work.12.refs_4_ = bf16[1040,128]{1,0:T(8,128)(2,1)S(1)} custom-call(bf16[3168,128]{1,0:T(8,128)(2,1)S(1)} %get-tuple-element.29.refs_0_, bf16[1056,128]{1,0:T(8,128)(2,1)S(1)} %collective-permute-done.4.refs_1_), custom_call_target="tpu_custom_call" | custom-call | flops 1 | bytes 1 | tf_op jit(solution)/shard_map/work/pallas_call | solution.py:260
  8.5 0.1 collective-permute-start.7
  8.6 0.4 %collective-permute-start.1 = (bf16[1024,128]{1,0:T(8,128)(2,1)S(1)}, bf16[1024,128]{1,0:T(8,128)(2,1)S(1)}, u32[]{:S(2)}, u32[]{:S(2)}) collective-permute-start(bf16[1024,128]{1,0:T(8,128)(2,1)S(1)} %get-tuple-element.30), channel_id=1, source_target_pairs={{0,1},{1,0},{2,3},{3,2},{4,5},{5,4},{6,7},{7,6},{8,9},{9,8},{10,11... | collective-permute-start | bytes 786440 | tf_op jit(solution)/shard_map/ppermute | solution.py:20
  9.1 0.1 collective-permute-start.3
  9.2 0.4 %collective-permute-start.2 = (bf16[64,128]{1,0:T(8,128)(2,1)S(1)}, bf16[64,128]{1,0:T(8,128)(2,1)S(1)}, u32[]{:S(2)}, u32[]{:S(2)}) collective-permute-start(bf16[64,128]{1,0:T(8,128)(2,1)S(1)} %get-tuple-element.31), channel_id=1, source_target_pairs={{0,1},{1,0},{2,3},{3,2},{4,5},{5,4},{6,7},{7,6},{8,9},{9,8},{10,11... | collective-permute-start | bytes 49160 | tf_op jit(solution)/shard_map/ppermute | solution.py:20
  9.6 1.0 %collective-permute-done.2.refs_2_ = bf16[64,128]{1,0:T(8,128)(2,1)S(1)} collective-permute-done((bf16[64,128]{1,0:T(8,128)(2,1)S(1)}, bf16[64,128]{1,0:T(8,128)(2,1)S(1)}, u32[]{:S(2)}, u32[]{:S(2)}) %collective-permute-start.2) | collective-permute-done | bytes 16416 | tf_op jit(solution)/shard_map/ppermute | solution.py:20
  10.6 0.0 collective-permute-done.1.refs_1_
  10.6 0.0 collective-permute-done.3.refs_3_
  10.6 2.8 %collective-permute-done.5.refs_5_.arrived = bf16[1040,128]{1,0:T(8,128)(2,1)S(1)} collective-permute-done((bf16[1040,128]{1,0:T(8,128)(2,1)S(1)}, bf16[1040,128]{1,0:T(8,128)(2,1)S(1)}, u32[]{:S(2)}, u32[]{:S(2)}) %collective-permute-start.5) | collective-permute-done | bytes 266272 | tf_op jit(solution)/shard_map/ppermute | solution.py:27
  13.4 0.7 %work.13 = (bf16[1552,128]{1,0:T(8,128)(2,1)S(1)}, bf16[528,128]{1,0:T(8,128)(2,1)S(1)}) custom-call(bf16[3168,128]{1,0:T(8,128)(2,1)S(1)} %get-tuple-element.29.refs_0_, bf16[1024,128]{1,0:T(8,128)(2,1)S(1)} %collective-permute-done.1.refs_1_, bf16[64,128]{1,0:T(8,128)(2,1)S(1)} %collective-permute-done.2.refs_2_, ...), custom_call_target="tpu_custom_call" | custom-call | flops 1 | bytes 1 | tf_op jit(solution)/shard_map/work/pallas_call | solution.py:260
  14.2 2.3 %collective-permute-start.13 = (bf16[1552,128]{1,0:T(8,128)(2,1)S(1)}, bf16[1552,128]{1,0:T(8,128)(2,1)S(1)}, u32[]{:S(2)}, u32[]{:S(2)}) collective-permute-start(bf16[1552,128]{1,0:T(8,128)(2,1)S(1)} %get-tuple-element.35.refs_7_), channel_id=1, source_target_pairs={{0,5},{1,4},{2,7},{3,6},{4,1},{5,0},{6,3},{7,2},{8,13},{9,12},{10,... | collective-permute-start | bytes 1191944 | tf_op jit(solution)/shard_map/ppermute | solution.py:27
  16.4 2.7 %collective-permute-done.7.refs_8_.arrived = bf16[1040,128]{1,0:T(8,128)(2,1)S(1)} collective-permute-done((bf16[1040,128]{1,0:T(8,128)(2,1)S(1)}, bf16[1040,128]{1,0:T(8,128)(2,1)S(1)}, u32[]{:S(2)}, u32[]{:S(2)}) %collective-permute-start.7) | collective-permute-done | bytes 266272 | tf_op jit(solution)/shard_map/ppermute | solution.py:27
  19.1 1.7 %work.14 = (bf16[128,128]{1,0:T(8,128)(2,1)S(1)}, bf16[1024,128]{1,0:T(8,128)(2,1)S(1)}, bf16[1024,128]{1,0:T(8,128)(2,1)S(1)}, bf16[1024,128]{1,0:T(8,128)(2,1)...) custom-call(bf16[16,1024,128]{2,1,0:T(8,128)(2,1)} %bitcast.6, bf16[16,2048]{1,0:T(8,128)(2,1)} %refs_1_.7, ...), custom_call_target="tpu_custom_call" | custom-call | flops 1 | bytes 1 | tf_op jit(solution)/shard_map/work/pallas_call | solution.py:260
  20.9 0.8 %collective-permute-start.8 = (bf16[1024,128]{1,0:T(8,128)(2,1)S(1)}, bf16[1024,128]{1,0:T(8,128)(2,1)S(1)}, u32[]{:S(2)}, u32[]{:S(2)}) collective-permute-start(bf16[1024,128]{1,0:T(8,128)(2,1)S(1)} %get-tuple-element.37), channel_id=1, source_target_pairs={{0,1},{1,0},{2,3},{3,2},{4,5},{5,4},{6,7},{7,6},{8,9},{9,8},{10,11... | collective-permute-start | bytes 786440 | tf_op jit(solution)/shard_map/ppermute | solution.py:20
  21.7 0.1 collective-permute-start.9
  21.8 0.4 %collective-permute-start.10 = (bf16[1024,128]{1,0:T(8,128)(2,1)S(1)}, bf16[1024,128]{1,0:T(8,128)(2,1)S(1)}, u32[]{:S(2)}, u32[]{:S(2)}) collective-permute-start(bf16[1024,128]{1,0:T(8,128)(2,1)S(1)} %get-tuple-element.39), channel_id=1, source_target_pairs={{0,1},{1,0},{2,3},{3,2},{4,5},{5,4},{6,7},{7,6},{8,9},{9,8},{10,11... | collective-permute-start | bytes 786440 | tf_op jit(solution)/shard_map/ppermute | solution.py:20
  22.2 0.1 collective-permute-start.11
  22.3 0.6 %collective-permute-done.9.refs_2_ = bf16[128,128]{1,0:T(8,128)(2,1)S(1)} collective-permute-done((bf16[128,128]{1,0:T(8,128)(2,1)S(1)}, bf16[128,128]{1,0:T(8,128)(2,1)S(1)}, u32[]{:S(2)}, u32[]{:S(2)}) %collective-permute-start.9) | collective-permute-done | bytes 32800 | tf_op jit(solution)/shard_map/ppermute | solution.py:20
  22.9 0.4 %collective-permute-start.12 = (bf16[1024,128]{1,0:T(8,128)(2,1)S(1)}, bf16[1024,128]{1,0:T(8,128)(2,1)S(1)}, u32[]{:S(2)}, u32[]{:S(2)}) collective-permute-start(bf16[1024,128]{1,0:T(8,128)(2,1)S(1)} %get-tuple-element.41), channel_id=1, source_target_pairs={{0,1},{1,0},{2,3},{3,2},{4,5},{5,4},{6,7},{7,6},{8,9},{9,8},{10,11... | collective-permute-start | bytes 786440 | tf_op jit(solution)/shard_map/ppermute | solution.py:20
  23.3 0.0 collective-permute-done.8.refs_1_
  23.3 1.6 %collective-permute-start.6 = (bf16[528,128]{1,0:T(8,128)(2,1)S(1)}, bf16[528,128]{1,0:T(8,128)(2,1)S(1)}, u32[]{:S(2)}, u32[]{:S(2)}) collective-permute-start(bf16[528,128]{1,0:T(8,128)(2,1)S(1)} %get-tuple-element.34), channel_id=1, source_target_pairs={{0,5},{1,4},{2,7},{3,6},{4,1},{5,0},{6,3},{7,2},{8,13},{9,12},{10,... | collective-permute-start | bytes 405512 | tf_op jit(solution)/shard_map/ppermute | solution.py:27
  24.9 0.0 collective-permute-done.10.refs_3_
  24.9 0.0 collective-permute-done.11.refs_4_
  24.9 0.0 collective-permute-done.12.refs_5_
  24.9 1.3 %work.15.kept = bf16[4160,128]{1,0:T(8,128)(2,1)S(1)} custom-call(bf16[4224,128]{1,0:T(8,128)(2,1)S(1)} %get-tuple-element.36.refs_0_, bf16[1024,128]{1,0:T(8,128)(2,1)S(1)} %collective-permute-done.8.refs_1_, bf16[128,128]{1,0:T(8,128)(2,1)S(1)} %collective-permute-done.9.refs_2_, bf16[1024,128]{1,0:T(8,128)(2,1)S(1)} %collective-permute-done.10.refs_3_, ...), custom_call_target="tpu_custom_call" | custom-call | flops 1 | bytes 1 | tf_op jit(solution)/shard_map/work/pallas_call | solution.py:260
  26.2 0.8 %add.4 = (bf16[4,1024,128]{2,1,0:T(8,128)(2,1)}, bf16[16,512]{1,0:T(8,128)(2,1)}) custom-call(bf16[1040,128]{1,0:T(8,128)(2,1)S(1)} %collective-permute-done.5.refs_5_.arrived, bf16[4160,128]{1,0:T(8,128)(2,1)S(1)} %work.15.kept), custom_call_target="tpu_custom_call" | custom-call | flops 1 | bytes 1 | tf_op jit(solution)/shard_map/add/pallas_call | solution.py:314
  27.0 0.8 %add.5 = (bf16[4,1024,128]{2,1,0:T(8,128)(2,1)}, bf16[16,512]{1,0:T(8,128)(2,1)}) custom-call(bf16[1040,128]{1,0:T(8,128)(2,1)S(1)} %collective-permute-done.7.refs_8_.arrived, bf16[4160,128]{1,0:T(8,128)(2,1)S(1)} %work.15.kept, bf16[4,1024,128]{2,1,0:T(8,128)(2,1)} %get-tuple-element.42.rest_0_, ...), custom_call_target="tpu_custom_call", output_to_operand_aliasing={{0}: (2, {}), {1}: (3, {})} | custom-call | flops 1 | bytes 1 | tf_op jit(solution)/shard_map/add/pallas_call | solution.py:314
  27.9 0.0 collective-permute-done.13.arrived
  27.9 0.9 %add.6 = (bf16[4,1024,128]{2,1,0:T(8,128)(2,1)}, bf16[16,512]{1,0:T(8,128)(2,1)}) custom-call(bf16[1552,128]{1,0:T(8,128)(2,1)S(1)} %collective-permute-done.13.arrived, bf16[4160,128]{1,0:T(8,128)(2,1)S(1)} %work.15.kept, bf16[4,1024,128]{2,1,0:T(8,128)(2,1)} %get-tuple-element.44.rest_0_, ...), custom_call_target="tpu_custom_call", output_to_operand_aliasing={{0}: (2, {}), {1}: (3, {})} | custom-call | flops 1 | bytes 1 | tf_op jit(solution)/shard_map/add/pallas_call | solution.py:314
  28.8 1.5 %collective-permute-done.6.arrived = bf16[528,128]{1,0:T(8,128)(2,1)S(1)} collective-permute-done((bf16[528,128]{1,0:T(8,128)(2,1)S(1)}, bf16[528,128]{1,0:T(8,128)(2,1)S(1)}, u32[]{:S(2)}, u32[]{:S(2)}) %collective-permute-start.6) | collective-permute-done | bytes 135200 | tf_op jit(solution)/shard_map/ppermute | solution.py:27
  30.2 0.8 %add.7 = (bf16[4,1024,128]{2,1,0:T(8,128)(2,1)}, bf16[16,512]{1,0:T(8,128)(2,1)}) custom-call(bf16[528,128]{1,0:T(8,128)(2,1)S(1)} %collective-permute-done.6.arrived, bf16[4160,128]{1,0:T(8,128)(2,1)S(1)} %work.15.kept, bf16[4,1024,128]{2,1,0:T(8,128)(2,1)} %get-tuple-element.46.rest_0_, ...), custom_call_target="tpu_custom_call", output_to_operand_aliasing={{0}: (2, {}), {1}: (3, {})} | custom-call | flops 1 | bytes 1 | tf_op jit(solution)/shard_map/add/pallas_call | solution.py:314
Async XLA Ops:
  1.9 1.7 %collective-permute-start = (bf16[1056,128]{1,0:T(8,128)(2,1)S(1)}, bf16[1056,128]{1,0:T(8,128)(2,1)S(1)}, u32[]{:S(2)}, u32[]{:S(2)}) collective-permute-start(bf16[1056,128]{1,0:T(8,128)(2,1)S(1)} %get-tuple-element.28.refs_7_), channel_id=1, source_target_pairs={{0,1},{1,0},{2,3},{3,2},{4,5},{5,4},{6,7},{7,6},{8,9},{9,8},{10,11... | collective-permute-start | bytes 811016 | tf_op jit(solution)/shard_map/ppermute | solution.py:20
  2.4 5.7 %collective-permute-start.4 = (bf16[1056,128]{1,0:T(8,128)(2,1)S(1)}, bf16[1056,128]{1,0:T(8,128)(2,1)S(1)}, u32[]{:S(2)}, u32[]{:S(2)}) collective-permute-start(bf16[1056,128]{1,0:T(8,128)(2,1)S(1)} %get-tuple-element.33), channel_id=1, source_target_pairs={{0,1},{1,0},{2,3},{3,2},{4,5},{5,4},{6,7},{7,6},{8,9},{9,8},{10,11... | collective-permute-start | bytes 811016 | tf_op jit(solution)/shard_map/ppermute | solution.py:20
  4.0 9.5 %collective-permute-start.5 = (bf16[1040,128]{1,0:T(8,128)(2,1)S(1)}, bf16[1040,128]{1,0:T(8,128)(2,1)S(1)}, u32[]{:S(2)}, u32[]{:S(2)}) collective-permute-start(bf16[1040,128]{1,0:T(8,128)(2,1)S(1)} %work.10.refs_7_), channel_id=1, source_target_pairs={{0,5},{1,4},{2,7},{3,6},{4,1},{5,0},{6,3},{7,2},{8,13},{9,12},{10,... | collective-permute-start | bytes 798728 | tf_op jit(solution)/shard_map/ppermute | solution.py:27
  8.5 10.6 %collective-permute-start.7 = (bf16[1040,128]{1,0:T(8,128)(2,1)S(1)}, bf16[1040,128]{1,0:T(8,128)(2,1)S(1)}, u32[]{:S(2)}, u32[]{:S(2)}) collective-permute-start(bf16[1040,128]{1,0:T(8,128)(2,1)S(1)} %work.12.refs_4_), channel_id=1, source_target_pairs={{0,5},{1,4},{2,7},{3,6},{4,1},{5,0},{6,3},{7,2},{8,13},{9,12},{10,... | collective-permute-start | bytes 798728 | tf_op jit(solution)/shard_map/ppermute | solution.py:27
  8.6 2.0 %collective-permute-start.1 = (bf16[1024,128]{1,0:T(8,128)(2,1)S(1)}, bf16[1024,128]{1,0:T(8,128)(2,1)S(1)}, u32[]{:S(2)}, u32[]{:S(2)}) collective-permute-start(bf16[1024,128]{1,0:T(8,128)(2,1)S(1)} %get-tuple-element.30), channel_id=1, source_target_pairs={{0,1},{1,0},{2,3},{3,2},{4,5},{5,4},{6,7},{7,6},{8,9},{9,8},{10,11... | collective-permute-start | bytes 786440 | tf_op jit(solution)/shard_map/ppermute | solution.py:20
  9.1 1.6 %collective-permute-start.3 = (bf16[1024,128]{1,0:T(8,128)(2,1)S(1)}, bf16[1024,128]{1,0:T(8,128)(2,1)S(1)}, u32[]{:S(2)}, u32[]{:S(2)}) collective-permute-start(bf16[1024,128]{1,0:T(8,128)(2,1)S(1)} %get-tuple-element.32), channel_id=1, source_target_pairs={{0,1},{1,0},{2,3},{3,2},{4,5},{5,4},{6,7},{7,6},{8,9},{9,8},{10,11... | collective-permute-start | bytes 786440 | tf_op jit(solution)/shard_map/ppermute | solution.py:20
  9.2 1.4 %collective-permute-start.2 = (bf16[64,128]{1,0:T(8,128)(2,1)S(1)}, bf16[64,128]{1,0:T(8,128)(2,1)S(1)}, u32[]{:S(2)}, u32[]{:S(2)}) collective-permute-start(bf16[64,128]{1,0:T(8,128)(2,1)S(1)} %get-tuple-element.31), channel_id=1, source_target_pairs={{0,1},{1,0},{2,3},{3,2},{4,5},{5,4},{6,7},{7,6},{8,9},{9,8},{10,11... | collective-permute-start | bytes 49160 | tf_op jit(solution)/shard_map/ppermute | solution.py:20
  14.2 13.7 %collective-permute-start.13 = (bf16[1552,128]{1,0:T(8,128)(2,1)S(1)}, bf16[1552,128]{1,0:T(8,128)(2,1)S(1)}, u32[]{:S(2)}, u32[]{:S(2)}) collective-permute-start(bf16[1552,128]{1,0:T(8,128)(2,1)S(1)} %get-tuple-element.35.refs_7_), channel_id=1, source_target_pairs={{0,5},{1,4},{2,7},{3,6},{4,1},{5,0},{6,3},{7,2},{8,13},{9,12},{10,... | collective-permute-start | bytes 1191944 | tf_op jit(solution)/shard_map/ppermute | solution.py:27
  20.9 2.4 %collective-permute-start.8 = (bf16[1024,128]{1,0:T(8,128)(2,1)S(1)}, bf16[1024,128]{1,0:T(8,128)(2,1)S(1)}, u32[]{:S(2)}, u32[]{:S(2)}) collective-permute-start(bf16[1024,128]{1,0:T(8,128)(2,1)S(1)} %get-tuple-element.37), channel_id=1, source_target_pairs={{0,1},{1,0},{2,3},{3,2},{4,5},{5,4},{6,7},{7,6},{8,9},{9,8},{10,11... | collective-permute-start | bytes 786440 | tf_op jit(solution)/shard_map/ppermute | solution.py:20
  21.7 1.2 %collective-permute-start.9 = (bf16[128,128]{1,0:T(8,128)(2,1)S(1)}, bf16[128,128]{1,0:T(8,128)(2,1)S(1)}, u32[]{:S(2)}, u32[]{:S(2)}) collective-permute-start(bf16[128,128]{1,0:T(8,128)(2,1)S(1)} %get-tuple-element.38.refs_6_), channel_id=1, source_target_pairs={{0,1},{1,0},{2,3},{3,2},{4,5},{5,4},{6,7},{7,6},{8,9},{9,8},{10,11... | collective-permute-start | bytes 98312 | tf_op jit(solution)/shard_map/ppermute | solution.py:20
  21.8 3.1 %collective-permute-start.10 = (bf16[1024,128]{1,0:T(8,128)(2,1)S(1)}, bf16[1024,128]{1,0:T(8,128)(2,1)S(1)}, u32[]{:S(2)}, u32[]{:S(2)}) collective-permute-start(bf16[1024,128]{1,0:T(8,128)(2,1)S(1)} %get-tuple-element.39), channel_id=1, source_target_pairs={{0,1},{1,0},{2,3},{3,2},{4,5},{5,4},{6,7},{7,6},{8,9},{9,8},{10,11... | collective-permute-start | bytes 786440 | tf_op jit(solution)/shard_map/ppermute | solution.py:20
  22.2 2.7 %collective-permute-start.11 = (bf16[1024,128]{1,0:T(8,128)(2,1)S(1)}, bf16[1024,128]{1,0:T(8,128)(2,1)S(1)}, u32[]{:S(2)}, u32[]{:S(2)}) collective-permute-start(bf16[1024,128]{1,0:T(8,128)(2,1)S(1)} %get-tuple-element.40), channel_id=1, source_target_pairs={{0,1},{1,0},{2,3},{3,2},{4,5},{5,4},{6,7},{7,6},{8,9},{9,8},{10,11... | collective-permute-start | bytes 786440 | tf_op jit(solution)/shard_map/ppermute | solution.py:20
  22.9 2.0 %collective-permute-start.12 = (bf16[1024,128]{1,0:T(8,128)(2,1)S(1)}, bf16[1024,128]{1,0:T(8,128)(2,1)S(1)}, u32[]{:S(2)}, u32[]{:S(2)}) collective-permute-start(bf16[1024,128]{1,0:T(8,128)(2,1)S(1)} %get-tuple-element.41), channel_id=1, source_target_pairs={{0,1},{1,0},{2,3},{3,2},{4,5},{5,4},{6,7},{7,6},{8,9},{9,8},{10,11... | collective-permute-start | bytes 786440 | tf_op jit(solution)/shard_map/ppermute | solution.py:20
  23.3 6.9 %collective-permute-start.6 = (bf16[528,128]{1,0:T(8,128)(2,1)S(1)}, bf16[528,128]{1,0:T(8,128)(2,1)S(1)}, u32[]{:S(2)}, u32[]{:S(2)}) collective-permute-start(bf16[528,128]{1,0:T(8,128)(2,1)S(1)} %get-tuple-element.34), channel_id=1, source_target_pairs={{0,5},{1,4},{2,7},{3,6},{4,1},{5,0},{6,3},{7,2},{8,13},{9,12},{10,... | collective-permute-start | bytes 405512 | tf_op jit(solution)/shard_map/ppermute | solution.py:27

commit v7 on v6

--- a/solution.py
+++ b/solution.py
@@ -39,6 +39,11 @@
     if size & (size - 1) == 0:
         return value >> (size.bit_length() - 1), value & (size - 1)
     return value // size, value % size
+
+
+def pieces_of(slots, count):
+    edges = [slots * at // count for at in range(count + 1)]
+    return list(zip(edges, edges[1:]))
 
 
 def tile_at(phase, piece, partner):
@@ -81,7 +86,7 @@
     out[...] = maps.astype(jnp.float32).astype(out.dtype)
 
 
-def merge_tile(slots, width, own, other, own_side, other_side, put):
+def merge_tile(slots, width, own, other, own_side, other_side, wanted, put):
     along = lax.broadcasted_iota(jnp.int32, (width, width), 0).astype(jnp.float32)
     own_maps, other_maps = (x[:HALF].astype(jnp.float32) for x in (own_side, other_side))
 
@@ -97,8 +102,9 @@
         )
 
     def block_of(parts, slot):
-        here, at = divmod(slot, slots // len(parts))
-        return parts[here][at * width : (at + 1) * width, :]
+        for part, (first, end) in zip(parts, pieces_of(slots, len(parts))):
+            if first <= slot < end:
+                return part[(slot - first) * width : (slot - first + 1) * width, :]
 
     def moved(rows_hot, tile, pair):
         blocks = [block_of(tile, slot) for slot in (2 * pair, 2 * pair + 1)]
@@ -108,14 +114,17 @@
         return [value[:, :width], value[:, width:]]
 
     own_rows, other_rows = hot(own_maps, slots), hot(other_maps, slots)
-    rows_done = []
+    rows_done = {}
     for pair in range(slots // 2):
-        halves = moved(own_rows, own, pair), moved(other_rows, other, pair)
-        rows_done += [jnp.concatenate(both, 1) for both in zip(*halves)]
-    for slot, value in enumerate(rows_done):
+        if wanted(2 * pair * width):
+            halves = moved(own_rows, own, pair), moved(other_rows, other, pair)
+            for at, both in enumerate(zip(*halves)):
+                rows_done[2 * pair + at] = jnp.concatenate(both, 1)
+    for slot, value in rows_done.items():
         put(slot * width, across(value, slot).astype(jnp.bfloat16))
-    feats = jnp.concatenate([own_side[HALF:], other_side[HALF:]], 1)
-    put(slots * width, across(feats, slots).astype(jnp.bfloat16))
+    if wanted(slots * width):
+        feats = jnp.concatenate([own_side[HALF:], other_side[HALF:]], 1)
+        put(slots * width, across(feats, slots).astype(jnp.bfloat16))
 
 
 def work_kernel(plan, refs):
@@ -137,12 +146,12 @@
             tile = tile_at(*pick)
             lanes = pl.ds(pl.multiple_of(tile * width, width), width)
             sides.append(refs[side].at[pl.ds(side_at, HALF)])
-            part = rows // len(mains)
-            for at, main in enumerate(mains):
+            for at, (first, end) in enumerate(pieces_of(rows // width, len(mains))):
+                size = (end - first) * width
                 copies.append(
                     start(
-                        adjacency.at[tile, pl.ds(at * part, part)],
-                        refs[main].at[pl.ds(main_at, part)],
+                        adjacency.at[tile, pl.ds(first * width, size)],
+                        refs[mains[at]].at[pl.ds(main_at, size)],
                         sems.at[plan.sems[i] + at],
                     )
                 )
@@ -155,17 +164,22 @@
             )
     for i, (own, other) in enumerate(plan.merges):
         tiles = [
-            [refs[main].at[pl.ds(at, rows // len(mains))] for main in mains]
+            [
+                None if main is None else refs[main].at[pl.ds(at, (end - first) * plan.width)]
+                for main, (first, end) in zip(mains, pieces_of(rows // plan.width, len(mains)))
+            ]
             for mains, at, _, _ in (own, other)
         ]
         ends = [refs[side][at : at + plan.depth - rows, :] for _, _, side, at in (own, other)]
 
+        def wanted(row, base=i * plan.sum_depth):
+            return plan.place(base + row) is not None
+
         def put(row, value, base=i * plan.sum_depth):
-            first, out = max(known for known in plan.outs if known[0] <= base + row)
-            here = pl.ds(base + row - first, value.shape[0])
-            refs[out][here, :] = value
-
-        merge_tile(rows // plan.width, plan.width, *tiles, *ends, put)
+            out, at = plan.place(base + row)
+            refs[out][pl.ds(at, value.shape[0]), :] = value
+
+        merge_tile(rows // plan.width, plan.width, *tiles, *ends, wanted, put)
     for copy in small:
         copy.wait()
     for i, pick in enumerate(plan.picks):
@@ -178,7 +192,14 @@
 
 
 class Plan:
-    pass
+    def place(self, row):
+        for out, segments in self.outs:
+            at = 0
+            for first, size in segments:
+                if first <= row < first + size:
+                    return out, at + row - first
+                at += size
+        return None
 
 
 class Work:
@@ -188,7 +209,7 @@
         self.span = span
         self.own, self.other = {}, {}
 
-    def run(self, merges=(), keys=(), leaving=(), apart=(), after=(), cuts=()):
+    def run(self, merges=(), keys=(), leaving=(), apart=(), joint=False, after=(), sums=None):
         adjacency, features, cols, match_one, match_two = self.sources
         rows, width = adjacency.shape[1:]
         plan = Plan()
@@ -209,12 +230,29 @@
         plan.sources = [take(value, HBM) for value in self.sources] if plan.picks else []
         plan.first = not self.tables
         plan.tables = [take(value, VMEM) for value in self.tables] if plan.picks else []
+        if sums is None:
+            sums = [[(0, len(merges) * plan.sum_depth)]] if merges else []
+        plan.outs = [(None, segments) for segments in sums]
+
+        def needed(i, mains, at):
+            first, end = pieces_of(rows // width, len(mains))[at]
+            base = i * plan.sum_depth
+            return any(plan.place(base + slot * width) for slot in range(first, end))
+
         plan.merges = [
             [
-                ([take(main, VMEM) for main in mains], at, take(side, VMEM), side_at)
+                (
+                    [
+                        take(main, VMEM) if needed(i, mains, piece) else None
+                        for piece, main in enumerate(mains)
+                    ],
+                    at,
+                    take(side, VMEM),
+                    side_at,
+                )
                 for mains, at, side, side_at in (self.own[key], self.other[key])
             ]
-            for key in merges
+            for i, key in enumerate(merges)
         ]
         for value in after:
             take(value, ANY)
@@ -223,16 +261,20 @@
             shapes.append(pltpu.VMEM((depth, width), adjacency.dtype))
             return len(ins) + len(shapes) - 1
 
-        edges = [0, *cuts, len(merges) * plan.sum_depth]
-        sizes = [high - low for low, high in zip(edges, edges[1:])] if merges else []
-        plan.outs = [(low, give(size)) for low, size in zip(edges, sizes)]
+        plan.outs = [(give(sum(size for _, size in segments)), segments) for segments in sums]
         extra = plan.depth - rows
         if apart:
-            side = give(len(leaving) * extra)
-            plan.targets = [
-                ([give(rows // parts) for _ in range(parts)], 0, side, i * extra)
-                for i, parts in enumerate(apart)
-            ]
+            ends = len(leaving) * extra
+            side = None if joint else give(ends)
+            plan.targets = []
+            for i, parts in enumerate(apart):
+                heights = [(end - first) * width for first, end in pieces_of(rows // width, parts)]
+                if i == 0:
+                    behind = heights[0] if joint else 0
+                    heights[0] += ends if joint else 0
+                mains = [give(height) for height in heights]
+                side = mains[0] if side is None else side
+                plan.targets.append((mains, 0, side, behind + i * extra))
         else:
             mains = [give(plan.depth) for _ in leaving]
             plan.targets = [([main], 0, main, rows) for main in mains]
@@ -278,33 +320,36 @@
                     value = swapped(made[place], "sub") if pick[2] else made[place]
                     crossed[place] = in_vmem(value)
             where[pick[:2]] = ([crossed[main] for main in mains], main_at, crossed[side], side_at)
-        return list(outs[: len(sizes)] if merges else outs)
-
-
-def add_kernel(begin, depth, rows, arrived, kept, *rest):
+        return list(outs[: len(sums)] if merges else outs)
+
+
+def add_kernel(segments, depth, rows, arrived, kept, *rest):
     tiles_out, feats_out, total, sems = rest[-4:]
     width = arrived.shape[-1]
-    end = begin + arrived.shape[0]
     copies = []
-    for tile in range(begin // depth, -(-end // depth)):
-        for low, high in ((0, rows), (rows, depth)):
-            low, high = max(begin, tile * depth + low), min(end, tile * depth + high)
-            if low >= high:
-                continue
-            here = slice(low - begin, high - begin)
-            value = kept[low:high].astype(jnp.float32) + arrived[here].astype(jnp.float32)
-            total[here] = value.astype(jnp.bfloat16)
-            if high - tile * depth > rows:
-                target = feats_out.at[:, pl.ds(tile * width, width)]
-            else:
-                target = tiles_out.at[tile, pl.ds(low - tile * depth, high - low)]
-            source = total.at[pl.ds(low - begin, high - low)]
-            copies.append(start(source, target, sems.at[len(copies)]))
+    begin = 0
+    for first, size in segments:
+        for tile in range(first // depth, -(-(first + size) // depth)):
+            for low, high in ((0, rows), (rows, depth)):
+                low, high = max(first, tile * depth + low), min(first + size, tile * depth + high)
+                if low >= high:
+                    continue
+                at = begin + low - first
+                value = kept[low:high].astype(jnp.float32)
+                value += arrived[at : at + high - low].astype(jnp.float32)
+                total[at : at + high - low] = value.astype(jnp.bfloat16)
+                if high - tile * depth > rows:
+                    target = feats_out.at[:, pl.ds(tile * width, width)]
+                else:
+                    target = tiles_out.at[tile, pl.ds(low - tile * depth, high - low)]
+                source = total.at[pl.ds(at, high - low)]
+                copies.append(start(source, target, sems.at[len(copies)]))
+        begin += size
     for copy in copies:
         copy.wait()
 
 
-def added(begin, depth, rows, arrived, kept, before):
+def added(segments, depth, rows, arrived, kept, before):
     size, width = arrived.shape
     quarter = kept.shape[0] // depth
     shapes = (
@@ -312,13 +357,13 @@
         jax.ShapeDtypeStruct((depth - rows, quarter * width), jnp.bfloat16),
     )
     return pl.pallas_call(
-        functools.partial(add_kernel, begin, depth, rows),
+        functools.partial(add_kernel, segments, depth, rows),
         out_shape=shapes,
         in_specs=[VMEM, VMEM] + [HBM] * len(before),
         out_specs=(HBM, HBM),
         scratch_shapes=[
             pltpu.VMEM((size, width), jnp.bfloat16),
-            pltpu.SemaphoreType.DMA((2 * quarter,)),
+            pltpu.SemaphoreType.DMA((2 * quarter + len(segments),)),
         ],
         input_output_aliases={2: 0, 3: 1} if before else {},
         compiler_params=pltpu.CompilerParams(vmem_limit_bytes=LIMIT),
@@ -339,25 +384,38 @@
     keep = [(1, piece) for piece in range(quarter)]
     rows = slots * width
     depth = rows + feat_count
-    first = work.run(leaving=send[:2])
-    work.run(keys=send[:1], after=first[:1])
-    parcels = work.run(merges=send[:1])
-    arrived = [crossed_over(parcels[0])]
-    work.run(keys=send[1:], leaving=send[2:], apart=[1] * (quarter - 2), after=parcels)
-    parcels = work.run(merges=send[1:2])
-    arrived.append(crossed_over(parcels[0]))
-    cut = (quarter - 3) * depth + slots // 2 * width
-    parcels = work.run(merges=send[2:], after=parcels + arrived[:1], cuts=[cut])
-    arrived += [crossed_over(parcel) for parcel in parcels]
+    half = slots // 2 * width
+    work.run(keys=send[:2], leaving=send[:2], apart=[2, 2], joint=True)
+    cut = 3 * depth + 5 * slots // 8 * width
+    parts = [
+        [(0, half), (rows, feat_count)],
+        [(half, rows - half), (depth, depth)],
+        [(2 * depth, cut - 2 * depth)],
+        [(cut, quarter * depth - cut)],
+    ]
+    arrived = []
+
+    def merge(keys, which, after):
+        base = keys[0][1] * depth
+        sums = [[(first - base, size) for first, size in parts[at]] for at in which]
+        parcels = work.run(merges=keys, sums=sums, after=after)
+        arrived.extend(crossed_over(parcel) for parcel in parcels)
+        return parcels
+
+    parcels = merge(send[:1], [0], [])
+    parcels = merge(send[:2], [1], parcels)
+    work.run(
+        keys=send[2:], leaving=send[2:], apart=[1] * (quarter - 2), joint=True,
+        after=parcels + arrived[:1],
+    )
+    parcels = merge(send[2:], [2, 3], [])
     last = work.run(
         keys=keep, leaving=keep, apart=[1] * quarter, after=parcels[:1] + arrived[1:2]
     )
     kept = work.run(merges=keep, after=last[:1])[0]
     out = []
-    begin = 0
-    for part in arrived:
-        out = added(begin, depth, rows, part, kept, out)
-        begin += part.shape[0]
+    for segments, part in zip(parts, arrived):
+        out = added(segments, depth, rows, part, kept, out)
     return out[0].reshape(quarter, slots, width, width), out[1]
 
 

time: 31.3 us -> 31.4 us (level)
  Pallas kernels: 11.6 us -> 10.9 us
  starting transfers between devices: 9.92 us -> 10.4 us
  waiting for transfers between devices: 8.75 us -> 9.11 us
    ppermute x10 -> x11, waiting for transfers between devices: 1.78 us -> 2.54 us  [swapped(): return lax.ppermute(value, axis, pairs)]
    pallas_call x8 -> x7, Pallas kernels: 8.27 us -> 7.58 us  [run(): pl.pallas_call(lambda *refs: work_kernel(plan, refs), out_shape=shapes, i...]
    ppermute x4, waiting for transfers between devices: 6.97 us -> 6.58 us  [crossed_over(): return lax.ppermute(value, ('blk', 'sub'), pairs)]
    ppermute x10 -> x11, starting transfers between devices: 3.32 us -> 3.56 us  [swapped(): return lax.ppermute(value, axis, pairs)]
  transfers between devices with their start and end apart: 14 -> 15, of which waited for: 6 -> 7; matrix products, arithmetic and copies ran while one was open for 0% -> 0% of each run, Pallas kernels for 31% -> 28%
where the time goes in v7:
time: 31.4 us; the launch traced here: 31.2 us
  Pallas kernels  10.9 us (35%)
  starting transfers between devices  10.4 us (33%)
  waiting for transfers between devices  9.11 us (29%)
  between operations  0.72 us (2%)
    pallas_call x7, Pallas kernels, run(): pl.pallas_call(lambda *refs: work_kernel(plan, refs), out_shape=shapes, i...  7.58 us
    ppermute x4, starting transfers between devices, crossed_over(): return lax.ppermute(value, ('blk', 'sub'), pairs)  6.85 us
    ppermute x4, waiting for transfers between devices, crossed_over(): return lax.ppermute(value, ('blk', 'sub'), pairs)  6.58 us
    ppermute x11, starting transfers between devices, swapped(): return lax.ppermute(value, axis, pairs)  3.56 us
    pallas_call x4, Pallas kernels, added(): pl.pallas_call(functools.partial(add_kernel, segments, depth, rows), out_...  3.34 us
    ppermute x11, waiting for transfers between devices, swapped(): return lax.ppermute(value, axis, pairs)  2.54 us
  transfers between devices with their start and end apart: 15, of which 7 were waited for; matrix products, arithmetic and copies ran while one was open for 0% of the time, Pallas kernels for 28%

profile of v7, /device:TPU:0, one launch (start us, length us, event | category | flops | bytes accessed | tf_op | source)
XLA Modules:
  0.0 31.2 jit_solution(6542131397543874190)
XLA Ops:
  0.6 1.5 %work.7 = (bf16[576,128]{1,0:T(8,128)(2,1)S(1)}, bf16[512,128]{1,0:T(8,128)(2,1)S(1)}, bf16[512,128]{1,0:T(8,128)(2,1)S(1)}, bf16[512,128]{1,0:T(8,128)(2,1)S(1)...) custom-call(bf16[16,1024,128]{2,1,0:T(8,128)(2,1)} %bitcast.3, ...), custom_call_target="tpu_custom_call" | custom-call | flops 1 | bytes 1 | tf_op jit(solution)/shard_map/work/pallas_call | solution.py:302
  2.2 0.5 %collective-permute-start.1 = (bf16[576,128]{1,0:T(8,128)(2,1)S(1)}, bf16[576,128]{1,0:T(8,128)(2,1)S(1)}, u32[]{:S(2)}, u32[]{:S(2)}) collective-permute-start(bf16[576,128]{1,0:T(8,128)(2,1)S(1)} %get-tuple-element.32), channel_id=1, source_target_pairs={{0,1},{1,0},{2,3},{3,2},{4,5},{5,4},{6,7},{7,6},{8,9},{9,8},{10,11... | collective-permute-start | bytes 442376 | tf_op jit(solution)/shard_map/ppermute | solution.py:20
  2.7 0.1 collective-permute-start
  2.8 0.4 %collective-permute-start.2 = (bf16[512,128]{1,0:T(8,128)(2,1)S(1)}, bf16[512,128]{1,0:T(8,128)(2,1)S(1)}, u32[]{:S(2)}, u32[]{:S(2)}) collective-permute-start(bf16[512,128]{1,0:T(8,128)(2,1)S(1)} %get-tuple-element.33), channel_id=1, source_target_pairs={{0,1},{1,0},{2,3},{3,2},{4,5},{5,4},{6,7},{7,6},{8,9},{9,8},{10,11... | collective-permute-start | bytes 393224 | tf_op jit(solution)/shard_map/ppermute | solution.py:20
  3.2 0.1 collective-permute-start.3
  3.3 0.4 %collective-permute-done.1.refs_1_.refs_2_ = bf16[576,128]{1,0:T(8,128)(2,1)S(1)} collective-permute-done((bf16[576,128]{1,0:T(8,128)(2,1)S(1)}, bf16[576,128]{1,0:T(8,128)(2,1)S(1)}, u32[]{:S(2)}, u32[]{:S(2)}) %collective-permute-start.1) | collective-permute-done | bytes 147488 | tf_op jit(solution)/shard_map/ppermute | solution.py:20
  3.7 0.3 %work.8.refs_5_ = bf16[528,128]{1,0:T(8,128)(2,1)S(1)} custom-call(bf16[2112,128]{1,0:T(8,128)(2,1)S(1)} %get-tuple-element.30.refs_0_, bf16[576,128]{1,0:T(8,128)(2,1)S(1)} %collective-permute-done.1.refs_1_.refs_2_), custom_call_target="tpu_custom_call" | custom-call | flops 1 | bytes 1 | tf_op jit(solution)/shard_map/work/pallas_call | solution.py:302
  4.0 2.7 %collective-permute-start.4 = (bf16[528,128]{1,0:T(8,128)(2,1)S(1)}, bf16[528,128]{1,0:T(8,128)(2,1)S(1)}, u32[]{:S(2)}, u32[]{:S(2)}) collective-permute-start(bf16[528,128]{1,0:T(8,128)(2,1)S(1)} %work.8.refs_5_), channel_id=1, source_target_pairs={{0,5},{1,4},{2,7},{3,6},{4,1},{5,0},{6,3},{7,2},{8,13},{9,12},{10,... | collective-permute-start | bytes 405512 | tf_op jit(solution)/shard_map/ppermute | solution.py:27
  6.7 0.0 collective-permute-done.refs_1_
  6.7 0.0 collective-permute-done.2.refs_3_
  6.7 0.0 collective-permute-done.3.refs_4_
  6.7 0.6 %work.9.refs_7_ = bf16[1552,128]{1,0:T(8,128)(2,1)S(1)} custom-call(bf16[2112,128]{1,0:T(8,128)(2,1)S(1)} %get-tuple-element.30.refs_0_, bf16[512,128]{1,0:T(8,128)(2,1)S(1)} %collective-permute-done.refs_1_, bf16[576,128]{1,0:T(8,128)(2,1)S(1)} %collective-permute-done.1.refs_1_.refs_2_, bf16[512,128]{1,0:T(8,128)(2,1)S(1)} %collective-permute-done.2.refs_3_, ...), custom_call_target="tpu_custom_call" | custom-call | flops 1 | bytes 1 | tf_op jit(solution)/shard_map/work/pallas_call | solution.py:302
  7.4 0.5 %collective-permute-start.8 = (bf16[1552,128]{1,0:T(8,128)(2,1)S(1)}, bf16[1552,128]{1,0:T(8,128)(2,1)S(1)}, u32[]{:S(2)}, u32[]{:S(2)}) collective-permute-start(bf16[1552,128]{1,0:T(8,128)(2,1)S(1)} %work.9.refs_7_), channel_id=1, source_target_pairs={{0,5},{1,4},{2,7},{3,6},{4,1},{5,0},{6,3},{7,2},{8,13},{9,12},{10,... | collective-permute-start | bytes 1191944 | tf_op jit(solution)/shard_map/ppermute | solution.py:27
  7.8 2.8 %collective-permute-done.4.refs_8_.arrived = bf16[528,128]{1,0:T(8,128)(2,1)S(1)} collective-permute-done((bf16[528,128]{1,0:T(8,128)(2,1)S(1)}, bf16[528,128]{1,0:T(8,128)(2,1)S(1)}, u32[]{:S(2)}, u32[]{:S(2)}) %collective-permute-start.4) | collective-permute-done | bytes 135200 | tf_op jit(solution)/shard_map/ppermute | solution.py:27
  10.7 1.3 %work.10 = (bf16[1088,128]{1,0:T(8,128)(2,1)S(1)}, bf16[1024,128]{1,0:T(8,128)(2,1)S(1)}, bf16[2112,128]{1,0:T(8,128)(2,1)S(1)}) custom-call(bf16[16,1024,128]{2,1,0:T(8,128)(2,1)} %bitcast.4, bf16[16,2048]{1,0:T(8,128)(2,1)} %refs_1_.5, s32[8,16]{1,0:T(8,128)} %bitcast.8, s32[256,128]{1,0:T(8,128)} %refs_3_.5, s32[128,128]{1,0:T(8,128)} %refs_4_.5, ...), custom_call_target="tpu_custom_call" | custom-call | flops 1 | bytes 1 | tf_op jit(solution)/shard_map/work/pallas_call | solution.py:302
  12.0 0.7 %collective-permute-start.5 = (bf16[1088,128]{1,0:T(8,128)(2,1)S(1)}, bf16[1088,128]{1,0:T(8,128)(2,1)S(1)}, u32[]{:S(2)}, u32[]{:S(2)}) collective-permute-start(bf16[1088,128]{1,0:T(8,128)(2,1)S(1)} %get-tuple-element.36), channel_id=1, source_target_pairs={{0,1},{1,0},{2,3},{3,2},{4,5},{5,4},{6,7},{7,6},{8,9},{9,8},{10,11... | collective-permute-start | bytes 835592 | tf_op jit(solution)/shard_map/ppermute | solution.py:20
  12.7 0.1 collective-permute-start.6
  12.8 1.5 %collective-permute-done.6.refs_2_ = bf16[1024,128]{1,0:T(8,128)(2,1)S(1)} collective-permute-done((bf16[1024,128]{1,0:T(8,128)(2,1)S(1)}, bf16[1024,128]{1,0:T(8,128)(2,1)S(1)}, u32[]{:S(2)}, u32[]{:S(2)}) %collective-permute-start.6) | collective-permute-done | bytes 262176 | tf_op jit(solution)/shard_map/ppermute | solution.py:20
  14.3 0.0 collective-permute-done.5.refs_1_
  14.3 0.7 %work.11 = (bf16[1680,128]{1,0:T(8,128)(2,1)S(1)}, bf16[400,128]{1,0:T(8,128)(2,1)S(1)}) custom-call(bf16[2112,128]{1,0:T(8,128)(2,1)S(1)} %get-tuple-element.35.refs_0_, bf16[1088,128]{1,0:T(8,128)(2,1)S(1)} %collective-permute-done.5.refs_1_, bf16[1024,128]{1,0:T(8,128)(2,1)S(1)} %collective-permute-done.6.refs_2_), custom_call_target="tpu_custom_call" | custom-call | flops 1 | bytes 1 | tf_op jit(solution)/shard_map/work/pallas_call | solution.py:302
  15.0 2.0 %collective-permute-start.14 = (bf16[1680,128]{1,0:T(8,128)(2,1)S(1)}, bf16[1680,128]{1,0:T(8,128)(2,1)S(1)}, u32[]{:S(2)}, u32[]{:S(2)}) collective-permute-start(bf16[1680,128]{1,0:T(8,128)(2,1)S(1)} %get-tuple-element.39.refs_7_), channel_id=1, source_target_pairs={{0,5},{1,4},{2,7},{3,6},{4,1},{5,0},{6,3},{7,2},{8,13},{9,12},{10,... | collective-permute-start | bytes 1290248 | tf_op jit(solution)/shard_map/ppermute | solution.py:27
  17.0 2.2 %collective-permute-done.8.refs_8_.arrived = bf16[1552,128]{1,0:T(8,128)(2,1)S(1)} collective-permute-done((bf16[1552,128]{1,0:T(8,128)(2,1)S(1)}, bf16[1552,128]{1,0:T(8,128)(2,1)S(1)}, u32[]{:S(2)}, u32[]{:S(2)}) %collective-permute-start.8) | collective-permute-done | bytes 397344 | tf_op jit(solution)/shard_map/ppermute | solution.py:27
  19.2 1.7 %work.12 = (bf16[128,128]{1,0:T(8,128)(2,1)S(1)}, bf16[1024,128]{1,0:T(8,128)(2,1)S(1)}, bf16[1024,128]{1,0:T(8,128)(2,1)S(1)}, bf16[1024,128]{1,0:T(8,128)(2,1)...) custom-call(bf16[16,1024,128]{2,1,0:T(8,128)(2,1)} %bitcast.5, bf16[16,2048]{1,0:T(8,128)(2,1)} %refs_1_.5, ...), custom_call_target="tpu_custom_call" | custom-call | flops 1 | bytes 1 | tf_op jit(solution)/shard_map/work/pallas_call | solution.py:302
  21.0 0.7 %collective-permute-start.9 = (bf16[1024,128]{1,0:T(8,128)(2,1)S(1)}, bf16[1024,128]{1,0:T(8,128)(2,1)S(1)}, u32[]{:S(2)}, u32[]{:S(2)}) collective-permute-start(bf16[1024,128]{1,0:T(8,128)(2,1)S(1)} %get-tuple-element.41), channel_id=1, source_target_pairs={{0,1},{1,0},{2,3},{3,2},{4,5},{5,4},{6,7},{7,6},{8,9},{9,8},{10,11... | collective-permute-start | bytes 786440 | tf_op jit(solution)/shard_map/ppermute | solution.py:20
  21.7 0.1 collective-permute-start.10
  21.7 0.4 %collective-permute-start.11 = (bf16[1024,128]{1,0:T(8,128)(2,1)S(1)}, bf16[1024,128]{1,0:T(8,128)(2,1)S(1)}, u32[]{:S(2)}, u32[]{:S(2)}) collective-permute-start(bf16[1024,128]{1,0:T(8,128)(2,1)S(1)} %get-tuple-element.43), channel_id=1, source_target_pairs={{0,1},{1,0},{2,3},{3,2},{4,5},{5,4},{6,7},{7,6},{8,9},{9,8},{10,11... | collective-permute-start | bytes 786440 | tf_op jit(solution)/shard_map/ppermute | solution.py:20
  22.2 0.1 collective-permute-start.12
  22.3 0.6 %collective-permute-done.10.refs_2_ = bf16[128,128]{1,0:T(8,128)(2,1)S(1)} collective-permute-done((bf16[128,128]{1,0:T(8,128)(2,1)S(1)}, bf16[128,128]{1,0:T(8,128)(2,1)S(1)}, u32[]{:S(2)}, u32[]{:S(2)}) %collective-permute-start.10) | collective-permute-done | bytes 32800 | tf_op jit(solution)/shard_map/ppermute | solution.py:20
  22.9 0.4 %collective-permute-start.13 = (bf16[1024,128]{1,0:T(8,128)(2,1)S(1)}, bf16[1024,128]{1,0:T(8,128)(2,1)S(1)}, u32[]{:S(2)}, u32[]{:S(2)}) collective-permute-start(bf16[1024,128]{1,0:T(8,128)(2,1)S(1)} %get-tuple-element.45), channel_id=1, source_target_pairs={{0,1},{1,0},{2,3},{3,2},{4,5},{5,4},{6,7},{7,6},{8,9},{9,8},{10,11... | collective-permute-start | bytes 786440 | tf_op jit(solution)/shard_map/ppermute | solution.py:20
  23.2 0.0 collective-permute-done.9.refs_1_
  23.2 1.7 %collective-permute-start.7 = (bf16[400,128]{1,0:T(8,128)(2,1)S(1)}, bf16[400,128]{1,0:T(8,128)(2,1)S(1)}, u32[]{:S(2)}, u32[]{:S(2)}) collective-permute-start(bf16[400,128]{1,0:T(8,128)(2,1)S(1)} %get-tuple-element.38), channel_id=1, source_target_pairs={{0,5},{1,4},{2,7},{3,6},{4,1},{5,0},{6,3},{7,2},{8,13},{9,12},{10,... | collective-permute-start | bytes 307208 | tf_op jit(solution)/shard_map/ppermute | solution.py:27
  24.9 0.0 collective-permute-done.11.refs_3_
  24.9 0.0 collective-permute-done.12.refs_4_
  25.0 0.0 collective-permute-done.13.refs_5_
  25.0 1.3 %work.13.kept = bf16[4160,128]{1,0:T(8,128)(2,1)S(1)} custom-call(bf16[4224,128]{1,0:T(8,128)(2,1)S(1)} %get-tuple-element.40.refs_0_, bf16[1024,128]{1,0:T(8,128)(2,1)S(1)} %collective-permute-done.9.refs_1_, bf16[128,128]{1,0:T(8,128)(2,1)S(1)} %collective-permute-done.10.refs_2_, bf16[1024,128]{1,0:T(8,128)(2,1)S(1)} %collective-permute-done.11.refs_3_, ...), custom_call_target="tpu_custom_call" | custom-call | flops 1 | bytes 1 | tf_op jit(solution)/shard_map/work/pallas_call | solution.py:302
  26.2 0.8 %add.4 = (bf16[4,1024,128]{2,1,0:T(8,128)(2,1)}, bf16[16,512]{1,0:T(8,128)(2,1)}) custom-call(bf16[528,128]{1,0:T(8,128)(2,1)S(1)} %collective-permute-done.4.refs_8_.arrived, bf16[4160,128]{1,0:T(8,128)(2,1)S(1)} %work.13.kept), custom_call_target="tpu_custom_call" | custom-call | flops 1 | bytes 1 | tf_op jit(solution)/shard_map/add/pallas_call | solution.py:359
  27.0 0.9 %add.5 = (bf16[4,1024,128]{2,1,0:T(8,128)(2,1)}, bf16[16,512]{1,0:T(8,128)(2,1)}) custom-call(bf16[1552,128]{1,0:T(8,128)(2,1)S(1)} %collective-permute-done.8.refs_8_.arrived, bf16[4160,128]{1,0:T(8,128)(2,1)S(1)} %work.13.kept, bf16[4,1024,128]{2,1,0:T(8,128)(2,1)} %get-tuple-element.46.rest_0_, ...), custom_call_target="tpu_custom_call", output_to_operand_aliasing={{0}: (2, {}), {1}: (3, {})} | custom-call | flops 1 | bytes 1 | tf_op jit(solution)/shard_map/add/pallas_call | solution.py:359
  27.9 0.5 %collective-permute-done.14.arrived = bf16[1680,128]{1,0:T(8,128)(2,1)S(1)} collective-permute-done((bf16[1680,128]{1,0:T(8,128)(2,1)S(1)}, bf16[1680,128]{1,0:T(8,128)(2,1)S(1)}, u32[]{:S(2)}, u32[]{:S(2)}) %collective-permute-start.14) | collective-permute-done | bytes 430112 | tf_op jit(solution)/shard_map/ppermute | solution.py:27
  28.4 0.9 %add.6 = (bf16[4,1024,128]{2,1,0:T(8,128)(2,1)}, bf16[16,512]{1,0:T(8,128)(2,1)}) custom-call(bf16[1680,128]{1,0:T(8,128)(2,1)S(1)} %collective-permute-done.14.arrived, bf16[4160,128]{1,0:T(8,128)(2,1)S(1)} %work.13.kept, bf16[4,1024,128]{2,1,0:T(8,128)(2,1)} %get-tuple-element.48.rest_0_, ...), custom_call_target="tpu_custom_call", output_to_operand_aliasing={{0}: (2, {}), {1}: (3, {})} | custom-call | flops 1 | bytes 1 | tf_op jit(solution)/shard_map/add/pallas_call | solution.py:359
  29.4 1.1 %collective-permute-done.7.arrived = bf16[400,128]{1,0:T(8,128)(2,1)S(1)} collective-permute-done((bf16[400,128]{1,0:T(8,128)(2,1)S(1)}, bf16[400,128]{1,0:T(8,128)(2,1)S(1)}, u32[]{:S(2)}, u32[]{:S(2)}) %collective-permute-start.7) | collective-permute-done | bytes 102432 | tf_op jit(solution)/shard_map/ppermute | solution.py:27
  30.4 0.7 %add.7 = (bf16[4,1024,128]{2,1,0:T(8,128)(2,1)}, bf16[16,512]{1,0:T(8,128)(2,1)}) custom-call(bf16[400,128]{1,0:T(8,128)(2,1)S(1)} %collective-permute-done.7.arrived, bf16[4160,128]{1,0:T(8,128)(2,1)S(1)} %work.13.kept, bf16[4,1024,128]{2,1,0:T(8,128)(2,1)} %get-tuple-element.50.rest_0_, ...), custom_call_target="tpu_custom_call", output_to_operand_aliasing={{0}: (2, {}), {1}: (3, {})} | custom-call | flops 1 | bytes 1 | tf_op jit(solution)/shard_map/add/pallas_call | solution.py:359
Async XLA Ops:
  2.2 1.5 %collective-permute-start.1 = (bf16[576,128]{1,0:T(8,128)(2,1)S(1)}, bf16[576,128]{1,0:T(8,128)(2,1)S(1)}, u32[]{:S(2)}, u32[]{:S(2)}) collective-permute-start(bf16[576,128]{1,0:T(8,128)(2,1)S(1)} %get-tuple-element.32), channel_id=1, source_target_pairs={{0,1},{1,0},{2,3},{3,2},{4,5},{5,4},{6,7},{7,6},{8,9},{9,8},{10,11... | collective-permute-start | bytes 442376 | tf_op jit(solution)/shard_map/ppermute | solution.py:20
  2.7 4.0 %collective-permute-start = (bf16[512,128]{1,0:T(8,128)(2,1)S(1)}, bf16[512,128]{1,0:T(8,128)(2,1)S(1)}, u32[]{:S(2)}, u32[]{:S(2)}) collective-permute-start(bf16[512,128]{1,0:T(8,128)(2,1)S(1)} %get-tuple-element.31), channel_id=1, source_target_pairs={{0,1},{1,0},{2,3},{3,2},{4,5},{5,4},{6,7},{7,6},{8,9},{9,8},{10,11... | collective-permute-start | bytes 393224 | tf_op jit(solution)/shard_map/ppermute | solution.py:20
  2.8 4.0 %collective-permute-start.2 = (bf16[512,128]{1,0:T(8,128)(2,1)S(1)}, bf16[512,128]{1,0:T(8,128)(2,1)S(1)}, u32[]{:S(2)}, u32[]{:S(2)}) collective-permute-start(bf16[512,128]{1,0:T(8,128)(2,1)S(1)} %get-tuple-element.33), channel_id=1, source_target_pairs={{0,1},{1,0},{2,3},{3,2},{4,5},{5,4},{6,7},{7,6},{8,9},{9,8},{10,11... | collective-permute-start | bytes 393224 | tf_op jit(solution)/shard_map/ppermute | solution.py:20
  3.2 3.5 %collective-permute-start.3 = (bf16[512,128]{1,0:T(8,128)(2,1)S(1)}, bf16[512,128]{1,0:T(8,128)(2,1)S(1)}, u32[]{:S(2)}, u32[]{:S(2)}) collective-permute-start(bf16[512,128]{1,0:T(8,128)(2,1)S(1)} %get-tuple-element.34), channel_id=1, source_target_pairs={{0,1},{1,0},{2,3},{3,2},{4,5},{5,4},{6,7},{7,6},{8,9},{9,8},{10,11... | collective-permute-start | bytes 393224 | tf_op jit(solution)/shard_map/ppermute | solution.py:20
  4.0 6.6 %collective-permute-start.4 = (bf16[528,128]{1,0:T(8,128)(2,1)S(1)}, bf16[528,128]{1,0:T(8,128)(2,1)S(1)}, u32[]{:S(2)}, u32[]{:S(2)}) collective-permute-start(bf16[528,128]{1,0:T(8,128)(2,1)S(1)} %work.8.refs_5_), channel_id=1, source_target_pairs={{0,5},{1,4},{2,7},{3,6},{4,1},{5,0},{6,3},{7,2},{8,13},{9,12},{10,... | collective-permute-start | bytes 405512 | tf_op jit(solution)/shard_map/ppermute | solution.py:27
  7.4 11.8 %collective-permute-start.8 = (bf16[1552,128]{1,0:T(8,128)(2,1)S(1)}, bf16[1552,128]{1,0:T(8,128)(2,1)S(1)}, u32[]{:S(2)}, u32[]{:S(2)}) collective-permute-start(bf16[1552,128]{1,0:T(8,128)(2,1)S(1)} %work.9.refs_7_), channel_id=1, source_target_pairs={{0,5},{1,4},{2,7},{3,6},{4,1},{5,0},{6,3},{7,2},{8,13},{9,12},{10,... | collective-permute-start | bytes 1191944 | tf_op jit(solution)/shard_map/ppermute | solution.py:27
  12.0 2.3 %collective-permute-start.5 = (bf16[1088,128]{1,0:T(8,128)(2,1)S(1)}, bf16[1088,128]{1,0:T(8,128)(2,1)S(1)}, u32[]{:S(2)}, u32[]{:S(2)}) collective-permute-start(bf16[1088,128]{1,0:T(8,128)(2,1)S(1)} %get-tuple-element.36), channel_id=1, source_target_pairs={{0,1},{1,0},{2,3},{3,2},{4,5},{5,4},{6,7},{7,6},{8,9},{9,8},{10,11... | collective-permute-start | bytes 835592 | tf_op jit(solution)/shard_map/ppermute | solution.py:20
  12.7 1.6 %collective-permute-start.6 = (bf16[1024,128]{1,0:T(8,128)(2,1)S(1)}, bf16[1024,128]{1,0:T(8,128)(2,1)S(1)}, u32[]{:S(2)}, u32[]{:S(2)}) collective-permute-start(bf16[1024,128]{1,0:T(8,128)(2,1)S(1)} %get-tuple-element.37), channel_id=1, source_target_pairs={{0,1},{1,0},{2,3},{3,2},{4,5},{5,4},{6,7},{7,6},{8,9},{9,8},{10,11... | collective-permute-start | bytes 786440 | tf_op jit(solution)/shard_map/ppermute | solution.py:20
  15.0 13.4 %collective-permute-start.14 = (bf16[1680,128]{1,0:T(8,128)(2,1)S(1)}, bf16[1680,128]{1,0:T(8,128)(2,1)S(1)}, u32[]{:S(2)}, u32[]{:S(2)}) collective-permute-start(bf16[1680,128]{1,0:T(8,128)(2,1)S(1)} %get-tuple-element.39.refs_7_), channel_id=1, source_target_pairs={{0,5},{1,4},{2,7},{3,6},{4,1},{5,0},{6,3},{7,2},{8,13},{9,12},{10,... | collective-permute-start | bytes 1290248 | tf_op jit(solution)/shard_map/ppermute | solution.py:27
  21.0 2.3 %collective-permute-start.9 = (bf16[1024,128]{1,0:T(8,128)(2,1)S(1)}, bf16[1024,128]{1,0:T(8,128)(2,1)S(1)}, u32[]{:S(2)}, u32[]{:S(2)}) collective-permute-start(bf16[1024,128]{1,0:T(8,128)(2,1)S(1)} %get-tuple-element.41), channel_id=1, source_target_pairs={{0,1},{1,0},{2,3},{3,2},{4,5},{5,4},{6,7},{7,6},{8,9},{9,8},{10,11... | collective-permute-start | bytes 786440 | tf_op jit(solution)/shard_map/ppermute | solution.py:20
  21.7 1.2 %collective-permute-start.10 = (bf16[128,128]{1,0:T(8,128)(2,1)S(1)}, bf16[128,128]{1,0:T(8,128)(2,1)S(1)}, u32[]{:S(2)}, u32[]{:S(2)}) collective-permute-start(bf16[128,128]{1,0:T(8,128)(2,1)S(1)} %get-tuple-element.42.refs_6_), channel_id=1, source_target_pairs={{0,1},{1,0},{2,3},{3,2},{4,5},{5,4},{6,7},{7,6},{8,9},{9,8},{10,11... | collective-permute-start | bytes 98312 | tf_op jit(solution)/shard_map/ppermute | solution.py:20
  21.7 3.2 %collective-permute-start.11 = (bf16[1024,128]{1,0:T(8,128)(2,1)S(1)}, bf16[1024,128]{1,0:T(8,128)(2,1)S(1)}, u32[]{:S(2)}, u32[]{:S(2)}) collective-permute-start(bf16[1024,128]{1,0:T(8,128)(2,1)S(1)} %get-tuple-element.43), channel_id=1, source_target_pairs={{0,1},{1,0},{2,3},{3,2},{4,5},{5,4},{6,7},{7,6},{8,9},{9,8},{10,11... | collective-permute-start | bytes 786440 | tf_op jit(solution)/shard_map/ppermute | solution.py:20
  22.2 2.8 %collective-permute-start.12 = (bf16[1024,128]{1,0:T(8,128)(2,1)S(1)}, bf16[1024,128]{1,0:T(8,128)(2,1)S(1)}, u32[]{:S(2)}, u32[]{:S(2)}) collective-permute-start(bf16[1024,128]{1,0:T(8,128)(2,1)S(1)} %get-tuple-element.44), channel_id=1, source_target_pairs={{0,1},{1,0},{2,3},{3,2},{4,5},{5,4},{6,7},{7,6},{8,9},{9,8},{10,11... | collective-permute-start | bytes 786440 | tf_op jit(solution)/shard_map/ppermute | solution.py:20
  22.9 2.1 %collective-permute-start.13 = (bf16[1024,128]{1,0:T(8,128)(2,1)S(1)}, bf16[1024,128]{1,0:T(8,128)(2,1)S(1)}, u32[]{:S(2)}, u32[]{:S(2)}) collective-permute-start(bf16[1024,128]{1,0:T(8,128)(2,1)S(1)} %get-tuple-element.45), channel_id=1, source_target_pairs={{0,1},{1,0},{2,3},{3,2},{4,5},{5,4},{6,7},{7,6},{8,9},{9,8},{10,11... | collective-permute-start | bytes 786440 | tf_op jit(solution)/shard_map/ppermute | solution.py:20
  23.2 7.2 %collective-permute-start.7 = (bf16[400,128]{1,0:T(8,128)(2,1)S(1)}, bf16[400,128]{1,0:T(8,128)(2,1)S(1)}, u32[]{:S(2)}, u32[]{:S(2)}) collective-permute-start(bf16[400,128]{1,0:T(8,128)(2,1)S(1)} %get-tuple-element.38), channel_id=1, source_target_pairs={{0,5},{1,4},{2,7},{3,6},{4,1},{5,0},{6,3},{7,2},{8,13},{9,12},{10,... | collective-permute-start | bytes 307208 | tf_op jit(solution)/shard_map/ppermute | solution.py:27

commit v8 on v7

--- a/solution.py
+++ b/solution.py
@@ -385,7 +385,8 @@
     rows = slots * width
     depth = rows + feat_count
     half = slots // 2 * width
-    work.run(keys=send[:2], leaving=send[:2], apart=[2, 2], joint=True)
+    first = work.run(leaving=send[:2])
+    work.run(keys=send[:2], after=first[:1])
     cut = 3 * depth + 5 * slots // 8 * width
     parts = [
         [(0, half), (rows, feat_count)],

time: 31.4 us -> 31.3 us (level)
  starting transfers between devices: 10.4 us -> 9.51 us
  Pallas kernels: 10.9 us -> 11.7 us
    pallas_call x7 -> x8, Pallas kernels: 7.58 us -> 8.37 us  [run(): pl.pallas_call(lambda *refs: work_kernel(plan, refs), out_shape=shapes, i...]
    ppermute x4, starting transfers between devices: 6.85 us -> 6.39 us  [crossed_over(): return lax.ppermute(value, ('blk', 'sub'), pairs)]
    ppermute x11 -> x9, starting transfers between devices: 3.56 us -> 3.11 us  [swapped(): return lax.ppermute(value, axis, pairs)]
    ppermute x11 -> x9, waiting for transfers between devices: 2.54 us -> 2.12 us  [swapped(): return lax.ppermute(value, axis, pairs)]
    ppermute x4, waiting for transfers between devices: 6.58 us -> 6.96 us  [crossed_over(): return lax.ppermute(value, ('blk', 'sub'), pairs)]
  transfers between devices with their start and end apart: 15 -> 13, of which waited for: 7 -> 6; matrix products, arithmetic and copies ran while one was open for 0% -> 0% of each run, Pallas kernels for 28% -> 31%
where the time goes in v8:
time: 31.3 us; the launch traced here: 31 us
  Pallas kernels  11.7 us (37%)
  starting transfers between devices  9.51 us (30%)
  waiting for transfers between devices  9.08 us (29%)
  between operations  0.73 us (2%)
    pallas_call x8, Pallas kernels, run(): pl.pallas_call(lambda *refs: work_kernel(plan, refs), out_shape=shapes, i...  8.37 us
    ppermute x4, waiting for transfers between devices, crossed_over(): return lax.ppermute(value, ('blk', 'sub'), pairs)  6.96 us
    ppermute x4, starting transfers between devices, crossed_over(): return lax.ppermute(value, ('blk', 'sub'), pairs)  6.39 us
    pallas_call x4, Pallas kernels, added(): pl.pallas_call(functools.partial(add_kernel, segments, depth, rows), out_...  3.34 us
    ppermute x9, starting transfers between devices, swapped(): return lax.ppermute(value, axis, pairs)  3.11 us
    ppermute x9, waiting for transfers between devices, swapped(): return lax.ppermute(value, axis, pairs)  2.12 us
  transfers between devices with their start and end apart: 13, of which 6 were waited for; matrix products, arithmetic and copies ran while one was open for 0% of the time, Pallas kernels for 31%

profile of v8, /device:TPU:0, one launch (start us, length us, event | category | flops | bytes accessed | tf_op | source)
XLA Modules:
  0.0 31.0 jit_solution(10805225251513236213)
XLA Ops:
  0.6 1.2 %work.8 = (bf16[1056,128]{1,0:T(8,128)(2,1)S(1)}, bf16[1056,128]{1,0:T(8,128)(2,1)S(1)}, s32[256,128]{1,0:T(8,128)S(1)}, s32[128,128]{1,0:T(8,128)S(1)}) custom-call(bf16[16,1024,128]{2,1,0:T(8,128)(2,1)} %bitcast.3, bf16[16,2048]{1,0:T(8,128)(2,1)} %refs_1_.7, s32[8,16]{1,0:T(8,128)} %bitcast.8, s32[256,128]{1,0:T(8,128)} %refs_3_.7, s32[128,128]{1,0:T(8,128)} %refs_4_.7), custom_call_target="tpu_custom_call" | custom-call | flops 1 | bytes 1 | tf_op jit(solution)/shard_map/work/pallas_call | solution.py:302
  1.9 0.5 %collective-permute-start = (bf16[1056,128]{1,0:T(8,128)(2,1)S(1)}, bf16[1056,128]{1,0:T(8,128)(2,1)S(1)}, u32[]{:S(2)}, u32[]{:S(2)}) collective-permute-start(bf16[1056,128]{1,0:T(8,128)(2,1)S(1)} %get-tuple-element.27.refs_7_), channel_id=1, source_target_pairs={{0,1},{1,0},{2,3},{3,2},{4,5},{5,4},{6,7},{7,6},{8,9},{9,8},{10,11... | collective-permute-start | bytes 811016 | tf_op jit(solution)/shard_map/ppermute | solution.py:20
  2.4 0.1 collective-permute-start.1
  2.5 1.1 %work.9.refs_0_ = bf16[2112,128]{1,0:T(8,128)(2,1)S(1)} custom-call(bf16[16,1024,128]{2,1,0:T(8,128)(2,1)} %bitcast.4, bf16[16,2048]{1,0:T(8,128)(2,1)} %refs_1_.7, s32[8,16]{1,0:T(8,128)} %bitcast.9, s32[256,128]{1,0:T(8,128)} %refs_3_.7, s32[128,128]{1,0:T(8,128)} %refs_4_.7, s32[256,128]{1,0:T(8,128)S(1)} %get-tuple-element.25.refs_5_, ...), custom_call_target="tpu_custom_call" | custom-call | flops 1 | bytes 1 | tf_op jit(solution)/shard_map/work/pallas_call | solution.py:302
  3.6 0.0 collective-permute-done.refs_1_
  3.6 0.3 %work.10.refs_3_ = bf16[528,128]{1,0:T(8,128)(2,1)S(1)} custom-call(bf16[2112,128]{1,0:T(8,128)(2,1)S(1)} %work.9.refs_0_, bf16[1056,128]{1,0:T(8,128)(2,1)S(1)} %collective-permute-done.refs_1_), custom_call_target="tpu_custom_call" | custom-call | flops 1 | bytes 1 | tf_op jit(solution)/shard_map/work/pallas_call | solution.py:302
  3.9 2.7 %collective-permute-start.2 = (bf16[528,128]{1,0:T(8,128)(2,1)S(1)}, bf16[528,128]{1,0:T(8,128)(2,1)S(1)}, u32[]{:S(2)}, u32[]{:S(2)}) collective-permute-start(bf16[528,128]{1,0:T(8,128)(2,1)S(1)} %work.10.refs_3_), channel_id=1, source_target_pairs={{0,5},{1,4},{2,7},{3,6},{4,1},{5,0},{6,3},{7,2},{8,13},{9,12},{10,... | collective-permute-start | bytes 405512 | tf_op jit(solution)/shard_map/ppermute | solution.py:27
  6.6 0.0 collective-permute-done.1.refs_2_
  6.6 0.6 %work.11.refs_7_ = bf16[1552,128]{1,0:T(8,128)(2,1)S(1)} custom-call(bf16[2112,128]{1,0:T(8,128)(2,1)S(1)} %work.9.refs_0_, bf16[1056,128]{1,0:T(8,128)(2,1)S(1)} %collective-permute-done.refs_1_, bf16[1056,128]{1,0:T(8,128)(2,1)S(1)} %collective-permute-done.1.refs_2_, bf16[528,128]{1,0:T(8,128)(2,1)S(1)} %work.10.refs_3_), custom_call_target="tpu_custom_call" | custom-call | flops 1 | bytes 1 | tf_op jit(solution)/shard_map/work/pallas_call | solution.py:302
  7.2 0.1 collective-permute-start.6
  7.3 3.3 %collective-permute-done.2.refs_8_.arrived = bf16[528,128]{1,0:T(8,128)(2,1)S(1)} collective-permute-done((bf16[528,128]{1,0:T(8,128)(2,1)S(1)}, bf16[528,128]{1,0:T(8,128)(2,1)S(1)}, u32[]{:S(2)}, u32[]{:S(2)}) %collective-permute-start.2) | collective-permute-done | bytes 135200 | tf_op jit(solution)/shard_map/ppermute | solution.py:27
  10.6 1.3 %work.12 = (bf16[1088,128]{1,0:T(8,128)(2,1)S(1)}, bf16[1024,128]{1,0:T(8,128)(2,1)S(1)}, bf16[2112,128]{1,0:T(8,128)(2,1)S(1)}) custom-call(bf16[16,1024,128]{2,1,0:T(8,128)(2,1)} %bitcast.5, bf16[16,2048]{1,0:T(8,128)(2,1)} %refs_1_.7, s32[8,16]{1,0:T(8,128)} %bitcast.10, s32[256,128]{1,0:T(8,128)} %refs_3_.7, s32[128,128]{1,0:T(8,128)} %refs_4_.7, ...), custom_call_target="tpu_custom_call" | custom-call | flops 1 | bytes 1 | tf_op jit(solution)/shard_map/work/pallas_call | solution.py:302
  11.9 0.7 %collective-permute-start.3 = (bf16[1088,128]{1,0:T(8,128)(2,1)S(1)}, bf16[1088,128]{1,0:T(8,128)(2,1)S(1)}, u32[]{:S(2)}, u32[]{:S(2)}) collective-permute-start(bf16[1088,128]{1,0:T(8,128)(2,1)S(1)} %get-tuple-element.30), channel_id=1, source_target_pairs={{0,1},{1,0},{2,3},{3,2},{4,5},{5,4},{6,7},{7,6},{8,9},{9,8},{10,11... | collective-permute-start | bytes 835592 | tf_op jit(solution)/shard_map/ppermute | solution.py:20
  12.7 0.1 collective-permute-start.4
  12.7 1.5 %collective-permute-done.4.refs_2_ = bf16[1024,128]{1,0:T(8,128)(2,1)S(1)} collective-permute-done((bf16[1024,128]{1,0:T(8,128)(2,1)S(1)}, bf16[1024,128]{1,0:T(8,128)(2,1)S(1)}, u32[]{:S(2)}, u32[]{:S(2)}) %collective-permute-start.4) | collective-permute-done | bytes 262176 | tf_op jit(solution)/shard_map/ppermute | solution.py:20
  14.2 0.0 collective-permute-done.3.refs_1_
  14.2 0.7 %work.13 = (bf16[1680,128]{1,0:T(8,128)(2,1)S(1)}, bf16[400,128]{1,0:T(8,128)(2,1)S(1)}) custom-call(bf16[2112,128]{1,0:T(8,128)(2,1)S(1)} %get-tuple-element.29.refs_0_, bf16[1088,128]{1,0:T(8,128)(2,1)S(1)} %collective-permute-done.3.refs_1_, bf16[1024,128]{1,0:T(8,128)(2,1)S(1)} %collective-permute-done.4.refs_2_), custom_call_target="tpu_custom_call" | custom-call | flops 1 | bytes 1 | tf_op jit(solution)/shard_map/work/pallas_call | solution.py:302
  14.9 2.0 %collective-permute-start.12 = (bf16[1680,128]{1,0:T(8,128)(2,1)S(1)}, bf16[1680,128]{1,0:T(8,128)(2,1)S(1)}, u32[]{:S(2)}, u32[]{:S(2)}) collective-permute-start(bf16[1680,128]{1,0:T(8,128)(2,1)S(1)} %get-tuple-element.33.refs_7_), channel_id=1, source_target_pairs={{0,5},{1,4},{2,7},{3,6},{4,1},{5,0},{6,3},{7,2},{8,13},{9,12},{10,... | collective-permute-start | bytes 1290248 | tf_op jit(solution)/shard_map/ppermute | solution.py:27
  16.9 2.2 %collective-permute-done.6.refs_8_.arrived = bf16[1552,128]{1,0:T(8,128)(2,1)S(1)} collective-permute-done((bf16[1552,128]{1,0:T(8,128)(2,1)S(1)}, bf16[1552,128]{1,0:T(8,128)(2,1)S(1)}, u32[]{:S(2)}, u32[]{:S(2)}) %collective-permute-start.6) | collective-permute-done | bytes 397344 | tf_op jit(solution)/shard_map/ppermute | solution.py:27
  19.1 1.7 %work.14 = (bf16[128,128]{1,0:T(8,128)(2,1)S(1)}, bf16[1024,128]{1,0:T(8,128)(2,1)S(1)}, bf16[1024,128]{1,0:T(8,128)(2,1)S(1)}, bf16[1024,128]{1,0:T(8,128)(2,1)...) custom-call(bf16[16,1024,128]{2,1,0:T(8,128)(2,1)} %bitcast.6, bf16[16,2048]{1,0:T(8,128)(2,1)} %refs_1_.7, ...), custom_call_target="tpu_custom_call" | custom-call | flops 1 | bytes 1 | tf_op jit(solution)/shard_map/work/pallas_call | solution.py:302
  20.9 0.7 %collective-permute-start.7 = (bf16[1024,128]{1,0:T(8,128)(2,1)S(1)}, bf16[1024,128]{1,0:T(8,128)(2,1)S(1)}, u32[]{:S(2)}, u32[]{:S(2)}) collective-permute-start(bf16[1024,128]{1,0:T(8,128)(2,1)S(1)} %get-tuple-element.35), channel_id=1, source_target_pairs={{0,1},{1,0},{2,3},{3,2},{4,5},{5,4},{6,7},{7,6},{8,9},{9,8},{10,11... | collective-permute-start | bytes 786440 | tf_op jit(solution)/shard_map/ppermute | solution.py:20
  21.6 0.1 collective-permute-start.8
  21.7 0.4 %collective-permute-start.9 = (bf16[1024,128]{1,0:T(8,128)(2,1)S(1)}, bf16[1024,128]{1,0:T(8,128)(2,1)S(1)}, u32[]{:S(2)}, u32[]{:S(2)}) collective-permute-start(bf16[1024,128]{1,0:T(8,128)(2,1)S(1)} %get-tuple-element.37), channel_id=1, source_target_pairs={{0,1},{1,0},{2,3},{3,2},{4,5},{5,4},{6,7},{7,6},{8,9},{9,8},{10,11... | collective-permute-start | bytes 786440 | tf_op jit(solution)/shard_map/ppermute | solution.py:20
  22.1 0.1 collective-permute-start.10
  22.2 0.6 %collective-permute-done.8.refs_2_ = bf16[128,128]{1,0:T(8,128)(2,1)S(1)} collective-permute-done((bf16[128,128]{1,0:T(8,128)(2,1)S(1)}, bf16[128,128]{1,0:T(8,128)(2,1)S(1)}, u32[]{:S(2)}, u32[]{:S(2)}) %collective-permute-start.8) | collective-permute-done | bytes 32800 | tf_op jit(solution)/shard_map/ppermute | solution.py:20
  22.8 0.4 %collective-permute-start.11 = (bf16[1024,128]{1,0:T(8,128)(2,1)S(1)}, bf16[1024,128]{1,0:T(8,128)(2,1)S(1)}, u32[]{:S(2)}, u32[]{:S(2)}) collective-permute-start(bf16[1024,128]{1,0:T(8,128)(2,1)S(1)} %get-tuple-element.39), channel_id=1, source_target_pairs={{0,1},{1,0},{2,3},{3,2},{4,5},{5,4},{6,7},{7,6},{8,9},{9,8},{10,11... | collective-permute-start | bytes 786440 | tf_op jit(solution)/shard_map/ppermute | solution.py:20
  23.2 0.0 collective-permute-done.7.refs_1_
  23.2 1.7 %collective-permute-start.5 = (bf16[400,128]{1,0:T(8,128)(2,1)S(1)}, bf16[400,128]{1,0:T(8,128)(2,1)S(1)}, u32[]{:S(2)}, u32[]{:S(2)}) collective-permute-start(bf16[400,128]{1,0:T(8,128)(2,1)S(1)} %get-tuple-element.32), channel_id=1, source_target_pairs={{0,5},{1,4},{2,7},{3,6},{4,1},{5,0},{6,3},{7,2},{8,13},{9,12},{10,... | collective-permute-start | bytes 307208 | tf_op jit(solution)/shard_map/ppermute | solution.py:27
  24.8 0.0 collective-permute-done.9.refs_3_
  24.8 0.0 collective-permute-done.10.refs_4_
  24.8 0.0 collective-permute-done.11.refs_5_
  24.9 1.3 %work.15.kept = bf16[4160,128]{1,0:T(8,128)(2,1)S(1)} custom-call(bf16[4224,128]{1,0:T(8,128)(2,1)S(1)} %get-tuple-element.34.refs_0_, bf16[1024,128]{1,0:T(8,128)(2,1)S(1)} %collective-permute-done.7.refs_1_, bf16[128,128]{1,0:T(8,128)(2,1)S(1)} %collective-permute-done.8.refs_2_, bf16[1024,128]{1,0:T(8,128)(2,1)S(1)} %collective-permute-done.9.refs_3_, ...), custom_call_target="tpu_custom_call" | custom-call | flops 1 | bytes 1 | tf_op jit(solution)/shard_map/work/pallas_call | solution.py:302
  26.1 0.8 %add.4 = (bf16[4,1024,128]{2,1,0:T(8,128)(2,1)}, bf16[16,512]{1,0:T(8,128)(2,1)}) custom-call(bf16[528,128]{1,0:T(8,128)(2,1)S(1)} %collective-permute-done.2.refs_8_.arrived, bf16[4160,128]{1,0:T(8,128)(2,1)S(1)} %work.15.kept), custom_call_target="tpu_custom_call" | custom-call | flops 1 | bytes 1 | tf_op jit(solution)/shard_map/add/pallas_call | solution.py:359
  26.9 0.9 %add.5 = (bf16[4,1024,128]{2,1,0:T(8,128)(2,1)}, bf16[16,512]{1,0:T(8,128)(2,1)}) custom-call(bf16[1552,128]{1,0:T(8,128)(2,1)S(1)} %collective-permute-done.6.refs_8_.arrived, bf16[4160,128]{1,0:T(8,128)(2,1)S(1)} %work.15.kept, bf16[4,1024,128]{2,1,0:T(8,128)(2,1)} %get-tuple-element.40.rest_0_, ...), custom_call_target="tpu_custom_call", output_to_operand_aliasing={{0}: (2, {}), {1}: (3, {})} | custom-call | flops 1 | bytes 1 | tf_op jit(solution)/shard_map/add/pallas_call | solution.py:359
  27.8 0.5 %collective-permute-done.12.arrived = bf16[1680,128]{1,0:T(8,128)(2,1)S(1)} collective-permute-done((bf16[1680,128]{1,0:T(8,128)(2,1)S(1)}, bf16[1680,128]{1,0:T(8,128)(2,1)S(1)}, u32[]{:S(2)}, u32[]{:S(2)}) %collective-permute-start.12) | collective-permute-done | bytes 430112 | tf_op jit(solution)/shard_map/ppermute | solution.py:27
  28.3 0.9 %add.6 = (bf16[4,1024,128]{2,1,0:T(8,128)(2,1)}, bf16[16,512]{1,0:T(8,128)(2,1)}) custom-call(bf16[1680,128]{1,0:T(8,128)(2,1)S(1)} %collective-permute-done.12.arrived, bf16[4160,128]{1,0:T(8,128)(2,1)S(1)} %work.15.kept, bf16[4,1024,128]{2,1,0:T(8,128)(2,1)} %get-tuple-element.42.rest_0_, ...), custom_call_target="tpu_custom_call", output_to_operand_aliasing={{0}: (2, {}), {1}: (3, {})} | custom-call | flops 1 | bytes 1 | tf_op jit(solution)/shard_map/add/pallas_call | solution.py:359
  29.2 1.0 %collective-permute-done.5.arrived = bf16[400,128]{1,0:T(8,128)(2,1)S(1)} collective-permute-done((bf16[400,128]{1,0:T(8,128)(2,1)S(1)}, bf16[400,128]{1,0:T(8,128)(2,1)S(1)}, u32[]{:S(2)}, u32[]{:S(2)}) %collective-permute-start.5) | collective-permute-done | bytes 102432 | tf_op jit(solution)/shard_map/ppermute | solution.py:27
  30.3 0.7 %add.7 = (bf16[4,1024,128]{2,1,0:T(8,128)(2,1)}, bf16[16,512]{1,0:T(8,128)(2,1)}) custom-call(bf16[400,128]{1,0:T(8,128)(2,1)S(1)} %collective-permute-done.5.arrived, bf16[4160,128]{1,0:T(8,128)(2,1)S(1)} %work.15.kept, bf16[4,1024,128]{2,1,0:T(8,128)(2,1)} %get-tuple-element.44.rest_0_, ...), custom_call_target="tpu_custom_call", output_to_operand_aliasing={{0}: (2, {}), {1}: (3, {})} | custom-call | flops 1 | bytes 1 | tf_op jit(solution)/shard_map/add/pallas_call | solution.py:359
Async XLA Ops:
  1.9 1.7 %collective-permute-start = (bf16[1056,128]{1,0:T(8,128)(2,1)S(1)}, bf16[1056,128]{1,0:T(8,128)(2,1)S(1)}, u32[]{:S(2)}, u32[]{:S(2)}) collective-permute-start(bf16[1056,128]{1,0:T(8,128)(2,1)S(1)} %get-tuple-element.27.refs_7_), channel_id=1, source_target_pairs={{0,1},{1,0},{2,3},{3,2},{4,5},{5,4},{6,7},{7,6},{8,9},{9,8},{10,11... | collective-permute-start | bytes 811016 | tf_op jit(solution)/shard_map/ppermute | solution.py:20
  2.4 4.2 %collective-permute-start.1 = (bf16[1056,128]{1,0:T(8,128)(2,1)S(1)}, bf16[1056,128]{1,0:T(8,128)(2,1)S(1)}, u32[]{:S(2)}, u32[]{:S(2)}) collective-permute-start(bf16[1056,128]{1,0:T(8,128)(2,1)S(1)} %get-tuple-element.28), channel_id=1, source_target_pairs={{0,1},{1,0},{2,3},{3,2},{4,5},{5,4},{6,7},{7,6},{8,9},{9,8},{10,11... | collective-permute-start | bytes 811016 | tf_op jit(solution)/shard_map/ppermute | solution.py:20
  3.9 6.6 %collective-permute-start.2 = (bf16[528,128]{1,0:T(8,128)(2,1)S(1)}, bf16[528,128]{1,0:T(8,128)(2,1)S(1)}, u32[]{:S(2)}, u32[]{:S(2)}) collective-permute-start(bf16[528,128]{1,0:T(8,128)(2,1)S(1)} %work.10.refs_3_), channel_id=1, source_target_pairs={{0,5},{1,4},{2,7},{3,6},{4,1},{5,0},{6,3},{7,2},{8,13},{9,12},{10,... | collective-permute-start | bytes 405512 | tf_op jit(solution)/shard_map/ppermute | solution.py:27
  7.2 11.9 %collective-permute-start.6 = (bf16[1552,128]{1,0:T(8,128)(2,1)S(1)}, bf16[1552,128]{1,0:T(8,128)(2,1)S(1)}, u32[]{:S(2)}, u32[]{:S(2)}) collective-permute-start(bf16[1552,128]{1,0:T(8,128)(2,1)S(1)} %work.11.refs_7_), channel_id=1, source_target_pairs={{0,5},{1,4},{2,7},{3,6},{4,1},{5,0},{6,3},{7,2},{8,13},{9,12},{10,... | collective-permute-start | bytes 1191944 | tf_op jit(solution)/shard_map/ppermute | solution.py:27
  11.9 2.3 %collective-permute-start.3 = (bf16[1088,128]{1,0:T(8,128)(2,1)S(1)}, bf16[1088,128]{1,0:T(8,128)(2,1)S(1)}, u32[]{:S(2)}, u32[]{:S(2)}) collective-permute-start(bf16[1088,128]{1,0:T(8,128)(2,1)S(1)} %get-tuple-element.30), channel_id=1, source_target_pairs={{0,1},{1,0},{2,3},{3,2},{4,5},{5,4},{6,7},{7,6},{8,9},{9,8},{10,11... | collective-permute-start | bytes 835592 | tf_op jit(solution)/shard_map/ppermute | solution.py:20
  12.7 1.6 %collective-permute-start.4 = (bf16[1024,128]{1,0:T(8,128)(2,1)S(1)}, bf16[1024,128]{1,0:T(8,128)(2,1)S(1)}, u32[]{:S(2)}, u32[]{:S(2)}) collective-permute-start(bf16[1024,128]{1,0:T(8,128)(2,1)S(1)} %get-tuple-element.31), channel_id=1, source_target_pairs={{0,1},{1,0},{2,3},{3,2},{4,5},{5,4},{6,7},{7,6},{8,9},{9,8},{10,11... | collective-permute-start | bytes 786440 | tf_op jit(solution)/shard_map/ppermute | solution.py:20
  14.9 13.4 %collective-permute-start.12 = (bf16[1680,128]{1,0:T(8,128)(2,1)S(1)}, bf16[1680,128]{1,0:T(8,128)(2,1)S(1)}, u32[]{:S(2)}, u32[]{:S(2)}) collective-permute-start(bf16[1680,128]{1,0:T(8,128)(2,1)S(1)} %get-tuple-element.33.refs_7_), channel_id=1, source_target_pairs={{0,5},{1,4},{2,7},{3,6},{4,1},{5,0},{6,3},{7,2},{8,13},{9,12},{10,... | collective-permute-start | bytes 1290248 | tf_op jit(solution)/shard_map/ppermute | solution.py:27
  20.9 2.3 %collective-permute-start.7 = (bf16[1024,128]{1,0:T(8,128)(2,1)S(1)}, bf16[1024,128]{1,0:T(8,128)(2,1)S(1)}, u32[]{:S(2)}, u32[]{:S(2)}) collective-permute-start(bf16[1024,128]{1,0:T(8,128)(2,1)S(1)} %get-tuple-element.35), channel_id=1, source_target_pairs={{0,1},{1,0},{2,3},{3,2},{4,5},{5,4},{6,7},{7,6},{8,9},{9,8},{10,11... | collective-permute-start | bytes 786440 | tf_op jit(solution)/shard_map/ppermute | solution.py:20
  21.6 1.2 %collective-permute-start.8 = (bf16[128,128]{1,0:T(8,128)(2,1)S(1)}, bf16[128,128]{1,0:T(8,128)(2,1)S(1)}, u32[]{:S(2)}, u32[]{:S(2)}) collective-permute-start(bf16[128,128]{1,0:T(8,128)(2,1)S(1)} %get-tuple-element.36.refs_6_), channel_id=1, source_target_pairs={{0,1},{1,0},{2,3},{3,2},{4,5},{5,4},{6,7},{7,6},{8,9},{9,8},{10,11... | collective-permute-start | bytes 98312 | tf_op jit(solution)/shard_map/ppermute | solution.py:20
  21.7 3.2 %collective-permute-start.9 = (bf16[1024,128]{1,0:T(8,128)(2,1)S(1)}, bf16[1024,128]{1,0:T(8,128)(2,1)S(1)}, u32[]{:S(2)}, u32[]{:S(2)}) collective-permute-start(bf16[1024,128]{1,0:T(8,128)(2,1)S(1)} %get-tuple-element.37), channel_id=1, source_target_pairs={{0,1},{1,0},{2,3},{3,2},{4,5},{5,4},{6,7},{7,6},{8,9},{9,8},{10,11... | collective-permute-start | bytes 786440 | tf_op jit(solution)/shard_map/ppermute | solution.py:20
  22.1 2.7 %collective-permute-start.10 = (bf16[1024,128]{1,0:T(8,128)(2,1)S(1)}, bf16[1024,128]{1,0:T(8,128)(2,1)S(1)}, u32[]{:S(2)}, u32[]{:S(2)}) collective-permute-start(bf16[1024,128]{1,0:T(8,128)(2,1)S(1)} %get-tuple-element.38), channel_id=1, source_target_pairs={{0,1},{1,0},{2,3},{3,2},{4,5},{5,4},{6,7},{7,6},{8,9},{9,8},{10,11... | collective-permute-start | bytes 786440 | tf_op jit(solution)/shard_map/ppermute | solution.py:20
  22.8 2.1 %collective-permute-start.11 = (bf16[1024,128]{1,0:T(8,128)(2,1)S(1)}, bf16[1024,128]{1,0:T(8,128)(2,1)S(1)}, u32[]{:S(2)}, u32[]{:S(2)}) collective-permute-start(bf16[1024,128]{1,0:T(8,128)(2,1)S(1)} %get-tuple-element.39), channel_id=1, source_target_pairs={{0,1},{1,0},{2,3},{3,2},{4,5},{5,4},{6,7},{7,6},{8,9},{9,8},{10,11... | collective-permute-start | bytes 786440 | tf_op jit(solution)/shard_map/ppermute | solution.py:20
  23.2 7.1 %collective-permute-start.5 = (bf16[400,128]{1,0:T(8,128)(2,1)S(1)}, bf16[400,128]{1,0:T(8,128)(2,1)S(1)}, u32[]{:S(2)}, u32[]{:S(2)}) collective-permute-start(bf16[400,128]{1,0:T(8,128)(2,1)S(1)} %get-tuple-element.32), channel_id=1, source_target_pairs={{0,5},{1,4},{2,7},{3,6},{4,1},{5,0},{6,3},{7,2},{8,13},{9,12},{10,... | collective-permute-start | bytes 307208 | tf_op jit(solution)/shard_map/ppermute | solution.py:27

commit v9 on v8

--- a/solution.py
+++ b/solution.py
@@ -323,12 +323,19 @@
         return list(outs[: len(sums)] if merges else outs)
 
 
-def add_kernel(segments, depth, rows, arrived, kept, *rest):
-    tiles_out, feats_out, total, sems = rest[-4:]
-    width = arrived.shape[-1]
+def add_kernel(parts, depth, rows, *refs):
+    tiles_out, feats_out, total, sems = refs[-4:]
+    kept = refs[len(parts)]
+    width = kept.shape[-1]
     copies = []
     begin = 0
-    for first, size in segments:
+    listed = []
+    for segments, arrived in zip(parts, refs):
+        top = begin
+        for first, size in segments:
+            listed.append((arrived, top, first, size, begin))
+            begin += size
+    for arrived, top, first, size, begin in listed:
         for tile in range(first // depth, -(-(first + size) // depth)):
             for low, high in ((0, rows), (rows, depth)):
                 low, high = max(first, tile * depth + low), min(first + size, tile * depth + high)
@@ -336,7 +343,7 @@
                     continue
                 at = begin + low - first
                 value = kept[low:high].astype(jnp.float32)
-                value += arrived[at : at + high - low].astype(jnp.float32)
+                value += arrived[at - top : at - top + high - low].astype(jnp.float32)
                 total[at : at + high - low] = value.astype(jnp.bfloat16)
                 if high - tile * depth > rows:
                     target = feats_out.at[:, pl.ds(tile * width, width)]
@@ -344,32 +351,31 @@
                     target = tiles_out.at[tile, pl.ds(low - tile * depth, high - low)]
                 source = total.at[pl.ds(at, high - low)]
                 copies.append(start(source, target, sems.at[len(copies)]))
-        begin += size
     for copy in copies:
         copy.wait()
 
 
-def added(segments, depth, rows, arrived, kept, before):
-    size, width = arrived.shape
+def added(parts, depth, rows, arrived, kept, before):
+    size, width = sum(part.shape[0] for part in arrived), kept.shape[1]
     quarter = kept.shape[0] // depth
     shapes = (
         jax.ShapeDtypeStruct((quarter, rows, width), jnp.bfloat16),
         jax.ShapeDtypeStruct((depth - rows, quarter * width), jnp.bfloat16),
     )
     return pl.pallas_call(
-        functools.partial(add_kernel, segments, depth, rows),
+        functools.partial(add_kernel, parts, depth, rows),
         out_shape=shapes,
-        in_specs=[VMEM, VMEM] + [HBM] * len(before),
+        in_specs=[VMEM] * (len(arrived) + 1) + [HBM] * len(before),
         out_specs=(HBM, HBM),
         scratch_shapes=[
             pltpu.VMEM((size, width), jnp.bfloat16),
-            pltpu.SemaphoreType.DMA((2 * quarter + len(segments),)),
+            pltpu.SemaphoreType.DMA((2 * quarter + sum(map(len, parts)),)),
         ],
-        input_output_aliases={2: 0, 3: 1} if before else {},
+        input_output_aliases={len(arrived) + at: at - 1 for at in (1, 2)} if before else {},
         compiler_params=pltpu.CompilerParams(vmem_limit_bytes=LIMIT),
         cost_estimate=LIGHT,
         name="add",
-    )(in_vmem(arrived), in_vmem(kept), *before)
+    )(*map(in_vmem, arrived), in_vmem(kept), *before)
 
 
 def per_device(features, adjacency, col_tiles, match_one, match_two):
@@ -415,8 +421,8 @@
     )
     kept = work.run(merges=keep, after=last[:1])[0]
     out = []
-    for segments, part in zip(parts, arrived):
-        out = added(segments, depth, rows, part, kept, out)
+    for low, high in ((0, 2), (2, 3), (3, 4)):
+        out = added(parts[low:high], depth, rows, arrived[low:high], kept, out)
     return out[0].reshape(quarter, slots, width, width), out[1]
 
 

time: 31.3 us -> 31.3 us (level)
  waiting for transfers between devices: 9.08 us -> 9.82 us
  Pallas kernels: 11.7 us -> 11 us
    ppermute x4, waiting for transfers between devices: 6.96 us -> 7.7 us  [crossed_over(): return lax.ppermute(value, ('blk', 'sub'), pairs)]
    pallas_call x4 -> x3, Pallas kernels: 3.34 us -> 2.61 us  [added(): pl.pallas_call(functools.partial(add_kernel, parts, depth, rows), out_sha...]
  transfers between devices with their start and end apart: 13 -> 13, of which waited for: 6 -> 6; matrix products, arithmetic and copies ran while one was open for 0% -> 0% of each run, Pallas kernels for 31% -> 29%
where the time goes in v9:
time: 31.3 us; the launch traced here: 31 us
  Pallas kernels  11 us (35%)
  waiting for transfers between devices  9.82 us (31%)
  starting transfers between devices  9.51 us (30%)
  between operations  0.72 us (2%)
    pallas_call x8, Pallas kernels, run(): pl.pallas_call(lambda *refs: work_kernel(plan, refs), out_shape=shapes, i...  8.37 us
    ppermute x4, waiting for transfers between devices, crossed_over(): return lax.ppermute(value, ('blk', 'sub'), pairs)  7.7 us
    ppermute x4, starting transfers between devices, crossed_over(): return lax.ppermute(value, ('blk', 'sub'), pairs)  6.39 us
    ppermute x9, starting transfers between devices, swapped(): return lax.ppermute(value, axis, pairs)  3.11 us
    pallas_call x3, Pallas kernels, added(): pl.pallas_call(functools.partial(add_kernel, parts, depth, rows), out_sha...  2.61 us
    ppermute x9, waiting for transfers between devices, swapped(): return lax.ppermute(value, axis, pairs)  2.12 us
  transfers between devices with their start and end apart: 13, of which 6 were waited for; matrix products, arithmetic and copies ran while one was open for 0% of the time, Pallas kernels for 29%

profile of v9, /device:TPU:0, one launch (start us, length us, event | category | flops | bytes accessed | tf_op | source)
XLA Modules:
  0.0 31.0 jit_solution(15117107475716499174)
XLA Ops:
  0.6 1.2 %work.8 = (bf16[1056,128]{1,0:T(8,128)(2,1)S(1)}, bf16[1056,128]{1,0:T(8,128)(2,1)S(1)}, s32[256,128]{1,0:T(8,128)S(1)}, s32[128,128]{1,0:T(8,128)S(1)}) custom-call(bf16[16,1024,128]{2,1,0:T(8,128)(2,1)} %bitcast.3, bf16[16,2048]{1,0:T(8,128)(2,1)} %refs_1_.7, s32[8,16]{1,0:T(8,128)} %bitcast.8, s32[256,128]{1,0:T(8,128)} %refs_3_.7, s32[128,128]{1,0:T(8,128)} %refs_4_.7), custom_call_target="tpu_custom_call" | custom-call | flops 1 | bytes 1 | tf_op jit(solution)/shard_map/work/pallas_call | solution.py:302
  1.9 0.5 %collective-permute-start = (bf16[1056,128]{1,0:T(8,128)(2,1)S(1)}, bf16[1056,128]{1,0:T(8,128)(2,1)S(1)}, u32[]{:S(2)}, u32[]{:S(2)}) collective-permute-start(bf16[1056,128]{1,0:T(8,128)(2,1)S(1)} %get-tuple-element.25.refs_7_), channel_id=1, source_target_pairs={{0,1},{1,0},{2,3},{3,2},{4,5},{5,4},{6,7},{7,6},{8,9},{9,8},{10,11... | collective-permute-start | bytes 811016 | tf_op jit(solution)/shard_map/ppermute | solution.py:20
  2.4 0.1 collective-permute-start.1
  2.5 1.1 %work.9.refs_0_ = bf16[2112,128]{1,0:T(8,128)(2,1)S(1)} custom-call(bf16[16,1024,128]{2,1,0:T(8,128)(2,1)} %bitcast.4, bf16[16,2048]{1,0:T(8,128)(2,1)} %refs_1_.7, s32[8,16]{1,0:T(8,128)} %bitcast.9, s32[256,128]{1,0:T(8,128)} %refs_3_.7, s32[128,128]{1,0:T(8,128)} %refs_4_.7, s32[256,128]{1,0:T(8,128)S(1)} %get-tuple-element.23.refs_5_, ...), custom_call_target="tpu_custom_call" | custom-call | flops 1 | bytes 1 | tf_op jit(solution)/shard_map/work/pallas_call | solution.py:302
  3.6 0.0 collective-permute-done.refs_1_
  3.6 0.3 %work.10.refs_3_ = bf16[528,128]{1,0:T(8,128)(2,1)S(1)} custom-call(bf16[2112,128]{1,0:T(8,128)(2,1)S(1)} %work.9.refs_0_, bf16[1056,128]{1,0:T(8,128)(2,1)S(1)} %collective-permute-done.refs_1_), custom_call_target="tpu_custom_call" | custom-call | flops 1 | bytes 1 | tf_op jit(solution)/shard_map/work/pallas_call | solution.py:302
  3.9 2.7 %collective-permute-start.2 = (bf16[528,128]{1,0:T(8,128)(2,1)S(1)}, bf16[528,128]{1,0:T(8,128)(2,1)S(1)}, u32[]{:S(2)}, u32[]{:S(2)}) collective-permute-start(bf16[528,128]{1,0:T(8,128)(2,1)S(1)} %work.10.refs_3_), channel_id=1, source_target_pairs={{0,5},{1,4},{2,7},{3,6},{4,1},{5,0},{6,3},{7,2},{8,13},{9,12},{10,... | collective-permute-start | bytes 405512 | tf_op jit(solution)/shard_map/ppermute | solution.py:27
  6.6 0.0 collective-permute-done.1.refs_2_
  6.6 0.6 %work.11.refs_7_ = bf16[1552,128]{1,0:T(8,128)(2,1)S(1)} custom-call(bf16[2112,128]{1,0:T(8,128)(2,1)S(1)} %work.9.refs_0_, bf16[1056,128]{1,0:T(8,128)(2,1)S(1)} %collective-permute-done.refs_1_, bf16[1056,128]{1,0:T(8,128)(2,1)S(1)} %collective-permute-done.1.refs_2_, bf16[528,128]{1,0:T(8,128)(2,1)S(1)} %work.10.refs_3_), custom_call_target="tpu_custom_call" | custom-call | flops 1 | bytes 1 | tf_op jit(solution)/shard_map/work/pallas_call | solution.py:302
  7.2 0.1 collective-permute-start.6
  7.3 3.3 %collective-permute-done.2.refs_8_.refs_0_ = bf16[528,128]{1,0:T(8,128)(2,1)S(1)} collective-permute-done((bf16[528,128]{1,0:T(8,128)(2,1)S(1)}, bf16[528,128]{1,0:T(8,128)(2,1)S(1)}, u32[]{:S(2)}, u32[]{:S(2)}) %collective-permute-start.2) | collective-permute-done | bytes 135200 | tf_op jit(solution)/shard_map/ppermute | solution.py:27
  10.6 1.3 %work.12 = (bf16[1088,128]{1,0:T(8,128)(2,1)S(1)}, bf16[1024,128]{1,0:T(8,128)(2,1)S(1)}, bf16[2112,128]{1,0:T(8,128)(2,1)S(1)}) custom-call(bf16[16,1024,128]{2,1,0:T(8,128)(2,1)} %bitcast.5, bf16[16,2048]{1,0:T(8,128)(2,1)} %refs_1_.7, s32[8,16]{1,0:T(8,128)} %bitcast.10, s32[256,128]{1,0:T(8,128)} %refs_3_.7, s32[128,128]{1,0:T(8,128)} %refs_4_.7, ...), custom_call_target="tpu_custom_call" | custom-call | flops 1 | bytes 1 | tf_op jit(solution)/shard_map/work/pallas_call | solution.py:302
  11.9 0.7 %collective-permute-start.3 = (bf16[1088,128]{1,0:T(8,128)(2,1)S(1)}, bf16[1088,128]{1,0:T(8,128)(2,1)S(1)}, u32[]{:S(2)}, u32[]{:S(2)}) collective-permute-start(bf16[1088,128]{1,0:T(8,128)(2,1)S(1)} %get-tuple-element.28), channel_id=1, source_target_pairs={{0,1},{1,0},{2,3},{3,2},{4,5},{5,4},{6,7},{7,6},{8,9},{9,8},{10,11... | collective-permute-start | bytes 835592 | tf_op jit(solution)/shard_map/ppermute | solution.py:20
  12.7 0.1 collective-permute-start.4
  12.7 1.5 %collective-permute-done.4.refs_2_ = bf16[1024,128]{1,0:T(8,128)(2,1)S(1)} collective-permute-done((bf16[1024,128]{1,0:T(8,128)(2,1)S(1)}, bf16[1024,128]{1,0:T(8,128)(2,1)S(1)}, u32[]{:S(2)}, u32[]{:S(2)}) %collective-permute-start.4) | collective-permute-done | bytes 262176 | tf_op jit(solution)/shard_map/ppermute | solution.py:20
  14.2 0.0 collective-permute-done.3.refs_1_
  14.2 0.7 %work.13 = (bf16[1680,128]{1,0:T(8,128)(2,1)S(1)}, bf16[400,128]{1,0:T(8,128)(2,1)S(1)}) custom-call(bf16[2112,128]{1,0:T(8,128)(2,1)S(1)} %get-tuple-element.27.refs_0_, bf16[1088,128]{1,0:T(8,128)(2,1)S(1)} %collective-permute-done.3.refs_1_, bf16[1024,128]{1,0:T(8,128)(2,1)S(1)} %collective-permute-done.4.refs_2_), custom_call_target="tpu_custom_call" | custom-call | flops 1 | bytes 1 | tf_op jit(solution)/shard_map/work/pallas_call | solution.py:302
  14.9 2.0 %collective-permute-start.12 = (bf16[1680,128]{1,0:T(8,128)(2,1)S(1)}, bf16[1680,128]{1,0:T(8,128)(2,1)S(1)}, u32[]{:S(2)}, u32[]{:S(2)}) collective-permute-start(bf16[1680,128]{1,0:T(8,128)(2,1)S(1)} %get-tuple-element.31.refs_7_), channel_id=1, source_target_pairs={{0,5},{1,4},{2,7},{3,6},{4,1},{5,0},{6,3},{7,2},{8,13},{9,12},{10,... | collective-permute-start | bytes 1290248 | tf_op jit(solution)/shard_map/ppermute | solution.py:27
  16.9 2.2 %collective-permute-done.6.refs_8_.refs_1_ = bf16[1552,128]{1,0:T(8,128)(2,1)S(1)} collective-permute-done((bf16[1552,128]{1,0:T(8,128)(2,1)S(1)}, bf16[1552,128]{1,0:T(8,128)(2,1)S(1)}, u32[]{:S(2)}, u32[]{:S(2)}) %collective-permute-start.6) | collective-permute-done | bytes 397344 | tf_op jit(solution)/shard_map/ppermute | solution.py:27
  19.1 1.7 %work.14 = (bf16[128,128]{1,0:T(8,128)(2,1)S(1)}, bf16[1024,128]{1,0:T(8,128)(2,1)S(1)}, bf16[1024,128]{1,0:T(8,128)(2,1)S(1)}, bf16[1024,128]{1,0:T(8,128)(2,1)...) custom-call(bf16[16,1024,128]{2,1,0:T(8,128)(2,1)} %bitcast.6, bf16[16,2048]{1,0:T(8,128)(2,1)} %refs_1_.7, ...), custom_call_target="tpu_custom_call" | custom-call | flops 1 | bytes 1 | tf_op jit(solution)/shard_map/work/pallas_call | solution.py:302
  20.9 0.7 %collective-permute-start.7 = (bf16[1024,128]{1,0:T(8,128)(2,1)S(1)}, bf16[1024,128]{1,0:T(8,128)(2,1)S(1)}, u32[]{:S(2)}, u32[]{:S(2)}) collective-permute-start(bf16[1024,128]{1,0:T(8,128)(2,1)S(1)} %get-tuple-element.33), channel_id=1, source_target_pairs={{0,1},{1,0},{2,3},{3,2},{4,5},{5,4},{6,7},{7,6},{8,9},{9,8},{10,11... | collective-permute-start | bytes 786440 | tf_op jit(solution)/shard_map/ppermute | solution.py:20
  21.6 0.1 collective-permute-start.8
  21.7 0.4 %collective-permute-start.9 = (bf16[1024,128]{1,0:T(8,128)(2,1)S(1)}, bf16[1024,128]{1,0:T(8,128)(2,1)S(1)}, u32[]{:S(2)}, u32[]{:S(2)}) collective-permute-start(bf16[1024,128]{1,0:T(8,128)(2,1)S(1)} %get-tuple-element.35), channel_id=1, source_target_pairs={{0,1},{1,0},{2,3},{3,2},{4,5},{5,4},{6,7},{7,6},{8,9},{9,8},{10,11... | collective-permute-start | bytes 786440 | tf_op jit(solution)/shard_map/ppermute | solution.py:20
  22.1 0.1 collective-permute-start.10
  22.2 0.6 %collective-permute-done.8.refs_2_ = bf16[128,128]{1,0:T(8,128)(2,1)S(1)} collective-permute-done((bf16[128,128]{1,0:T(8,128)(2,1)S(1)}, bf16[128,128]{1,0:T(8,128)(2,1)S(1)}, u32[]{:S(2)}, u32[]{:S(2)}) %collective-permute-start.8) | collective-permute-done | bytes 32800 | tf_op jit(solution)/shard_map/ppermute | solution.py:20
  22.8 0.4 %collective-permute-start.11 = (bf16[1024,128]{1,0:T(8,128)(2,1)S(1)}, bf16[1024,128]{1,0:T(8,128)(2,1)S(1)}, u32[]{:S(2)}, u32[]{:S(2)}) collective-permute-start(bf16[1024,128]{1,0:T(8,128)(2,1)S(1)} %get-tuple-element.37), channel_id=1, source_target_pairs={{0,1},{1,0},{2,3},{3,2},{4,5},{5,4},{6,7},{7,6},{8,9},{9,8},{10,11... | collective-permute-start | bytes 786440 | tf_op jit(solution)/shard_map/ppermute | solution.py:20
  23.2 0.0 collective-permute-done.7.refs_1_
  23.2 1.7 %collective-permute-start.5 = (bf16[400,128]{1,0:T(8,128)(2,1)S(1)}, bf16[400,128]{1,0:T(8,128)(2,1)S(1)}, u32[]{:S(2)}, u32[]{:S(2)}) collective-permute-start(bf16[400,128]{1,0:T(8,128)(2,1)S(1)} %get-tuple-element.30), channel_id=1, source_target_pairs={{0,5},{1,4},{2,7},{3,6},{4,1},{5,0},{6,3},{7,2},{8,13},{9,12},{10,... | collective-permute-start | bytes 307208 | tf_op jit(solution)/shard_map/ppermute | solution.py:27
  24.8 0.0 collective-permute-done.9.refs_3_
  24.8 0.0 collective-permute-done.10.refs_4_
  24.8 0.0 collective-permute-done.11.refs_5_
  24.9 1.3 %work.15.refs_2_.refs_1_ = bf16[4160,128]{1,0:T(8,128)(2,1)S(1)} custom-call(bf16[4224,128]{1,0:T(8,128)(2,1)S(1)} %get-tuple-element.32.refs_0_, bf16[1024,128]{1,0:T(8,128)(2,1)S(1)} %collective-permute-done.7.refs_1_, bf16[128,128]{1,0:T(8,128)(2,1)S(1)} %collective-permute-done.8.refs_2_, bf16[1024,128]{1,0:T(8,128)(2,1)S(1)} %collective-permute-done.9.refs_3_, ...), custom_call_target="tpu_custom_call" | custom-call | flops 1 | bytes 1 | tf_op jit(solution)/shard_map/work/pallas_call | solution.py:302
  26.1 0.9 %add.3 = (bf16[4,1024,128]{2,1,0:T(8,128)(2,1)}, bf16[16,512]{1,0:T(8,128)(2,1)}) custom-call(bf16[528,128]{1,0:T(8,128)(2,1)S(1)} %collective-permute-done.2.refs_8_.refs_0_, bf16[1552,128]{1,0:T(8,128)(2,1)S(1)} %collective-permute-done.6.refs_8_.refs_1_, bf16[4160,128]{1,0:T(8,128)(2,1)S(1)} %work.15.refs_2_.refs_1_), custom_call_target="tpu_custom_call" | custom-call | flops 1 | bytes 1 | tf_op jit(solution)/shard_map/add/pallas_call | solution.py:365
  27.1 1.2 %collective-permute-done.12.refs_0_ = bf16[1680,128]{1,0:T(8,128)(2,1)S(1)} collective-permute-done((bf16[1680,128]{1,0:T(8,128)(2,1)S(1)}, bf16[1680,128]{1,0:T(8,128)(2,1)S(1)}, u32[]{:S(2)}, u32[]{:S(2)}) %collective-permute-start.12) | collective-permute-done | bytes 430112 | tf_op jit(solution)/shard_map/ppermute | solution.py:27
  28.3 0.9 %add.4 = (bf16[4,1024,128]{2,1,0:T(8,128)(2,1)}, bf16[16,512]{1,0:T(8,128)(2,1)}) custom-call(bf16[1680,128]{1,0:T(8,128)(2,1)S(1)} %collective-permute-done.12.refs_0_, bf16[4160,128]{1,0:T(8,128)(2,1)S(1)} %work.15.refs_2_.refs_1_, bf16[4,1024,128]{2,1,0:T(8,128)(2,1)} %get-tuple-element.38.refs_2_, ...), custom_call_target="tpu_custom_call", output_to_operand_aliasing={{0}: (2, {}), {1}: (3, {})} | custom-call | flops 1 | bytes 1 | tf_op jit(solution)/shard_map/add/pallas_call | solution.py:365
  29.2 1.0 %collective-permute-done.5.refs_0_ = bf16[400,128]{1,0:T(8,128)(2,1)S(1)} collective-permute-done((bf16[400,128]{1,0:T(8,128)(2,1)S(1)}, bf16[400,128]{1,0:T(8,128)(2,1)S(1)}, u32[]{:S(2)}, u32[]{:S(2)}) %collective-permute-start.5) | collective-permute-done | bytes 102432 | tf_op jit(solution)/shard_map/ppermute | solution.py:27
  30.3 0.7 %add.5 = (bf16[4,1024,128]{2,1,0:T(8,128)(2,1)}, bf16[16,512]{1,0:T(8,128)(2,1)}) custom-call(bf16[400,128]{1,0:T(8,128)(2,1)S(1)} %collective-permute-done.5.refs_0_, bf16[4160,128]{1,0:T(8,128)(2,1)S(1)} %work.15.refs_2_.refs_1_, bf16[4,1024,128]{2,1,0:T(8,128)(2,1)} %get-tuple-element.40.refs_2_, ...), custom_call_target="tpu_custom_call", output_to_operand_aliasing={{0}: (2, {}), {1}: (3, {})} | custom-call | flops 1 | bytes 1 | tf_op jit(solution)/shard_map/add/pallas_call | solution.py:365
Async XLA Ops:
  1.9 1.7 %collective-permute-start = (bf16[1056,128]{1,0:T(8,128)(2,1)S(1)}, bf16[1056,128]{1,0:T(8,128)(2,1)S(1)}, u32[]{:S(2)}, u32[]{:S(2)}) collective-permute-start(bf16[1056,128]{1,0:T(8,128)(2,1)S(1)} %get-tuple-element.25.refs_7_), channel_id=1, source_target_pairs={{0,1},{1,0},{2,3},{3,2},{4,5},{5,4},{6,7},{7,6},{8,9},{9,8},{10,11... | collective-permute-start | bytes 811016 | tf_op jit(solution)/shard_map/ppermute | solution.py:20
  2.4 4.2 %collective-permute-start.1 = (bf16[1056,128]{1,0:T(8,128)(2,1)S(1)}, bf16[1056,128]{1,0:T(8,128)(2,1)S(1)}, u32[]{:S(2)}, u32[]{:S(2)}) collective-permute-start(bf16[1056,128]{1,0:T(8,128)(2,1)S(1)} %get-tuple-element.26), channel_id=1, source_target_pairs={{0,1},{1,0},{2,3},{3,2},{4,5},{5,4},{6,7},{7,6},{8,9},{9,8},{10,11... | collective-permute-start | bytes 811016 | tf_op jit(solution)/shard_map/ppermute | solution.py:20
  3.9 6.6 %collective-permute-start.2 = (bf16[528,128]{1,0:T(8,128)(2,1)S(1)}, bf16[528,128]{1,0:T(8,128)(2,1)S(1)}, u32[]{:S(2)}, u32[]{:S(2)}) collective-permute-start(bf16[528,128]{1,0:T(8,128)(2,1)S(1)} %work.10.refs_3_), channel_id=1, source_target_pairs={{0,5},{1,4},{2,7},{3,6},{4,1},{5,0},{6,3},{7,2},{8,13},{9,12},{10,... | collective-permute-start | bytes 405512 | tf_op jit(solution)/shard_map/ppermute | solution.py:27
  7.2 11.9 %collective-permute-start.6 = (bf16[1552,128]{1,0:T(8,128)(2,1)S(1)}, bf16[1552,128]{1,0:T(8,128)(2,1)S(1)}, u32[]{:S(2)}, u32[]{:S(2)}) collective-permute-start(bf16[1552,128]{1,0:T(8,128)(2,1)S(1)} %work.11.refs_7_), channel_id=1, source_target_pairs={{0,5},{1,4},{2,7},{3,6},{4,1},{5,0},{6,3},{7,2},{8,13},{9,12},{10,... | collective-permute-start | bytes 1191944 | tf_op jit(solution)/shard_map/ppermute | solution.py:27
  11.9 2.3 %collective-permute-start.3 = (bf16[1088,128]{1,0:T(8,128)(2,1)S(1)}, bf16[1088,128]{1,0:T(8,128)(2,1)S(1)}, u32[]{:S(2)}, u32[]{:S(2)}) collective-permute-start(bf16[1088,128]{1,0:T(8,128)(2,1)S(1)} %get-tuple-element.28), channel_id=1, source_target_pairs={{0,1},{1,0},{2,3},{3,2},{4,5},{5,4},{6,7},{7,6},{8,9},{9,8},{10,11... | collective-permute-start | bytes 835592 | tf_op jit(solution)/shard_map/ppermute | solution.py:20
  12.7 1.6 %collective-permute-start.4 = (bf16[1024,128]{1,0:T(8,128)(2,1)S(1)}, bf16[1024,128]{1,0:T(8,128)(2,1)S(1)}, u32[]{:S(2)}, u32[]{:S(2)}) collective-permute-start(bf16[1024,128]{1,0:T(8,128)(2,1)S(1)} %get-tuple-element.29), channel_id=1, source_target_pairs={{0,1},{1,0},{2,3},{3,2},{4,5},{5,4},{6,7},{7,6},{8,9},{9,8},{10,11... | collective-permute-start | bytes 786440 | tf_op jit(solution)/shard_map/ppermute | solution.py:20
  14.9 13.4 %collective-permute-start.12 = (bf16[1680,128]{1,0:T(8,128)(2,1)S(1)}, bf16[1680,128]{1,0:T(8,128)(2,1)S(1)}, u32[]{:S(2)}, u32[]{:S(2)}) collective-permute-start(bf16[1680,128]{1,0:T(8,128)(2,1)S(1)} %get-tuple-element.31.refs_7_), channel_id=1, source_target_pairs={{0,5},{1,4},{2,7},{3,6},{4,1},{5,0},{6,3},{7,2},{8,13},{9,12},{10,... | collective-permute-start | bytes 1290248 | tf_op jit(solution)/shard_map/ppermute | solution.py:27
  20.9 2.3 %collective-permute-start.7 = (bf16[1024,128]{1,0:T(8,128)(2,1)S(1)}, bf16[1024,128]{1,0:T(8,128)(2,1)S(1)}, u32[]{:S(2)}, u32[]{:S(2)}) collective-permute-start(bf16[1024,128]{1,0:T(8,128)(2,1)S(1)} %get-tuple-element.33), channel_id=1, source_target_pairs={{0,1},{1,0},{2,3},{3,2},{4,5},{5,4},{6,7},{7,6},{8,9},{9,8},{10,11... | collective-permute-start | bytes 786440 | tf_op jit(solution)/shard_map/ppermute | solution.py:20
  21.6 1.2 %collective-permute-start.8 = (bf16[128,128]{1,0:T(8,128)(2,1)S(1)}, bf16[128,128]{1,0:T(8,128)(2,1)S(1)}, u32[]{:S(2)}, u32[]{:S(2)}) collective-permute-start(bf16[128,128]{1,0:T(8,128)(2,1)S(1)} %get-tuple-element.34.refs_6_), channel_id=1, source_target_pairs={{0,1},{1,0},{2,3},{3,2},{4,5},{5,4},{6,7},{7,6},{8,9},{9,8},{10,11... | collective-permute-start | bytes 98312 | tf_op jit(solution)/shard_map/ppermute | solution.py:20
  21.7 3.2 %collective-permute-start.9 = (bf16[1024,128]{1,0:T(8,128)(2,1)S(1)}, bf16[1024,128]{1,0:T(8,128)(2,1)S(1)}, u32[]{:S(2)}, u32[]{:S(2)}) collective-permute-start(bf16[1024,128]{1,0:T(8,128)(2,1)S(1)} %get-tuple-element.35), channel_id=1, source_target_pairs={{0,1},{1,0},{2,3},{3,2},{4,5},{5,4},{6,7},{7,6},{8,9},{9,8},{10,11... | collective-permute-start | bytes 786440 | tf_op jit(solution)/shard_map/ppermute | solution.py:20
  22.1 2.7 %collective-permute-start.10 = (bf16[1024,128]{1,0:T(8,128)(2,1)S(1)}, bf16[1024,128]{1,0:T(8,128)(2,1)S(1)}, u32[]{:S(2)}, u32[]{:S(2)}) collective-permute-start(bf16[1024,128]{1,0:T(8,128)(2,1)S(1)} %get-tuple-element.36), channel_id=1, source_target_pairs={{0,1},{1,0},{2,3},{3,2},{4,5},{5,4},{6,7},{7,6},{8,9},{9,8},{10,11... | collective-permute-start | bytes 786440 | tf_op jit(solution)/shard_map/ppermute | solution.py:20
  22.8 2.1 %collective-permute-start.11 = (bf16[1024,128]{1,0:T(8,128)(2,1)S(1)}, bf16[1024,128]{1,0:T(8,128)(2,1)S(1)}, u32[]{:S(2)}, u32[]{:S(2)}) collective-permute-start(bf16[1024,128]{1,0:T(8,128)(2,1)S(1)} %get-tuple-element.37), channel_id=1, source_target_pairs={{0,1},{1,0},{2,3},{3,2},{4,5},{5,4},{6,7},{7,6},{8,9},{9,8},{10,11... | collective-permute-start | bytes 786440 | tf_op jit(solution)/shard_map/ppermute | solution.py:20
  23.2 7.1 %collective-permute-start.5 = (bf16[400,128]{1,0:T(8,128)(2,1)S(1)}, bf16[400,128]{1,0:T(8,128)(2,1)S(1)}, u32[]{:S(2)}, u32[]{:S(2)}) collective-permute-start(bf16[400,128]{1,0:T(8,128)(2,1)S(1)} %get-tuple-element.30), channel_id=1, source_target_pairs={{0,5},{1,4},{2,7},{3,6},{4,1},{5,0},{6,3},{7,2},{8,13},{9,12},{10,... | collective-permute-start | bytes 307208 | tf_op jit(solution)/shard_map/ppermute | solution.py:27

commit v10 on v8

--- a/solution.py
+++ b/solution.py
@@ -411,7 +411,7 @@
     )
     parcels = merge(send[2:], [2, 3], [])
     last = work.run(
-        keys=keep, leaving=keep, apart=[1] * quarter, after=parcels[:1] + arrived[1:2]
+        keys=keep, leaving=keep, apart=[1] * quarter, joint=True, after=parcels[:1] + arrived[1:2]
     )
     kept = work.run(merges=keep, after=last[:1])[0]
     out = []

time: 31.3 us -> 31.3 us (level)
    ppermute x9 -> x8, starting transfers between devices: 3.11 us -> 2.73 us  [swapped(): return lax.ppermute(value, axis, pairs)]
    ppermute x9 -> x8, waiting for transfers between devices: 2.12 us -> 2.07 us  [swapped(): return lax.ppermute(value, axis, pairs)]
  transfers between devices with their start and end apart: 13 -> 12, of which waited for: 6 -> 6; matrix products, arithmetic and copies ran while one was open for 0% -> 0% of each run, Pallas kernels for 31% -> 31%
where the time goes in v10:
time: 31.3 us; the launch traced here: 31 us
  Pallas kernels  11.7 us (37%)
  starting transfers between devices  9.37 us (30%)
  waiting for transfers between devices  9.22 us (29%)
  between operations  0.73 us (2%)
    pallas_call x8, Pallas kernels, run(): pl.pallas_call(lambda *refs: work_kernel(plan, refs), out_shape=shapes, i...  8.37 us
    ppermute x4, waiting for transfers between devices, crossed_over(): return lax.ppermute(value, ('blk', 'sub'), pairs)  7.15 us
    ppermute x4, starting transfers between devices, crossed_over(): return lax.ppermute(value, ('blk', 'sub'), pairs)  6.64 us
    pallas_call x4, Pallas kernels, added(): pl.pallas_call(functools.partial(add_kernel, segments, depth, rows), out_...  3.34 us
    ppermute x8, starting transfers between devices, swapped(): return lax.ppermute(value, axis, pairs)  2.73 us
    ppermute x8, waiting for transfers between devices, swapped(): return lax.ppermute(value, axis, pairs)  2.07 us
  transfers between devices with their start and end apart: 12, of which 6 were waited for; matrix products, arithmetic and copies ran while one was open for 0% of the time, Pallas kernels for 31%

profile of v10, /device:TPU:0, one launch (start us, length us, event | category | flops | bytes accessed | tf_op | source)
XLA Modules:
  0.0 31.0 jit_solution(9219012415973619906)
XLA Ops:
  0.6 1.2 %work.8 = (bf16[1056,128]{1,0:T(8,128)(2,1)S(1)}, bf16[1056,128]{1,0:T(8,128)(2,1)S(1)}, s32[256,128]{1,0:T(8,128)S(1)}, s32[128,128]{1,0:T(8,128)S(1)}) custom-call(bf16[16,1024,128]{2,1,0:T(8,128)(2,1)} %bitcast.3, bf16[16,2048]{1,0:T(8,128)(2,1)} %refs_1_.7, s32[8,16]{1,0:T(8,128)} %bitcast.8, s32[256,128]{1,0:T(8,128)} %refs_3_.7, s32[128,128]{1,0:T(8,128)} %refs_4_.7), custom_call_target="tpu_custom_call" | custom-call | flops 1 | bytes 1 | tf_op jit(solution)/shard_map/work/pallas_call | solution.py:302
  1.9 0.5 %collective-permute-start = (bf16[1056,128]{1,0:T(8,128)(2,1)S(1)}, bf16[1056,128]{1,0:T(8,128)(2,1)S(1)}, u32[]{:S(2)}, u32[]{:S(2)}) collective-permute-start(bf16[1056,128]{1,0:T(8,128)(2,1)S(1)} %get-tuple-element.26.refs_7_), channel_id=1, source_target_pairs={{0,1},{1,0},{2,3},{3,2},{4,5},{5,4},{6,7},{7,6},{8,9},{9,8},{10,11... | collective-permute-start | bytes 811016 | tf_op jit(solution)/shard_map/ppermute | solution.py:20
  2.4 0.1 collective-permute-start.1
  2.5 1.1 %work.9.refs_0_ = bf16[2112,128]{1,0:T(8,128)(2,1)S(1)} custom-call(bf16[16,1024,128]{2,1,0:T(8,128)(2,1)} %bitcast.4, bf16[16,2048]{1,0:T(8,128)(2,1)} %refs_1_.7, s32[8,16]{1,0:T(8,128)} %bitcast.9, s32[256,128]{1,0:T(8,128)} %refs_3_.7, s32[128,128]{1,0:T(8,128)} %refs_4_.7, s32[256,128]{1,0:T(8,128)S(1)} %get-tuple-element.24.refs_5_, ...), custom_call_target="tpu_custom_call" | custom-call | flops 1 | bytes 1 | tf_op jit(solution)/shard_map/work/pallas_call | solution.py:302
  3.6 0.0 collective-permute-done.refs_1_
  3.6 0.3 %work.10.refs_3_ = bf16[528,128]{1,0:T(8,128)(2,1)S(1)} custom-call(bf16[2112,128]{1,0:T(8,128)(2,1)S(1)} %work.9.refs_0_, bf16[1056,128]{1,0:T(8,128)(2,1)S(1)} %collective-permute-done.refs_1_), custom_call_target="tpu_custom_call" | custom-call | flops 1 | bytes 1 | tf_op jit(solution)/shard_map/work/pallas_call | solution.py:302
  3.9 2.7 %collective-permute-start.2 = (bf16[528,128]{1,0:T(8,128)(2,1)S(1)}, bf16[528,128]{1,0:T(8,128)(2,1)S(1)}, u32[]{:S(2)}, u32[]{:S(2)}) collective-permute-start(bf16[528,128]{1,0:T(8,128)(2,1)S(1)} %work.10.refs_3_), channel_id=1, source_target_pairs={{0,5},{1,4},{2,7},{3,6},{4,1},{5,0},{6,3},{7,2},{8,13},{9,12},{10,... | collective-permute-start | bytes 405512 | tf_op jit(solution)/shard_map/ppermute | solution.py:27
  6.6 0.0 collective-permute-done.1.refs_2_
  6.6 0.6 %work.11.refs_7_ = bf16[1552,128]{1,0:T(8,128)(2,1)S(1)} custom-call(bf16[2112,128]{1,0:T(8,128)(2,1)S(1)} %work.9.refs_0_, bf16[1056,128]{1,0:T(8,128)(2,1)S(1)} %collective-permute-done.refs_1_, bf16[1056,128]{1,0:T(8,128)(2,1)S(1)} %collective-permute-done.1.refs_2_, bf16[528,128]{1,0:T(8,128)(2,1)S(1)} %work.10.refs_3_), custom_call_target="tpu_custom_call" | custom-call | flops 1 | bytes 1 | tf_op jit(solution)/shard_map/work/pallas_call | solution.py:302
  7.2 0.1 collective-permute-start.6
  7.3 3.2 %collective-permute-done.2.refs_8_.arrived = bf16[528,128]{1,0:T(8,128)(2,1)S(1)} collective-permute-done((bf16[528,128]{1,0:T(8,128)(2,1)S(1)}, bf16[528,128]{1,0:T(8,128)(2,1)S(1)}, u32[]{:S(2)}, u32[]{:S(2)}) %collective-permute-start.2) | collective-permute-done | bytes 135200 | tf_op jit(solution)/shard_map/ppermute | solution.py:27
  10.6 1.3 %work.12 = (bf16[1088,128]{1,0:T(8,128)(2,1)S(1)}, bf16[1024,128]{1,0:T(8,128)(2,1)S(1)}, bf16[2112,128]{1,0:T(8,128)(2,1)S(1)}) custom-call(bf16[16,1024,128]{2,1,0:T(8,128)(2,1)} %bitcast.5, bf16[16,2048]{1,0:T(8,128)(2,1)} %refs_1_.7, s32[8,16]{1,0:T(8,128)} %bitcast.10, s32[256,128]{1,0:T(8,128)} %refs_3_.7, s32[128,128]{1,0:T(8,128)} %refs_4_.7, ...), custom_call_target="tpu_custom_call" | custom-call | flops 1 | bytes 1 | tf_op jit(solution)/shard_map/work/pallas_call | solution.py:302
  11.9 0.7 %collective-permute-start.3 = (bf16[1088,128]{1,0:T(8,128)(2,1)S(1)}, bf16[1088,128]{1,0:T(8,128)(2,1)S(1)}, u32[]{:S(2)}, u32[]{:S(2)}) collective-permute-start(bf16[1088,128]{1,0:T(8,128)(2,1)S(1)} %get-tuple-element.29), channel_id=1, source_target_pairs={{0,1},{1,0},{2,3},{3,2},{4,5},{5,4},{6,7},{7,6},{8,9},{9,8},{10,11... | collective-permute-start | bytes 835592 | tf_op jit(solution)/shard_map/ppermute | solution.py:20
  12.7 0.1 collective-permute-start.4
  12.7 1.5 %collective-permute-done.4.refs_2_ = bf16[1024,128]{1,0:T(8,128)(2,1)S(1)} collective-permute-done((bf16[1024,128]{1,0:T(8,128)(2,1)S(1)}, bf16[1024,128]{1,0:T(8,128)(2,1)S(1)}, u32[]{:S(2)}, u32[]{:S(2)}) %collective-permute-start.4) | collective-permute-done | bytes 262176 | tf_op jit(solution)/shard_map/ppermute | solution.py:20
  14.2 0.0 collective-permute-done.3.refs_1_
  14.2 0.7 %work.13 = (bf16[1680,128]{1,0:T(8,128)(2,1)S(1)}, bf16[400,128]{1,0:T(8,128)(2,1)S(1)}) custom-call(bf16[2112,128]{1,0:T(8,128)(2,1)S(1)} %get-tuple-element.28.refs_0_, bf16[1088,128]{1,0:T(8,128)(2,1)S(1)} %collective-permute-done.3.refs_1_, bf16[1024,128]{1,0:T(8,128)(2,1)S(1)} %collective-permute-done.4.refs_2_), custom_call_target="tpu_custom_call" | custom-call | flops 1 | bytes 1 | tf_op jit(solution)/shard_map/work/pallas_call | solution.py:302
  14.9 2.0 %collective-permute-start.11 = (bf16[1680,128]{1,0:T(8,128)(2,1)S(1)}, bf16[1680,128]{1,0:T(8,128)(2,1)S(1)}, u32[]{:S(2)}, u32[]{:S(2)}) collective-permute-start(bf16[1680,128]{1,0:T(8,128)(2,1)S(1)} %get-tuple-element.32.refs_7_), channel_id=1, source_target_pairs={{0,5},{1,4},{2,7},{3,6},{4,1},{5,0},{6,3},{7,2},{8,13},{9,12},{10,... | collective-permute-start | bytes 1290248 | tf_op jit(solution)/shard_map/ppermute | solution.py:27
  16.9 2.2 %collective-permute-done.6.refs_8_.arrived = bf16[1552,128]{1,0:T(8,128)(2,1)S(1)} collective-permute-done((bf16[1552,128]{1,0:T(8,128)(2,1)S(1)}, bf16[1552,128]{1,0:T(8,128)(2,1)S(1)}, u32[]{:S(2)}, u32[]{:S(2)}) %collective-permute-start.6) | collective-permute-done | bytes 397344 | tf_op jit(solution)/shard_map/ppermute | solution.py:27
  19.1 1.7 %work.14 = (bf16[1152,128]{1,0:T(8,128)(2,1)S(1)}, bf16[1024,128]{1,0:T(8,128)(2,1)S(1)}, bf16[1024,128]{1,0:T(8,128)(2,1)S(1)}, bf16[1024,128]{1,0:T(8,128)(2,1)S(1)}, bf16[4224,128]{1,0:T(8,128)(2,1)S(1)}) custom-call(bf16[16,1024,128]{2,1,0:T(8,128)(2,1)} %bitcast.6, bf16[16,2048]{1,0:T(8,128)(2,1)} %refs_1_.7, s32[8,16]{1,0:T(8,128)} %bitcast.11, ...), custom_call_target="tpu_custom_call" | custom-call | flops 1 | bytes 1 | tf_op jit(solution)/shard_map/work/pallas_call | solution.py:302
  20.9 0.7 %collective-permute-start.8 = (bf16[1024,128]{1,0:T(8,128)(2,1)S(1)}, bf16[1024,128]{1,0:T(8,128)(2,1)S(1)}, u32[]{:S(2)}, u32[]{:S(2)}) collective-permute-start(bf16[1024,128]{1,0:T(8,128)(2,1)S(1)} %get-tuple-element.35), channel_id=1, source_target_pairs={{0,1},{1,0},{2,3},{3,2},{4,5},{5,4},{6,7},{7,6},{8,9},{9,8},{10,11... | collective-permute-start | bytes 786440 | tf_op jit(solution)/shard_map/ppermute | solution.py:20
  21.6 0.1 collective-permute-start.7
  21.7 0.4 %collective-permute-start.9 = (bf16[1024,128]{1,0:T(8,128)(2,1)S(1)}, bf16[1024,128]{1,0:T(8,128)(2,1)S(1)}, u32[]{:S(2)}, u32[]{:S(2)}) collective-permute-start(bf16[1024,128]{1,0:T(8,128)(2,1)S(1)} %get-tuple-element.36), channel_id=1, source_target_pairs={{0,1},{1,0},{2,3},{3,2},{4,5},{5,4},{6,7},{7,6},{8,9},{9,8},{10,11... | collective-permute-start | bytes 786440 | tf_op jit(solution)/shard_map/ppermute | solution.py:20
  22.1 0.1 collective-permute-start.10
  22.2 0.6 %collective-permute-done.8.refs_2_ = bf16[1024,128]{1,0:T(8,128)(2,1)S(1)} collective-permute-done((bf16[1024,128]{1,0:T(8,128)(2,1)S(1)}, bf16[1024,128]{1,0:T(8,128)(2,1)S(1)}, u32[]{:S(2)}, u32[]{:S(2)}) %collective-permute-start.8) | collective-permute-done | bytes 262176 | tf_op jit(solution)/shard_map/ppermute | solution.py:20
  22.7 1.9 %collective-permute-start.5 = (bf16[400,128]{1,0:T(8,128)(2,1)S(1)}, bf16[400,128]{1,0:T(8,128)(2,1)S(1)}, u32[]{:S(2)}, u32[]{:S(2)}) collective-permute-start(bf16[400,128]{1,0:T(8,128)(2,1)S(1)} %get-tuple-element.31), channel_id=1, source_target_pairs={{0,5},{1,4},{2,7},{3,6},{4,1},{5,0},{6,3},{7,2},{8,13},{9,12},{10,... | collective-permute-start | bytes 307208 | tf_op jit(solution)/shard_map/ppermute | solution.py:27
  24.7 0.0 collective-permute-done.9.refs_3_
  24.7 0.0 collective-permute-done.10.refs_4_
  24.7 0.0 collective-permute-done.7.refs_1_
  24.7 1.3 %work.15.kept = bf16[4160,128]{1,0:T(8,128)(2,1)S(1)} custom-call(bf16[4224,128]{1,0:T(8,128)(2,1)S(1)} %get-tuple-element.33.refs_0_, bf16[1152,128]{1,0:T(8,128)(2,1)S(1)} %collective-permute-done.7.refs_1_, bf16[1024,128]{1,0:T(8,128)(2,1)S(1)} %collective-permute-done.8.refs_2_, bf16[1024,128]{1,0:T(8,128)(2,1)S(1)} %collective-permute-done.9.refs_3_, ...), custom_call_target="tpu_custom_call" | custom-call | flops 1 | bytes 1 | tf_op jit(solution)/shard_map/work/pallas_call | solution.py:302
  25.9 0.8 %add.4 = (bf16[4,1024,128]{2,1,0:T(8,128)(2,1)}, bf16[16,512]{1,0:T(8,128)(2,1)}) custom-call(bf16[528,128]{1,0:T(8,128)(2,1)S(1)} %collective-permute-done.2.refs_8_.arrived, bf16[4160,128]{1,0:T(8,128)(2,1)S(1)} %work.15.kept), custom_call_target="tpu_custom_call" | custom-call | flops 1 | bytes 1 | tf_op jit(solution)/shard_map/add/pallas_call | solution.py:359
  26.7 0.9 %add.5 = (bf16[4,1024,128]{2,1,0:T(8,128)(2,1)}, bf16[16,512]{1,0:T(8,128)(2,1)}) custom-call(bf16[1552,128]{1,0:T(8,128)(2,1)S(1)} %collective-permute-done.6.refs_8_.arrived, bf16[4160,128]{1,0:T(8,128)(2,1)S(1)} %work.15.kept, bf16[4,1024,128]{2,1,0:T(8,128)(2,1)} %get-tuple-element.38.rest_0_, ...), custom_call_target="tpu_custom_call", output_to_operand_aliasing={{0}: (2, {}), {1}: (3, {})} | custom-call | flops 1 | bytes 1 | tf_op jit(solution)/shard_map/add/pallas_call | solution.py:359
  27.6 0.7 %collective-permute-done.11.arrived = bf16[1680,128]{1,0:T(8,128)(2,1)S(1)} collective-permute-done((bf16[1680,128]{1,0:T(8,128)(2,1)S(1)}, bf16[1680,128]{1,0:T(8,128)(2,1)S(1)}, u32[]{:S(2)}, u32[]{:S(2)}) %collective-permute-start.11) | collective-permute-done | bytes 430112 | tf_op jit(solution)/shard_map/ppermute | solution.py:27
  28.3 0.9 %add.6 = (bf16[4,1024,128]{2,1,0:T(8,128)(2,1)}, bf16[16,512]{1,0:T(8,128)(2,1)}) custom-call(bf16[1680,128]{1,0:T(8,128)(2,1)S(1)} %collective-permute-done.11.arrived, bf16[4160,128]{1,0:T(8,128)(2,1)S(1)} %work.15.kept, bf16[4,1024,128]{2,1,0:T(8,128)(2,1)} %get-tuple-element.40.rest_0_, ...), custom_call_target="tpu_custom_call", output_to_operand_aliasing={{0}: (2, {}), {1}: (3, {})} | custom-call | flops 1 | bytes 1 | tf_op jit(solution)/shard_map/add/pallas_call | solution.py:359
  29.2 1.0 %collective-permute-done.5.arrived = bf16[400,128]{1,0:T(8,128)(2,1)S(1)} collective-permute-done((bf16[400,128]{1,0:T(8,128)(2,1)S(1)}, bf16[400,128]{1,0:T(8,128)(2,1)S(1)}, u32[]{:S(2)}, u32[]{:S(2)}) %collective-permute-start.5) | collective-permute-done | bytes 102432 | tf_op jit(solution)/shard_map/ppermute | solution.py:27
  30.3 0.7 %add.7 = (bf16[4,1024,128]{2,1,0:T(8,128)(2,1)}, bf16[16,512]{1,0:T(8,128)(2,1)}) custom-call(bf16[400,128]{1,0:T(8,128)(2,1)S(1)} %collective-permute-done.5.arrived, bf16[4160,128]{1,0:T(8,128)(2,1)S(1)} %work.15.kept, bf16[4,1024,128]{2,1,0:T(8,128)(2,1)} %get-tuple-element.42.rest_0_, ...), custom_call_target="tpu_custom_call", output_to_operand_aliasing={{0}: (2, {}), {1}: (3, {})} | custom-call | flops 1 | bytes 1 | tf_op jit(solution)/shard_map/add/pallas_call | solution.py:359
Async XLA Ops:
  1.9 1.7 %collective-permute-start = (bf16[1056,128]{1,0:T(8,128)(2,1)S(1)}, bf16[1056,128]{1,0:T(8,128)(2,1)S(1)}, u32[]{:S(2)}, u32[]{:S(2)}) collective-permute-start(bf16[1056,128]{1,0:T(8,128)(2,1)S(1)} %get-tuple-element.26.refs_7_), channel_id=1, source_target_pairs={{0,1},{1,0},{2,3},{3,2},{4,5},{5,4},{6,7},{7,6},{8,9},{9,8},{10,11... | collective-permute-start | bytes 811016 | tf_op jit(solution)/shard_map/ppermute | solution.py:20
  2.4 4.2 %collective-permute-start.1 = (bf16[1056,128]{1,0:T(8,128)(2,1)S(1)}, bf16[1056,128]{1,0:T(8,128)(2,1)S(1)}, u32[]{:S(2)}, u32[]{:S(2)}) collective-permute-start(bf16[1056,128]{1,0:T(8,128)(2,1)S(1)} %get-tuple-element.27), channel_id=1, source_target_pairs={{0,1},{1,0},{2,3},{3,2},{4,5},{5,4},{6,7},{7,6},{8,9},{9,8},{10,11... | collective-permute-start | bytes 811016 | tf_op jit(solution)/shard_map/ppermute | solution.py:20
  3.9 6.6 %collective-permute-start.2 = (bf16[528,128]{1,0:T(8,128)(2,1)S(1)}, bf16[528,128]{1,0:T(8,128)(2,1)S(1)}, u32[]{:S(2)}, u32[]{:S(2)}) collective-permute-start(bf16[528,128]{1,0:T(8,128)(2,1)S(1)} %work.10.refs_3_), channel_id=1, source_target_pairs={{0,5},{1,4},{2,7},{3,6},{4,1},{5,0},{6,3},{7,2},{8,13},{9,12},{10,... | collective-permute-start | bytes 405512 | tf_op jit(solution)/shard_map/ppermute | solution.py:27
  7.2 11.9 %collective-permute-start.6 = (bf16[1552,128]{1,0:T(8,128)(2,1)S(1)}, bf16[1552,128]{1,0:T(8,128)(2,1)S(1)}, u32[]{:S(2)}, u32[]{:S(2)}) collective-permute-start(bf16[1552,128]{1,0:T(8,128)(2,1)S(1)} %work.11.refs_7_), channel_id=1, source_target_pairs={{0,5},{1,4},{2,7},{3,6},{4,1},{5,0},{6,3},{7,2},{8,13},{9,12},{10,... | collective-permute-start | bytes 1191944 | tf_op jit(solution)/shard_map/ppermute | solution.py:27
  11.9 2.3 %collective-permute-start.3 = (bf16[1088,128]{1,0:T(8,128)(2,1)S(1)}, bf16[1088,128]{1,0:T(8,128)(2,1)S(1)}, u32[]{:S(2)}, u32[]{:S(2)}) collective-permute-start(bf16[1088,128]{1,0:T(8,128)(2,1)S(1)} %get-tuple-element.29), channel_id=1, source_target_pairs={{0,1},{1,0},{2,3},{3,2},{4,5},{5,4},{6,7},{7,6},{8,9},{9,8},{10,11... | collective-permute-start | bytes 835592 | tf_op jit(solution)/shard_map/ppermute | solution.py:20
  12.7 1.6 %collective-permute-start.4 = (bf16[1024,128]{1,0:T(8,128)(2,1)S(1)}, bf16[1024,128]{1,0:T(8,128)(2,1)S(1)}, u32[]{:S(2)}, u32[]{:S(2)}) collective-permute-start(bf16[1024,128]{1,0:T(8,128)(2,1)S(1)} %get-tuple-element.30), channel_id=1, source_target_pairs={{0,1},{1,0},{2,3},{3,2},{4,5},{5,4},{6,7},{7,6},{8,9},{9,8},{10,11... | collective-permute-start | bytes 786440 | tf_op jit(solution)/shard_map/ppermute | solution.py:20
  14.9 13.4 %collective-permute-start.11 = (bf16[1680,128]{1,0:T(8,128)(2,1)S(1)}, bf16[1680,128]{1,0:T(8,128)(2,1)S(1)}, u32[]{:S(2)}, u32[]{:S(2)}) collective-permute-start(bf16[1680,128]{1,0:T(8,128)(2,1)S(1)} %get-tuple-element.32.refs_7_), channel_id=1, source_target_pairs={{0,5},{1,4},{2,7},{3,6},{4,1},{5,0},{6,3},{7,2},{8,13},{9,12},{10,... | collective-permute-start | bytes 1290248 | tf_op jit(solution)/shard_map/ppermute | solution.py:27
  20.9 1.9 %collective-permute-start.8 = (bf16[1024,128]{1,0:T(8,128)(2,1)S(1)}, bf16[1024,128]{1,0:T(8,128)(2,1)S(1)}, u32[]{:S(2)}, u32[]{:S(2)}) collective-permute-start(bf16[1024,128]{1,0:T(8,128)(2,1)S(1)} %get-tuple-element.35), channel_id=1, source_target_pairs={{0,1},{1,0},{2,3},{3,2},{4,5},{5,4},{6,7},{7,6},{8,9},{9,8},{10,11... | collective-permute-start | bytes 786440 | tf_op jit(solution)/shard_map/ppermute | solution.py:20
  21.6 3.1 %collective-permute-start.7 = (bf16[1152,128]{1,0:T(8,128)(2,1)S(1)}, bf16[1152,128]{1,0:T(8,128)(2,1)S(1)}, u32[]{:S(2)}, u32[]{:S(2)}) collective-permute-start(bf16[1152,128]{1,0:T(8,128)(2,1)S(1)} %get-tuple-element.34.refs_5_), channel_id=1, source_target_pairs={{0,1},{1,0},{2,3},{3,2},{4,5},{5,4},{6,7},{7,6},{8,9},{9,8},{10,11... | collective-permute-start | bytes 884744 | tf_op jit(solution)/shard_map/ppermute | solution.py:20
  21.7 3.0 %collective-permute-start.9 = (bf16[1024,128]{1,0:T(8,128)(2,1)S(1)}, bf16[1024,128]{1,0:T(8,128)(2,1)S(1)}, u32[]{:S(2)}, u32[]{:S(2)}) collective-permute-start(bf16[1024,128]{1,0:T(8,128)(2,1)S(1)} %get-tuple-element.36), channel_id=1, source_target_pairs={{0,1},{1,0},{2,3},{3,2},{4,5},{5,4},{6,7},{7,6},{8,9},{9,8},{10,11... | collective-permute-start | bytes 786440 | tf_op jit(solution)/shard_map/ppermute | solution.py:20
  22.1 2.6 %collective-permute-start.10 = (bf16[1024,128]{1,0:T(8,128)(2,1)S(1)}, bf16[1024,128]{1,0:T(8,128)(2,1)S(1)}, u32[]{:S(2)}, u32[]{:S(2)}) collective-permute-start(bf16[1024,128]{1,0:T(8,128)(2,1)S(1)} %get-tuple-element.37), channel_id=1, source_target_pairs={{0,1},{1,0},{2,3},{3,2},{4,5},{5,4},{6,7},{7,6},{8,9},{9,8},{10,11... | collective-permute-start | bytes 786440 | tf_op jit(solution)/shard_map/ppermute | solution.py:20
  22.7 7.5 %collective-permute-start.5 = (bf16[400,128]{1,0:T(8,128)(2,1)S(1)}, bf16[400,128]{1,0:T(8,128)(2,1)S(1)}, u32[]{:S(2)}, u32[]{:S(2)}) collective-permute-start(bf16[400,128]{1,0:T(8,128)(2,1)S(1)} %get-tuple-element.31), channel_id=1, source_target_pairs={{0,5},{1,4},{2,7},{3,6},{4,1},{5,0},{6,3},{7,2},{8,13},{9,12},{10,... | collective-permute-start | bytes 307208 | tf_op jit(solution)/shard_map/ppermute | solution.py:27

commit v11 on v9

--- a/solution.py
+++ b/solution.py
@@ -417,7 +417,7 @@
     )
     parcels = merge(send[2:], [2, 3], [])
     last = work.run(
-        keys=keep, leaving=keep, apart=[1] * quarter, after=parcels[:1] + arrived[1:2]
+        keys=keep, leaving=keep, apart=[1] * quarter, joint=True, after=parcels[:1] + arrived[1:2]
     )
     kept = work.run(merges=keep, after=last[:1])[0]
     out = []

time: 31.3 us -> 31.3 us (level)
    ppermute x9 -> x8, starting transfers between devices: 3.11 us -> 2.73 us  [swapped(): return lax.ppermute(value, axis, pairs)]
    ppermute x9 -> x8, waiting for transfers between devices: 2.12 us -> 2.07 us  [swapped(): return lax.ppermute(value, axis, pairs)]
  transfers between devices with their start and end apart: 13 -> 12, of which waited for: 6 -> 6; matrix products, arithmetic and copies ran while one was open for 0% -> 0% of each run, Pallas kernels for 29% -> 29%
where the time goes in v11:
time: 31.3 us; the launch traced here: 31 us
  Pallas kernels  11 us (35%)
  waiting for transfers between devices  9.96 us (32%)
  starting transfers between devices  9.37 us (30%)
  between operations  0.72 us (2%)
    pallas_call x8, Pallas kernels, run(): pl.pallas_call(lambda *refs: work_kernel(plan, refs), out_shape=shapes, i...  8.37 us
    ppermute x4, waiting for transfers between devices, crossed_over(): return lax.ppermute(value, ('blk', 'sub'), pairs)  7.89 us
    ppermute x4, starting transfers between devices, crossed_over(): return lax.ppermute(value, ('blk', 'sub'), pairs)  6.64 us
    ppermute x8, starting transfers between devices, swapped(): return lax.ppermute(value, axis, pairs)  2.73 us
    pallas_call x3, Pallas kernels, added(): pl.pallas_call(functools.partial(add_kernel, parts, depth, rows), out_sha...  2.61 us
    ppermute x8, waiting for transfers between devices, swapped(): return lax.ppermute(value, axis, pairs)  2.07 us
  transfers between devices with their start and end apart: 12, of which 6 were waited for; matrix products, arithmetic and copies ran while one was open for 0% of the time, Pallas kernels for 29%

profile of v11, /device:TPU:0, one launch (start us, length us, event | category | flops | bytes accessed | tf_op | source)
XLA Modules:
  0.0 31.0 jit_solution(4294232534748985028)
XLA Ops:
  0.6 1.2 %work.8 = (bf16[1056,128]{1,0:T(8,128)(2,1)S(1)}, bf16[1056,128]{1,0:T(8,128)(2,1)S(1)}, s32[256,128]{1,0:T(8,128)S(1)}, s32[128,128]{1,0:T(8,128)S(1)}) custom-call(bf16[16,1024,128]{2,1,0:T(8,128)(2,1)} %bitcast.3, bf16[16,2048]{1,0:T(8,128)(2,1)} %refs_1_.7, s32[8,16]{1,0:T(8,128)} %bitcast.8, s32[256,128]{1,0:T(8,128)} %refs_3_.7, s32[128,128]{1,0:T(8,128)} %refs_4_.7), custom_call_target="tpu_custom_call" | custom-call | flops 1 | bytes 1 | tf_op jit(solution)/shard_map/work/pallas_call | solution.py:302
  1.9 0.5 %collective-permute-start = (bf16[1056,128]{1,0:T(8,128)(2,1)S(1)}, bf16[1056,128]{1,0:T(8,128)(2,1)S(1)}, u32[]{:S(2)}, u32[]{:S(2)}) collective-permute-start(bf16[1056,128]{1,0:T(8,128)(2,1)S(1)} %get-tuple-element.24.refs_7_), channel_id=1, source_target_pairs={{0,1},{1,0},{2,3},{3,2},{4,5},{5,4},{6,7},{7,6},{8,9},{9,8},{10,11... | collective-permute-start | bytes 811016 | tf_op jit(solution)/shard_map/ppermute | solution.py:20
  2.4 0.1 collective-permute-start.1
  2.5 1.1 %work.9.refs_0_ = bf16[2112,128]{1,0:T(8,128)(2,1)S(1)} custom-call(bf16[16,1024,128]{2,1,0:T(8,128)(2,1)} %bitcast.4, bf16[16,2048]{1,0:T(8,128)(2,1)} %refs_1_.7, s32[8,16]{1,0:T(8,128)} %bitcast.9, s32[256,128]{1,0:T(8,128)} %refs_3_.7, s32[128,128]{1,0:T(8,128)} %refs_4_.7, s32[256,128]{1,0:T(8,128)S(1)} %get-tuple-element.22.refs_5_, ...), custom_call_target="tpu_custom_call" | custom-call | flops 1 | bytes 1 | tf_op jit(solution)/shard_map/work/pallas_call | solution.py:302
  3.6 0.0 collective-permute-done.refs_1_
  3.6 0.3 %work.10.refs_3_ = bf16[528,128]{1,0:T(8,128)(2,1)S(1)} custom-call(bf16[2112,128]{1,0:T(8,128)(2,1)S(1)} %work.9.refs_0_, bf16[1056,128]{1,0:T(8,128)(2,1)S(1)} %collective-permute-done.refs_1_), custom_call_target="tpu_custom_call" | custom-call | flops 1 | bytes 1 | tf_op jit(solution)/shard_map/work/pallas_call | solution.py:302
  3.9 2.7 %collective-permute-start.2 = (bf16[528,128]{1,0:T(8,128)(2,1)S(1)}, bf16[528,128]{1,0:T(8,128)(2,1)S(1)}, u32[]{:S(2)}, u32[]{:S(2)}) collective-permute-start(bf16[528,128]{1,0:T(8,128)(2,1)S(1)} %work.10.refs_3_), channel_id=1, source_target_pairs={{0,5},{1,4},{2,7},{3,6},{4,1},{5,0},{6,3},{7,2},{8,13},{9,12},{10,... | collective-permute-start | bytes 405512 | tf_op jit(solution)/shard_map/ppermute | solution.py:27
  6.6 0.0 collective-permute-done.1.refs_2_
  6.6 0.6 %work.11.refs_7_ = bf16[1552,128]{1,0:T(8,128)(2,1)S(1)} custom-call(bf16[2112,128]{1,0:T(8,128)(2,1)S(1)} %work.9.refs_0_, bf16[1056,128]{1,0:T(8,128)(2,1)S(1)} %collective-permute-done.refs_1_, bf16[1056,128]{1,0:T(8,128)(2,1)S(1)} %collective-permute-done.1.refs_2_, bf16[528,128]{1,0:T(8,128)(2,1)S(1)} %work.10.refs_3_), custom_call_target="tpu_custom_call" | custom-call | flops 1 | bytes 1 | tf_op jit(solution)/shard_map/work/pallas_call | solution.py:302
  7.2 0.1 collective-permute-start.6
  7.3 3.2 %collective-permute-done.2.refs_8_.refs_0_ = bf16[528,128]{1,0:T(8,128)(2,1)S(1)} collective-permute-done((bf16[528,128]{1,0:T(8,128)(2,1)S(1)}, bf16[528,128]{1,0:T(8,128)(2,1)S(1)}, u32[]{:S(2)}, u32[]{:S(2)}) %collective-permute-start.2) | collective-permute-done | bytes 135200 | tf_op jit(solution)/shard_map/ppermute | solution.py:27
  10.6 1.3 %work.12 = (bf16[1088,128]{1,0:T(8,128)(2,1)S(1)}, bf16[1024,128]{1,0:T(8,128)(2,1)S(1)}, bf16[2112,128]{1,0:T(8,128)(2,1)S(1)}) custom-call(bf16[16,1024,128]{2,1,0:T(8,128)(2,1)} %bitcast.5, bf16[16,2048]{1,0:T(8,128)(2,1)} %refs_1_.7, s32[8,16]{1,0:T(8,128)} %bitcast.10, s32[256,128]{1,0:T(8,128)} %refs_3_.7, s32[128,128]{1,0:T(8,128)} %refs_4_.7, ...), custom_call_target="tpu_custom_call" | custom-call | flops 1 | bytes 1 | tf_op jit(solution)/shard_map/work/pallas_call | solution.py:302
  11.9 0.7 %collective-permute-start.3 = (bf16[1088,128]{1,0:T(8,128)(2,1)S(1)}, bf16[1088,128]{1,0:T(8,128)(2,1)S(1)}, u32[]{:S(2)}, u32[]{:S(2)}) collective-permute-start(bf16[1088,128]{1,0:T(8,128)(2,1)S(1)} %get-tuple-element.27), channel_id=1, source_target_pairs={{0,1},{1,0},{2,3},{3,2},{4,5},{5,4},{6,7},{7,6},{8,9},{9,8},{10,11... | collective-permute-start | bytes 835592 | tf_op jit(solution)/shard_map/ppermute | solution.py:20
  12.7 0.1 collective-permute-start.4
  12.7 1.5 %collective-permute-done.4.refs_2_ = bf16[1024,128]{1,0:T(8,128)(2,1)S(1)} collective-permute-done((bf16[1024,128]{1,0:T(8,128)(2,1)S(1)}, bf16[1024,128]{1,0:T(8,128)(2,1)S(1)}, u32[]{:S(2)}, u32[]{:S(2)}) %collective-permute-start.4) | collective-permute-done | bytes 262176 | tf_op jit(solution)/shard_map/ppermute | solution.py:20
  14.2 0.0 collective-permute-done.3.refs_1_
  14.2 0.7 %work.13 = (bf16[1680,128]{1,0:T(8,128)(2,1)S(1)}, bf16[400,128]{1,0:T(8,128)(2,1)S(1)}) custom-call(bf16[2112,128]{1,0:T(8,128)(2,1)S(1)} %get-tuple-element.26.refs_0_, bf16[1088,128]{1,0:T(8,128)(2,1)S(1)} %collective-permute-done.3.refs_1_, bf16[1024,128]{1,0:T(8,128)(2,1)S(1)} %collective-permute-done.4.refs_2_), custom_call_target="tpu_custom_call" | custom-call | flops 1 | bytes 1 | tf_op jit(solution)/shard_map/work/pallas_call | solution.py:302
  14.9 2.0 %collective-permute-start.11 = (bf16[1680,128]{1,0:T(8,128)(2,1)S(1)}, bf16[1680,128]{1,0:T(8,128)(2,1)S(1)}, u32[]{:S(2)}, u32[]{:S(2)}) collective-permute-start(bf16[1680,128]{1,0:T(8,128)(2,1)S(1)} %get-tuple-element.30.refs_7_), channel_id=1, source_target_pairs={{0,5},{1,4},{2,7},{3,6},{4,1},{5,0},{6,3},{7,2},{8,13},{9,12},{10,... | collective-permute-start | bytes 1290248 | tf_op jit(solution)/shard_map/ppermute | solution.py:27
  16.9 2.2 %collective-permute-done.6.refs_8_.refs_1_ = bf16[1552,128]{1,0:T(8,128)(2,1)S(1)} collective-permute-done((bf16[1552,128]{1,0:T(8,128)(2,1)S(1)}, bf16[1552,128]{1,0:T(8,128)(2,1)S(1)}, u32[]{:S(2)}, u32[]{:S(2)}) %collective-permute-start.6) | collective-permute-done | bytes 397344 | tf_op jit(solution)/shard_map/ppermute | solution.py:27
  19.1 1.7 %work.14 = (bf16[1152,128]{1,0:T(8,128)(2,1)S(1)}, bf16[1024,128]{1,0:T(8,128)(2,1)S(1)}, bf16[1024,128]{1,0:T(8,128)(2,1)S(1)}, bf16[1024,128]{1,0:T(8,128)(2,1)S(1)}, bf16[4224,128]{1,0:T(8,128)(2,1)S(1)}) custom-call(bf16[16,1024,128]{2,1,0:T(8,128)(2,1)} %bitcast.6, bf16[16,2048]{1,0:T(8,128)(2,1)} %refs_1_.7, s32[8,16]{1,0:T(8,128)} %bitcast.11, ...), custom_call_target="tpu_custom_call" | custom-call | flops 1 | bytes 1 | tf_op jit(solution)/shard_map/work/pallas_call | solution.py:302
  20.9 0.7 %collective-permute-start.8 = (bf16[1024,128]{1,0:T(8,128)(2,1)S(1)}, bf16[1024,128]{1,0:T(8,128)(2,1)S(1)}, u32[]{:S(2)}, u32[]{:S(2)}) collective-permute-start(bf16[1024,128]{1,0:T(8,128)(2,1)S(1)} %get-tuple-element.33), channel_id=1, source_target_pairs={{0,1},{1,0},{2,3},{3,2},{4,5},{5,4},{6,7},{7,6},{8,9},{9,8},{10,11... | collective-permute-start | bytes 786440 | tf_op jit(solution)/shard_map/ppermute | solution.py:20
  21.6 0.1 collective-permute-start.7
  21.7 0.4 %collective-permute-start.9 = (bf16[1024,128]{1,0:T(8,128)(2,1)S(1)}, bf16[1024,128]{1,0:T(8,128)(2,1)S(1)}, u32[]{:S(2)}, u32[]{:S(2)}) collective-permute-start(bf16[1024,128]{1,0:T(8,128)(2,1)S(1)} %get-tuple-element.34), channel_id=1, source_target_pairs={{0,1},{1,0},{2,3},{3,2},{4,5},{5,4},{6,7},{7,6},{8,9},{9,8},{10,11... | collective-permute-start | bytes 786440 | tf_op jit(solution)/shard_map/ppermute | solution.py:20
  22.1 0.1 collective-permute-start.10
  22.2 0.6 %collective-permute-done.8.refs_2_ = bf16[1024,128]{1,0:T(8,128)(2,1)S(1)} collective-permute-done((bf16[1024,128]{1,0:T(8,128)(2,1)S(1)}, bf16[1024,128]{1,0:T(8,128)(2,1)S(1)}, u32[]{:S(2)}, u32[]{:S(2)}) %collective-permute-start.8) | collective-permute-done | bytes 262176 | tf_op jit(solution)/shard_map/ppermute | solution.py:20
  22.7 1.9 %collective-permute-start.5 = (bf16[400,128]{1,0:T(8,128)(2,1)S(1)}, bf16[400,128]{1,0:T(8,128)(2,1)S(1)}, u32[]{:S(2)}, u32[]{:S(2)}) collective-permute-start(bf16[400,128]{1,0:T(8,128)(2,1)S(1)} %get-tuple-element.29), channel_id=1, source_target_pairs={{0,5},{1,4},{2,7},{3,6},{4,1},{5,0},{6,3},{7,2},{8,13},{9,12},{10,... | collective-permute-start | bytes 307208 | tf_op jit(solution)/shard_map/ppermute | solution.py:27
  24.7 0.0 collective-permute-done.9.refs_3_
  24.7 0.0 collective-permute-done.10.refs_4_
  24.7 0.0 collective-permute-done.7.refs_1_
  24.7 1.3 %work.15.refs_2_.refs_1_ = bf16[4160,128]{1,0:T(8,128)(2,1)S(1)} custom-call(bf16[4224,128]{1,0:T(8,128)(2,1)S(1)} %get-tuple-element.31.refs_0_, bf16[1152,128]{1,0:T(8,128)(2,1)S(1)} %collective-permute-done.7.refs_1_, bf16[1024,128]{1,0:T(8,128)(2,1)S(1)} %collective-permute-done.8.refs_2_, bf16[1024,128]{1,0:T(8,128)(2,1)S(1)} %collective-permute-done.9.refs_3_, ...), custom_call_target="tpu_custom_call" | custom-call | flops 1 | bytes 1 | tf_op jit(solution)/shard_map/work/pallas_call | solution.py:302
  25.9 0.9 %add.3 = (bf16[4,1024,128]{2,1,0:T(8,128)(2,1)}, bf16[16,512]{1,0:T(8,128)(2,1)}) custom-call(bf16[528,128]{1,0:T(8,128)(2,1)S(1)} %collective-permute-done.2.refs_8_.refs_0_, bf16[1552,128]{1,0:T(8,128)(2,1)S(1)} %collective-permute-done.6.refs_8_.refs_1_, bf16[4160,128]{1,0:T(8,128)(2,1)S(1)} %work.15.refs_2_.refs_1_), custom_call_target="tpu_custom_call" | custom-call | flops 1 | bytes 1 | tf_op jit(solution)/shard_map/add/pallas_call | solution.py:365
  26.9 1.4 %collective-permute-done.11.refs_0_ = bf16[1680,128]{1,0:T(8,128)(2,1)S(1)} collective-permute-done((bf16[1680,128]{1,0:T(8,128)(2,1)S(1)}, bf16[1680,128]{1,0:T(8,128)(2,1)S(1)}, u32[]{:S(2)}, u32[]{:S(2)}) %collective-permute-start.11) | collective-permute-done | bytes 430112 | tf_op jit(solution)/shard_map/ppermute | solution.py:27
  28.3 0.9 %add.4 = (bf16[4,1024,128]{2,1,0:T(8,128)(2,1)}, bf16[16,512]{1,0:T(8,128)(2,1)}) custom-call(bf16[1680,128]{1,0:T(8,128)(2,1)S(1)} %collective-permute-done.11.refs_0_, bf16[4160,128]{1,0:T(8,128)(2,1)S(1)} %work.15.refs_2_.refs_1_, bf16[4,1024,128]{2,1,0:T(8,128)(2,1)} %get-tuple-element.36.refs_2_, ...), custom_call_target="tpu_custom_call", output_to_operand_aliasing={{0}: (2, {}), {1}: (3, {})} | custom-call | flops 1 | bytes 1 | tf_op jit(solution)/shard_map/add/pallas_call | solution.py:365
  29.2 1.0 %collective-permute-done.5.refs_0_ = bf16[400,128]{1,0:T(8,128)(2,1)S(1)} collective-permute-done((bf16[400,128]{1,0:T(8,128)(2,1)S(1)}, bf16[400,128]{1,0:T(8,128)(2,1)S(1)}, u32[]{:S(2)}, u32[]{:S(2)}) %collective-permute-start.5) | collective-permute-done | bytes 102432 | tf_op jit(solution)/shard_map/ppermute | solution.py:27
  30.3 0.7 %add.5 = (bf16[4,1024,128]{2,1,0:T(8,128)(2,1)}, bf16[16,512]{1,0:T(8,128)(2,1)}) custom-call(bf16[400,128]{1,0:T(8,128)(2,1)S(1)} %collective-permute-done.5.refs_0_, bf16[4160,128]{1,0:T(8,128)(2,1)S(1)} %work.15.refs_2_.refs_1_, bf16[4,1024,128]{2,1,0:T(8,128)(2,1)} %get-tuple-element.38.refs_2_, ...), custom_call_target="tpu_custom_call", output_to_operand_aliasing={{0}: (2, {}), {1}: (3, {})} | custom-call | flops 1 | bytes 1 | tf_op jit(solution)/shard_map/add/pallas_call | solution.py:365
Async XLA Ops:
  1.9 1.7 %collective-permute-start = (bf16[1056,128]{1,0:T(8,128)(2,1)S(1)}, bf16[1056,128]{1,0:T(8,128)(2,1)S(1)}, u32[]{:S(2)}, u32[]{:S(2)}) collective-permute-start(bf16[1056,128]{1,0:T(8,128)(2,1)S(1)} %get-tuple-element.24.refs_7_), channel_id=1, source_target_pairs={{0,1},{1,0},{2,3},{3,2},{4,5},{5,4},{6,7},{7,6},{8,9},{9,8},{10,11... | collective-permute-start | bytes 811016 | tf_op jit(solution)/shard_map/ppermute | solution.py:20
  2.4 4.2 %collective-permute-start.1 = (bf16[1056,128]{1,0:T(8,128)(2,1)S(1)}, bf16[1056,128]{1,0:T(8,128)(2,1)S(1)}, u32[]{:S(2)}, u32[]{:S(2)}) collective-permute-start(bf16[1056,128]{1,0:T(8,128)(2,1)S(1)} %get-tuple-element.25), channel_id=1, source_target_pairs={{0,1},{1,0},{2,3},{3,2},{4,5},{5,4},{6,7},{7,6},{8,9},{9,8},{10,11... | collective-permute-start | bytes 811016 | tf_op jit(solution)/shard_map/ppermute | solution.py:20
  3.9 6.6 %collective-permute-start.2 = (bf16[528,128]{1,0:T(8,128)(2,1)S(1)}, bf16[528,128]{1,0:T(8,128)(2,1)S(1)}, u32[]{:S(2)}, u32[]{:S(2)}) collective-permute-start(bf16[528,128]{1,0:T(8,128)(2,1)S(1)} %work.10.refs_3_), channel_id=1, source_target_pairs={{0,5},{1,4},{2,7},{3,6},{4,1},{5,0},{6,3},{7,2},{8,13},{9,12},{10,... | collective-permute-start | bytes 405512 | tf_op jit(solution)/shard_map/ppermute | solution.py:27
  7.2 11.9 %collective-permute-start.6 = (bf16[1552,128]{1,0:T(8,128)(2,1)S(1)}, bf16[1552,128]{1,0:T(8,128)(2,1)S(1)}, u32[]{:S(2)}, u32[]{:S(2)}) collective-permute-start(bf16[1552,128]{1,0:T(8,128)(2,1)S(1)} %work.11.refs_7_), channel_id=1, source_target_pairs={{0,5},{1,4},{2,7},{3,6},{4,1},{5,0},{6,3},{7,2},{8,13},{9,12},{10,... | collective-permute-start | bytes 1191944 | tf_op jit(solution)/shard_map/ppermute | solution.py:27
  11.9 2.3 %collective-permute-start.3 = (bf16[1088,128]{1,0:T(8,128)(2,1)S(1)}, bf16[1088,128]{1,0:T(8,128)(2,1)S(1)}, u32[]{:S(2)}, u32[]{:S(2)}) collective-permute-start(bf16[1088,128]{1,0:T(8,128)(2,1)S(1)} %get-tuple-element.27), channel_id=1, source_target_pairs={{0,1},{1,0},{2,3},{3,2},{4,5},{5,4},{6,7},{7,6},{8,9},{9,8},{10,11... | collective-permute-start | bytes 835592 | tf_op jit(solution)/shard_map/ppermute | solution.py:20
  12.7 1.6 %collective-permute-start.4 = (bf16[1024,128]{1,0:T(8,128)(2,1)S(1)}, bf16[1024,128]{1,0:T(8,128)(2,1)S(1)}, u32[]{:S(2)}, u32[]{:S(2)}) collective-permute-start(bf16[1024,128]{1,0:T(8,128)(2,1)S(1)} %get-tuple-element.28), channel_id=1, source_target_pairs={{0,1},{1,0},{2,3},{3,2},{4,5},{5,4},{6,7},{7,6},{8,9},{9,8},{10,11... | collective-permute-start | bytes 786440 | tf_op jit(solution)/shard_map/ppermute | solution.py:20
  14.9 13.4 %collective-permute-start.11 = (bf16[1680,128]{1,0:T(8,128)(2,1)S(1)}, bf16[1680,128]{1,0:T(8,128)(2,1)S(1)}, u32[]{:S(2)}, u32[]{:S(2)}) collective-permute-start(bf16[1680,128]{1,0:T(8,128)(2,1)S(1)} %get-tuple-element.30.refs_7_), channel_id=1, source_target_pairs={{0,5},{1,4},{2,7},{3,6},{4,1},{5,0},{6,3},{7,2},{8,13},{9,12},{10,... | collective-permute-start | bytes 1290248 | tf_op jit(solution)/shard_map/ppermute | solution.py:27
  20.9 1.9 %collective-permute-start.8 = (bf16[1024,128]{1,0:T(8,128)(2,1)S(1)}, bf16[1024,128]{1,0:T(8,128)(2,1)S(1)}, u32[]{:S(2)}, u32[]{:S(2)}) collective-permute-start(bf16[1024,128]{1,0:T(8,128)(2,1)S(1)} %get-tuple-element.33), channel_id=1, source_target_pairs={{0,1},{1,0},{2,3},{3,2},{4,5},{5,4},{6,7},{7,6},{8,9},{9,8},{10,11... | collective-permute-start | bytes 786440 | tf_op jit(solution)/shard_map/ppermute | solution.py:20
  21.6 3.1 %collective-permute-start.7 = (bf16[1152,128]{1,0:T(8,128)(2,1)S(1)}, bf16[1152,128]{1,0:T(8,128)(2,1)S(1)}, u32[]{:S(2)}, u32[]{:S(2)}) collective-permute-start(bf16[1152,128]{1,0:T(8,128)(2,1)S(1)} %get-tuple-element.32.refs_5_), channel_id=1, source_target_pairs={{0,1},{1,0},{2,3},{3,2},{4,5},{5,4},{6,7},{7,6},{8,9},{9,8},{10,11... | collective-permute-start | bytes 884744 | tf_op jit(solution)/shard_map/ppermute | solution.py:20
  21.7 3.0 %collective-permute-start.9 = (bf16[1024,128]{1,0:T(8,128)(2,1)S(1)}, bf16[1024,128]{1,0:T(8,128)(2,1)S(1)}, u32[]{:S(2)}, u32[]{:S(2)}) collective-permute-start(bf16[1024,128]{1,0:T(8,128)(2,1)S(1)} %get-tuple-element.34), channel_id=1, source_target_pairs={{0,1},{1,0},{2,3},{3,2},{4,5},{5,4},{6,7},{7,6},{8,9},{9,8},{10,11... | collective-permute-start | bytes 786440 | tf_op jit(solution)/shard_map/ppermute | solution.py:20
  22.1 2.6 %collective-permute-start.10 = (bf16[1024,128]{1,0:T(8,128)(2,1)S(1)}, bf16[1024,128]{1,0:T(8,128)(2,1)S(1)}, u32[]{:S(2)}, u32[]{:S(2)}) collective-permute-start(bf16[1024,128]{1,0:T(8,128)(2,1)S(1)} %get-tuple-element.35), channel_id=1, source_target_pairs={{0,1},{1,0},{2,3},{3,2},{4,5},{5,4},{6,7},{7,6},{8,9},{9,8},{10,11... | collective-permute-start | bytes 786440 | tf_op jit(solution)/shard_map/ppermute | solution.py:20
  22.7 7.5 %collective-permute-start.5 = (bf16[400,128]{1,0:T(8,128)(2,1)S(1)}, bf16[400,128]{1,0:T(8,128)(2,1)S(1)}, u32[]{:S(2)}, u32[]{:S(2)}) collective-permute-start(bf16[400,128]{1,0:T(8,128)(2,1)S(1)} %get-tuple-element.29), channel_id=1, source_target_pairs={{0,5},{1,4},{2,7},{3,6},{4,1},{5,0},{6,3},{7,2},{8,13},{9,12},{10,... | collective-permute-start | bytes 307208 | tf_op jit(solution)/shard_map/ppermute | solution.py:27
